TPU v7x, 32 devices: a whole 2x2x4 slice. The times are simulated.
32 devices in a mesh: grp: 2 (over y), seq: 16 (over z, x, core).
Axes of the slice: x: 2, y: 2, z: 4, core: 2. Of those that a mesh axis runs over, the one named last changes fastest.
Arguments:
- queries: bfloat16 [8192, 2048], P(('grp', 'seq')), parts along dimension 0, may hold values from -6 to 6
- keys: bfloat16 [8192, 2048], P(('grp', 'seq')), parts along dimension 0, may hold values from -6 to 6
- values: bfloat16 [8192, 2048], P(('grp', 'seq')), parts along dimension 0, may hold values from -6 to 6
- level_index: int32 [8192], P(('grp', 'seq')), parts along dimension 0, may hold values from 0 to 63
- level_table: float32 [64, 18, 16], replicated, may hold values from 0 to 10
- norm_gain: float32 [2048], replicated, may hold values from 0.1 to 1.9
- out_weight: bfloat16 [2048, 2048], P(None, 'seq'), may hold values from -0.125 to 0.125
Outputs:
- block_out: bfloat16 [8192, 2048], P(('grp', 'seq')), parts along dimension 0
There are 2 independent parts, one for each index of `grp`. A program takes and returns all parts, laid end to end along the dimension named above; an argument that names none is the same for every part. Nothing has to cross between parts.
All inputs are finite; a program needn't handle non-finite values.
Results may differ from a plain program's by a relative error of at most 0.0057.
Values may be sent and summed in bfloat16 or wider, within the bound.
No kernel may reach another device: no remote copies, remote signals or barrier semaphores. Data moves between devices by JAX's collectives and lax.ppermute only.
A program may use at most 128 MiB of HBM per device.

v0:
```python
import math

import jax
import jax.numpy as jnp
from jax import lax
from jax.sharding import PartitionSpec as P


def from_partner(block, axis, apart):
    count = lax.axis_size(axis)
    route = []
    for low in range(count):
        high = low | 1 << apart
        if high != low and high < count:
            route += [(low, high), (high, low)]
    return lax.ppermute(block, axis, route)


def body(queries, keys, values, level_index, level_table, norm_gain, out_weight):
    stretch, width = queries.shape
    table_rows, level_count, heads = level_table.shape
    head_dim = width // heads
    scale = 1.0 / math.sqrt(head_dim)
    log_stretch = stretch.bit_length() - 1
    log_blocks = lax.axis_size("seq").bit_length() - 1
    rank = lax.axis_index("seq")
    q_heads = jnp.transpose(queries.reshape(stretch, heads, head_dim), (1, 0, 2))
    k_heads = jnp.transpose(keys.reshape(stretch, heads, head_dim), (1, 0, 2))
    v_heads = jnp.transpose(values.reshape(stretch, heads, head_dim), (1, 0, 2))
    selector = (level_index[:, None] == jnp.arange(table_rows, dtype=jnp.int32)[None, :]).astype(
        jnp.float32
    )
    lam = jnp.dot(
        selector,
        level_table.reshape(table_rows, level_count * heads),
        precision=lax.Precision.HIGHEST,
    )
    lam_heads = jnp.transpose(lam.reshape(stretch, level_count, heads), (2, 0, 1))
    state = jnp.einsum("hse,hsf->hef", k_heads, v_heads, preferred_element_type=jnp.float32)
    positions = jnp.arange(stretch, dtype=jnp.int32)
    level_grid = jnp.zeros((positions.shape[0], positions.shape[0]), jnp.int32)
    for bit in range(log_stretch):
        level_grid = level_grid + (
            jnp.right_shift(positions[:, None], bit) != jnp.right_shift(positions[None, :], bit)
        ).astype(jnp.int32)
    scores = (
        jnp.einsum("hte,hse->hts", q_heads, k_heads, preferred_element_type=jnp.float32) * scale
    )
    picked = jnp.zeros_like(scores)
    for level in range(log_stretch + 1):
        picked = jnp.where((level_grid == level)[None], lam_heads[:, :, level : level + 1], picked)
    weighted = jnp.where(
        (positions[None, :] <= positions[:, None])[None], picked * scores, 0.0
    ).astype(jnp.bfloat16)
    pieces = jnp.einsum("hts,hsf->htf", weighted, v_heads, preferred_element_type=jnp.float32)
    group = state
    far = jnp.zeros((heads, stretch, head_dim), jnp.float32)
    for bit in range(log_blocks):
        owned = jnp.right_shift(rank, bit) % 2 == 1
        other = from_partner(group, "seq", bit)
        bucket = other.astype(jnp.bfloat16)
        term = jnp.einsum("hte,hef->htf", q_heads, bucket, preferred_element_type=jnp.float32)
        weight = lam_heads[:, :, log_stretch + 1 + bit : log_stretch + 2 + bit]
        far = far + jnp.where(owned, weight * term * scale, 0.0)
        if bit + 1 < log_blocks:
            group = group + other
    mixed = pieces + far
    normed = (
        mixed
        * lax.rsqrt(jnp.mean(mixed * mixed, axis=2, keepdims=True) + 1e-06)
        * norm_gain.reshape(heads, 1, head_dim)
    )
    normed = jnp.transpose(normed, (1, 0, 2)).reshape(stretch, width).astype(jnp.bfloat16)
    full_weight = lax.all_gather(out_weight, "seq", axis=1, tiled=True)
    return jnp.dot(normed, full_weight, preferred_element_type=jnp.float32).astype(jnp.bfloat16)


def solution(mesh):
    placed = (
        P(("grp", "seq"), None),
        P(("grp", "seq"), None),
        P(("grp", "seq"), None),
        P(("grp", "seq")),
        P(),
        P(),
        P(None, "seq"),
    )
    return jax.shard_map(
        body, mesh=mesh, in_specs=placed, out_specs=P(("grp", "seq"), None), check_vma=False
    )
```

profile of v0, /device:TPU:0, one launch (start us, length us, event | category | flops | bytes accessed | tf_op | source)
XLA Modules:
  0.0 159.7 jit_solution(18002641853276145586)
XLA Ops:
  6.5 0.0 copy-start
  6.5 0.0 copy-start.1
  6.5 0.0 all-gather.2.cloned.1.call-start
  6.5 0.7 all-gather.2.cloned.1.call-update
  7.3 1.5 copy.30
  8.7 0.0 copy-start.2
  8.8 0.0 copy-start.7
  8.8 0.0 copy-start.10
  8.8 0.0 copy-done.1
  8.8 0.4 fusion.18
  9.2 0.5 collective-permute-start
  9.7 0.6 iota_shift-right-arithmetic_fusion
  10.3 0.5 iota_shift-right-arithmetic_fusion.2
  10.9 0.0 copy-done.7
  10.9 0.0 copy-done.10
  10.9 0.3 convolution_bitcast_fusion
  11.2 0.2 fusion.41
  11.4 0.7 collective-permute-done
  12.0 0.0 copy-start.3
  12.0 0.1 add.400
  12.2 0.0 copy-done.2
  12.2 2.9 %collective-permute-start.1 = (f32[16,128,128]{2,1,0:T(8,128)S(1)}, f32[16,128,128]{2,1,0:T(8,128)S(1)}, u32[]{:S(2)}, u32[]{:S(2)}) collective-permute-start(f32[16,128,128]{2,1,0:T(8,128)S(1)} %add.400), channel_id=1, source_target_pairs={{0,2},{2,0},{1,3},{3,1},{4,6},{6,4},{5,7},{7,5},{8,10},{10,8},{9,1... | collective-permute-start | bytes 3145736 | tf_op jit(solution)/shard_map/ppermute | solution.py:16
  15.1 0.5 iota_shift-right-arithmetic_fusion.4
  15.6 0.7 iota_compare_fusion
  16.3 0.6 copy_bitcast_fusion
  16.9 0.6 copy_bitcast_fusion.2
  17.5 0.6 copy_bitcast_fusion.4
  18.1 0.6 copy_bitcast_fusion.6
  18.7 25.4 %collective-permute-done.1 = f32[16,128,128]{2,1,0:T(8,128)S(1)} collective-permute-done((f32[16,128,128]{2,1,0:T(8,128)S(1)}, f32[16,128,128]{2,1,0:T(8,128)S(1)}, u32[]{:S(2)}, u32[]{:S(2)}) %collective-permute-start.1) | collective-permute-done | bytes 1048608 | tf_op jit(solution)/shard_map/ppermute | solution.py:16
  44.2 0.0 copy-start.5
  44.2 0.1 add.403
  44.3 0.0 copy-done.3
  44.3 1.9 %collective-permute-start.2 = (f32[16,128,128]{2,1,0:T(8,128)S(1)}, f32[16,128,128]{2,1,0:T(8,128)}, u32[]{:S(2)}, u32[]{:S(2)}) collective-permute-start(f32[16,128,128]{2,1,0:T(8,128)S(1)} %add.403), channel_id=1, source_target_pairs={{0,4},{4,0},{1,5},{5,1},{2,6},{6,2},{3,7},{7,3},{8,12},{12,8},{9,1... | collective-permute-start | bytes 3145736 | tf_op jit(solution)/shard_map/ppermute | solution.py:16
  46.2 0.0 copy-done.5
  46.2 0.6 iota_shift-right-arithmetic_fusion.6
  46.8 0.0 copy-start.8
  46.8 0.0 copy-start.9
  46.8 0.0 copy-start.4
  46.8 1.2 copy.48
  48.0 0.6 copy_bitcast_fusion.9
  48.6 0.6 copy_bitcast_fusion.11
  49.2 0.0 copy-done.8
  49.2 0.0 copy-done.9
  49.2 2.2 %broadcast_compare_fusion.8 = (pred[256,256]{1,0:T(8,128)(4,1)S(1)}, pred[256,256]{1,0:T(8,128)(4,1)S(1)}, pred[256,256]{1,0:T(8,128)(4,1)S(1)}, pred[256,256]{1...) fusion(s32[256]{0:T(256)} %get-tuple-element.48, ...), kind=kLoop, calls=%fused_computation.55 | loop fusion | flops 2097152 | bytes 598016 | tf_op jit(solution)/shard_map/eq | solution.py:51
  51.5 0.0 copy-done
  51.5 0.0 copy-done.4
  51.5 1.8 %fusion.23 = f32[16,128,256]{2,1,0:T(8,128)} fusion(f32[16,128,128]{2,1,0:T(8,128)S(1)} %copy-done.4, bf16[256,2048]{1,0:T(8,128)(2,1)S(1)} %copy-done), kind=kOutput, calls=%fused_computation.33 | convolution fusion | flops 134479872 | bytes 4194304 | tf_op jit(solution)/shard_map/hte,hef->htf/dot_general | solution.py:62
  53.3 0.0 copy-start.6
  53.3 43.1 %collective-permute-done.2 = f32[16,128,128]{2,1,0:T(8,128)} collective-permute-done((f32[16,128,128]{2,1,0:T(8,128)S(1)}, f32[16,128,128]{2,1,0:T(8,128)}, u32[]{:S(2)}, u32[]{:S(2)}) %collective-permute-start.2) | collective-permute-done | bytes 1048608 | tf_op jit(solution)/shard_map/ppermute | solution.py:16
  96.4 1.3 add.406
  97.7 0.9 collective-permute-start.3
  98.6 0.0 copy-done.6
  98.6 1.8 %fusion.22 = f32[16,128,256]{2,1,0:T(8,128)} fusion(f32[16,128,128]{2,1,0:T(8,128)S(1)} %copy-done.6, bf16[256,2048]{1,0:T(8,128)(2,1)S(1)} %copy-done), kind=kOutput, calls=%fused_computation.32 | convolution fusion | flops 134479872 | bytes 4194304 | tf_op jit(solution)/shard_map/hte,hef->htf/dot_general | solution.py:62
  100.5 3.2 %fusion.21 = f32[16,128,256]{2,1,0:T(8,128)} fusion(f32[16,128,128]{2,1,0:T(8,128)} %collective-permute-done.2, bf16[256,2048]{1,0:T(8,128)(2,1)S(1)} %copy-done), kind=kOutput, calls=%fused_computation.31 | convolution fusion | flops 134479872 | bytes 4194304 | tf_op jit(solution)/shard_map/hte,hef->htf/dot_general | solution.py:62
  103.7 25.3 %collective-permute-done.3 = bf16[16,128,128]{2,1,0:T(8,128)(2,1)S(1)} collective-permute-done((bf16[16,128,128]{2,1,0:T(8,128)(2,1)S(1)}, bf16[16,128,128]{2,1,0:T(8,128)(2,1)S(1)}, u32[]{:S(2)}, u32[]{:S(2)}) %collective-permute-start.3) | collective-permute-done | bytes 524320 | tf_op jit(solution)/shard_map/ppermute | solution.py:16
  128.9 0.5 fusion.20
  129.4 10.6 %fusion.1 = (f32[16,256]{1,0:T(8,128)}, f32[16,256,128]{1,2,0:T(8,128)}) fusion(f32[16,128,256]{2,1,0:T(8,128)S(1)} %fusion.20, f32[16,128,256]{2,1,0:T(8,128)} %fusion.21, f32[16,128,256]{2,1,0:T(8,128)} %fusion.22, f32[16,128,256]{2,1,0:T(8,128)} %fusion.23, f32[16,256]{1,0:T(8,128)S(1)} %get-tuple-element.25, f32[16,256]{1,0:T(8,128)} %get-tuple-element.23, ...), kind=kOutput, calls=%fused_computation.4 | convolution fusion | flops 559935488 | bytes 14516228 | tf_op jit(solution)/shard_map/hts,hsf->htf/dot_general | solution.py:55
  140.1 0.7 rsqrt_bitcast_fusion
  140.8 5.0 %fusion.8 = bf16[256,16,128]{0,2,1:T(8,128)(2,1)} fusion(f32[16,128,256]{2,1,0:T(8,128)S(1)} %fusion.20, f32[16,128,256]{2,1,0:T(8,128)} %fusion.21, f32[16,128,256]{2,1,0:T(8,128)} %fusion.22, f32[16,128,256]{2,1,0:T(8,128)} %fusion.23, f32[16,256,128]{1,2,0:T(8,128)} %get-tuple-element.36, f32[16,128]{1,0:T(8,128)} %bitcast.172, ...), kind=kLoop, calls=%fused_computation.12 | loop fusion | flops 9961472 | bytes 11624452 | tf_op jit(solution)/shard_map/convert_element_type | solution.py:73
  145.8 0.0 all-gather.2.cloned.1.call-done
  145.8 7.0 %convolution_convert_fusion = bf16[256,2048]{1,0:T(8,128)(2,1)} fusion(bf16[256,2048]{0,1:T(8,128)(2,1)} %bitcast.164, bf16[2048,2048]{1,0:T(8,128)(2,1)} %all-gather.2.cloned.1.call-done), kind=kOutput, calls=%fused_computation.1 | convolution fusion | flops 2148007936 | bytes 10485760 | tf_op jit(solution)/shard_map/dot_general | solution.py:75
  (1 shorter events, 0.0 us)
Async XLA Ops:
  6.5 44.9 %copy-start = (bf16[256,2048]{1,0:T(8,128)(2,1)S(1)}, bf16[256,2048]{1,0:T(8,128)(2,1)}, u32[]{:S(2)}) copy-start(bf16[256,2048]{1,0:T(8,128)(2,1)} %param.7) | copy-start | bytes 3145732
  6.5 2.2 %copy-start.1 = (bf16[256,2048]{1,0:T(8,128)(2,1)S(1)}, bf16[256,2048]{1,0:T(8,128)(2,1)}, u32[]{:S(2)}) copy-start(bf16[256,2048]{1,0:T(8,128)(2,1)} %param.9) | copy-start | bytes 3145732
  6.5 139.3 %all-gather.2.cloned.1.call-start = ((), (), s32[]{:S(2)}) async-start(), calls=%async_computation | async-start | bytes 8912896 | tf_op jit(solution)/shard_map/all_gather | solution.py:74
  8.7 3.4 %copy-start.2 = (bf16[256,2048]{0,1:T(8,128)(2,1)}, bf16[256,2048]{0,1:T(8,128)(2,1)S(1)}, u32[]{:S(2)}) copy-start(bf16[256,2048]{0,1:T(8,128)(2,1)S(1)} %copy.30) | copy-start | bytes 3145732
  8.8 2.1 %copy-start.7 = (f32[64,18,16]{0,2,1:T(8,128)S(1)}, f32[64,18,16]{0,2,1:T(8,128)}, u32[]{:S(2)}) copy-start(f32[64,18,16]{0,2,1:T(8,128)} %param.11) | copy-start | bytes 221188
  8.8 2.1 %copy-start.10 = (s32[256]{0:T(256)S(1)}, s32[256]{0:T(256)}, u32[]{:S(2)}) copy-start(s32[256]{0:T(256)} %param.10) | copy-start | bytes 3076
  9.2 2.8 %collective-permute-start = (f32[16,128,128]{2,1,0:T(8,128)S(1)}, f32[16,128,128]{2,1,0:T(8,128)S(1)}, u32[]{:S(2)}, u32[]{:S(2)}) collective-permute-start(f32[16,128,128]{2,1,0:T(8,128)S(1)} %fusion.18), channel_id=1, source_target_pairs={{0,1},{1,0},{2,3},{3,2},{4,5},{5,4},{6,7},{7,6},{8,9},{9,8},{10,11... | collective-permute-start | bytes 3145736 | tf_op jit(solution)/shard_map/ppermute | solution.py:16
  12.0 32.3 %copy-start.3 = (f32[16,128,128]{2,1,0:T(8,128)}, f32[16,128,128]{2,1,0:T(8,128)S(1)}, u32[]{:S(2)}) copy-start(f32[16,128,128]{2,1,0:T(8,128)S(1)} %collective-permute-done) | copy-start | bytes 3145732
  12.2 32.0 %collective-permute-start.1 = (f32[16,128,128]{2,1,0:T(8,128)S(1)}, f32[16,128,128]{2,1,0:T(8,128)S(1)}, u32[]{:S(2)}, u32[]{:S(2)}) collective-permute-start(f32[16,128,128]{2,1,0:T(8,128)S(1)} %add.400), channel_id=1, source_target_pairs={{0,2},{2,0},{1,3},{3,1},{4,6},{6,4},{5,7},{7,5},{8,10},{10,8},{9,1... | collective-permute-start | bytes 3145736 | tf_op jit(solution)/shard_map/ppermute | solution.py:16
  44.2 2.0 %copy-start.5 = (f32[16,128,128]{2,1,0:T(8,128)}, f32[16,128,128]{2,1,0:T(8,128)S(1)}, u32[]{:S(2)}) copy-start(f32[16,128,128]{2,1,0:T(8,128)S(1)} %collective-permute-done.1) | copy-start | bytes 3145732
  44.3 52.1 %collective-permute-start.2 = (f32[16,128,128]{2,1,0:T(8,128)S(1)}, f32[16,128,128]{2,1,0:T(8,128)}, u32[]{:S(2)}, u32[]{:S(2)}) collective-permute-start(f32[16,128,128]{2,1,0:T(8,128)S(1)} %add.403), channel_id=1, source_target_pairs={{0,4},{4,0},{1,5},{5,1},{2,6},{6,2},{3,7},{7,3},{8,12},{12,8},{9,1... | collective-permute-start | bytes 3145736 | tf_op jit(solution)/shard_map/ppermute | solution.py:16
  46.8 2.4 %copy-start.8 = (s32[256]{0:T(256)S(1)}, s32[256]{0:T(256)}, u32[]{:S(2)}) copy-start(s32[256]{0:T(256)} %get-tuple-element.54) | copy-start | bytes 3076
  46.8 2.4 %copy-start.9 = (s32[256]{0:T(256)S(1)}, s32[256]{0:T(256)}, u32[]{:S(2)}) copy-start(s32[256]{0:T(256)} %get-tuple-element.55) | copy-start | bytes 3076
  46.8 4.7 %copy-start.4 = (f32[16,128,128]{2,1,0:T(8,128)S(1)}, f32[16,128,128]{2,1,0:T(8,128)}, u32[]{:S(2)}) copy-start(f32[16,128,128]{2,1,0:T(8,128)} %copy-done.3) | copy-start | bytes 3145732
  53.3 45.4 %copy-start.6 = (f32[16,128,128]{2,1,0:T(8,128)S(1)}, f32[16,128,128]{2,1,0:T(8,128)}, u32[]{:S(2)}) copy-start(f32[16,128,128]{2,1,0:T(8,128)} %copy-done.5) | copy-start | bytes 3145732
  97.7 31.2 %collective-permute-start.3 = (bf16[16,128,128]{2,1,0:T(8,128)(2,1)S(1)}, bf16[16,128,128]{2,1,0:T(8,128)(2,1)S(1)}, u32[]{:S(2)}, u32[]{:S(2)}) collective-permute-start(bf16[16,128,128]{2,1,0:T(8,128)(2,1)S(1)} %add.406), channel_id=1, source_target_pairs={{0,8},{8,0},{1,9},{9,1},{2,10},{10,2},{3,11},{11,3},{4,12},{12,4},... | collective-permute-start | bytes 1572872 | tf_op jit(solution)/shard_map/ppermute | solution.py:16
Sparse Core Ops, SparseCore 0:
  9.5 116.8 all-gather.1
where the time goes:
time: 160 us
  waiting for transfers between devices  95.2 us (60%)
  matrix products  25.7 us (16%)
  between operations  13.5 us (8%)
  other arithmetic  12.5 us (8%)
  local copies, waits for them, and re-layouts  6.56 us (4%)
  starting transfers between devices  6.22 us (4%)
    ppermute x4, waiting for transfers between devices, from_partner(): return lax.ppermute(block, axis, route)  94.5 us
    dot_general x1, matrix products, body(): jnp.einsum('hts,hsf->htf', weighted, v_heads, preferred_element_type=jnp....  10.6 us
    dot_general x4, matrix products, body(): jnp.einsum('hte,hef->htf', q_heads, bucket, preferred_element_type=jnp.fl...  7.32 us
    dot_general x1, matrix products, body(): jnp.dot(normed, full_weight, preferred_element_type=jnp.float32)  7.04 us
    ppermute x4, starting transfers between devices, from_partner(): return lax.ppermute(block, axis, route)  6.22 us
    convert_element_type x1, other arithmetic, body(): jnp.transpose(normed, (1, 0, 2)).reshape(stretch, width)  5.02 us
    unnamed x28, local copies, waits for them, and re-layouts  3.69 us
  transfers between devices with their start and end apart: 5, of which 4 were waited for; matrix products, arithmetic and copies ran while one was open for 24% of the time, Pallas kernels for 0%

commit v1 on v0

v1 whole, which is shorter than its diff:
```python
import functools
import math

import numpy as np

import jax
import jax.numpy as jnp
from jax import lax
from jax.experimental import pallas as pl
from jax.experimental.pallas import tpu as pltpu
from jax.sharding import PartitionSpec as P

TILE = 128
VM = pl.BlockSpec(memory_space=pltpu.VMEM)
SM = pl.BlockSpec(memory_space=pltpu.SMEM)
PARAMS = pltpu.CompilerParams(vmem_limit_bytes=8 * 1024 * 1024)


def call(kernel, out_shape, in_specs, flops, moved, *operands):
    outs = jax.tree.map(lambda _: VM, out_shape)
    return pl.pallas_call(
        kernel,
        out_shape=out_shape,
        in_specs=in_specs,
        out_specs=outs,
        compiler_params=PARAMS,
        cost_estimate=pl.CostEstimate(flops=flops, bytes_accessed=moved, transcendentals=0),
    )(*operands)


def lanes(start, size):
    return pl.ds(pl.multiple_of(start, TILE), size)


def dot(a, b, ca=1, cb=0):
    return lax.dot_general(a, b, (((ca,), (cb,)), ((), ())), preferred_element_type=jnp.float32)


def state_kernel(info, k_ref, v_ref, got_ref, sum_ref, send_ref, even_ref):
    heads, dim, _ = sum_ref.shape
    rows = k_ref.shape[0]
    core = info[0]
    for h in range(heads):
        own = lanes(core * heads * dim + h * dim, dim)
        far = pl.ds(h * dim, dim)
        mine = dot(k_ref[:, own], v_ref[:, own], 0, 0)
        theirs = dot(got_ref[pl.ds(0, rows), far], got_ref[pl.ds(rows, rows), far], 0, 0)
        both = mine + theirs
        sum_ref[h] = both
        send_ref[h] = both.astype(jnp.bfloat16)
        even_ref[h] = jnp.where(core == 0, mine, theirs).astype(jnp.bfloat16)


def pick_rows(index_ref, table, rows, start):
    found = index_ref[pl.ds(start, rows), :] == lax.broadcasted_iota(jnp.int32, (rows, table.shape[0]), 1)
    return lax.dot_general(
        found.astype(jnp.float32),
        table,
        (((1,), (0,)), ((), ())),
        precision=lax.Precision.HIGHEST,
        preferred_element_type=jnp.float32,
    )


def local_kernel(log_stretch, info, q_ref, k_ref, v_ref, got_ref, index_ref, table_ref, even_ref, out_ref):
    heads, dim = even_ref.shape[0], even_ref.shape[1]
    rows = q_ref.shape[0]
    core = info[0]
    scale = 1.0 / math.sqrt(dim)
    step = min(TILE, rows)
    t_at = lax.broadcasted_iota(jnp.int32, (step, step), 0)
    s_at = lax.broadcasted_iota(jnp.int32, (step, step), 1)
    grid = jnp.zeros((step, step), jnp.int32)
    log_step = step.bit_length() - 1
    for bit in range(log_step):
        grid = grid + (jnp.right_shift(t_at, bit) != jnp.right_shift(s_at, bit)).astype(jnp.int32)
    grid = jnp.where(s_at <= t_at, grid, -1)

    def one(h, _):
        own = lanes(core * heads * dim + h * dim, dim)
        far = lanes(h * dim, dim)
        table = table_ref[core * heads + h]
        for side in range(2):
            if side == 0:
                odd = core

                def part(which, block):
                    ref = (k_ref, v_ref, q_ref)[which]
                    return ref[pl.ds(block * step, step), own]
            else:
                odd = 1 - core

                def part(which, block):
                    return got_ref[pl.ds(which * rows + block * step, step), far]

            lam = pick_rows(index_ref, table, rows, side * rows) * scale
            for block in range(rows // step):
                lam_b = lam[block * step : (block + 1) * step]
                q = part(2, block)
                weight = jnp.where(odd == 1, lam_b[:, log_stretch + 1 : log_stretch + 2], 0.0)
                total = weight * dot(q, even_ref[h])
                for other in range(block + 1):
                    scores = dot(q, part(0, other), 1, 1)
                    if other == block:
                        picked = jnp.zeros((step, step), jnp.float32)
                        for level in range(log_step + 1):
                            picked = jnp.where(grid == level, lam_b[:, level : level + 1], picked)
                    else:
                        level = log_step + (block ^ other).bit_length()
                        picked = lam_b[:, level : level + 1]
                    total = total + dot((picked * scores).astype(jnp.bfloat16), part(1, other))
                out_ref[pl.ds(side * rows + block * step, step), far] = total
        return 0

    lax.fori_loop(0, heads, one, 0)


def far_kernel(levels, final, log_stretch, *refs):
    count = len(levels)
    info, q_ref, got_ref, index_ref, table_ref, base_ref = refs[:6]
    buckets = refs[6 : 6 + count]
    rows = q_ref.shape[0]
    heads = table_ref.shape[0] // 2
    dim = base_ref.shape[1] // heads
    core = info[0]
    scale = 1.0 / math.sqrt(dim)
    if final:
        gain_ref, out_ref = refs[6 + count :]
    else:
        (out_ref,) = refs[6 + count :]

    def one(h, _):
        own = lanes(core * heads * dim + h * dim, dim)
        far = lanes(h * dim, dim)
        table = table_ref[core * heads + h]
        for side in range(2):
            lam = pick_rows(index_ref, table, rows, side * rows)
            q = q_ref[:, own] if side == 0 else got_ref[pl.ds(2 * rows, rows), far]
            total = base_ref[pl.ds(side * rows, rows), far]
            for at, level in enumerate(levels):
                column = log_stretch + 1 + level
                weight = jnp.where(info[1 + level] == 1, lam[:, column : column + 1] * scale, 0.0)
                total = total + weight * dot(q, buckets[at][h])
            if final:
                mean = jnp.mean(total * total, axis=1, keepdims=True)
                total = total * lax.rsqrt(mean + 1e-06) * gain_ref[:, own]
            out_ref[pl.ds(side * rows, rows), far] = total.astype(out_ref.dtype)
        return 0

    lax.fori_loop(0, heads, one, 0)


def project_kernel(side, plan, info, normed_ref, *refs):
    out_ref = refs[-1]
    rows = out_ref.shape[0]
    for chip_slot, parts in plan:
        total = None
        for at, row0, k_slot, k_add, size in parts:
            piece = refs[at]
            start = k_add if k_slot is None else info[k_slot] + k_add
            a = normed_ref[pl.ds(side * rows, rows), lanes(start, size)]
            term = dot(a, piece[pl.ds(row0, size), :])
            total = term if total is None else total + term
        width = refs[parts[0][0]].shape[1]
        column = 0 if chip_slot is None else info[chip_slot] * width
        out_ref[:, lanes(column, width)] = total.astype(out_ref.dtype)


def ring_order(chips):
    return list(range(0, chips, 2)) + list(range(chips - 1, 0, -2))


def body(groups, queries, keys, values, level_index, level_table, norm_gain, out_weight):
    stretch, width = queries.shape
    table_rows, level_count, heads = level_table.shape
    head_dim = width // heads
    columns = out_weight.shape[1]
    log_stretch = stretch.bit_length() - 1
    devices = lax.axis_size("seq")
    log_blocks = devices.bit_length() - 1
    rank = lax.axis_index("seq")
    group = lax.axis_index("grp")
    core = rank % 2
    half = width // 2
    pair_heads = heads // 2
    chips = devices // 2
    ringed = (2 * columns) % TILE == 0 and chips >= 4
    shared = (3 * half // 8) // TILE * TILE if ringed and groups == 2 else 0
    kept = half - shared
    cut = kept // TILE // 2 * TILE

    order = ring_order(chips)
    facts = np.zeros((groups, devices, 1 + log_blocks + 2 + chips), np.int32)
    for g in range(groups):
        for r in range(devices):
            place = order.index(r // 2) if ringed else 0
            facts[g, r] = (
                [r % 2]
                + [r >> bit & 1 for bit in range(log_blocks)]
                + [g * shared, (1 - g) * kept]
                + [order[(place - d) % chips] if ringed else 0 for d in range(chips)]
            )
    k_mine, k_lacks, chip_at = 1 + log_blocks, 2 + log_blocks, 3 + log_blocks
    info = lax.dynamic_slice(jnp.asarray(facts), (group, rank, 0), (1, 1, facts.shape[2])).reshape(-1)

    def swap(block, bit, upward=False):
        route = [(r, r ^ 1 << bit) for r in range(devices) if not (upward and r >> bit & 1)]
        return lax.ppermute(block, "seq", route)

    other = (1 - core) * half
    w_got = swap(lax.dynamic_slice(out_weight, (other, 0), (half, columns)), 0)
    got = swap(
        jnp.concatenate(
            [lax.dynamic_slice(x, (0, other), (stretch, half)) for x in (keys, values, queries)], axis=0
        ),
        0,
    )
    index = jnp.concatenate([level_index, swap(level_index, 0)]).reshape(-1, 1)
    table = jnp.transpose(level_table, (2, 0, 1))

    w_own = lax.dynamic_slice(out_weight, (core * half, 0), (half, columns))
    whole = jnp.where(
        core == 0,
        jnp.concatenate([w_own, w_got], axis=1),
        jnp.concatenate([w_got, w_own], axis=1),
    )
    pieces = []
    plan = []
    if ringed:
        clockwise = []
        for at, chip in enumerate(order):
            follows = order[(at + 1) % chips]
            clockwise += [(2 * chip + c, 2 * follows + c) for c in range(2)]
        counter = [(b, a) for a, b in clockwise]
        pieces.append(whole)
        plan.append((chip_at, [(0, 0, None, 0, half)]))
        right = left = lax.dynamic_slice(whole, (group * shared, 0), (kept, 2 * columns)) if shared else whole
        rounds = chips // 2
        for r in range(1, rounds + 1):
            last = r == rounds
            if last:
                right, left = right[:cut], left[cut:]
            right = lax.ppermute(right, "seq", clockwise)
            left = lax.ppermute(left, "seq", counter)
            at = len(pieces)
            pieces += [right, left]
            if last:
                parts = [[(at, 0, k_mine, 0, cut), (at + 1, 0, k_mine, cut, kept - cut)]]
                distances = [r]
            else:
                parts = [[(at, 0, k_mine, 0, kept)], [(at + 1, 0, k_mine, 0, kept)]]
                distances = [r, chips - r]
            if shared:
                first = group * (kept - shared)
                if last:
                    wanted = lax.dynamic_slice(
                        jnp.concatenate([right, left], axis=0), (first, 0), (shared, 2 * columns)
                    )
                else:
                    wanted = jnp.concatenate(
                        [lax.dynamic_slice(x, (first, 0), (shared, 2 * columns)) for x in (right, left)], axis=0
                    )
                pieces.append(lax.ppermute(wanted, "grp", [(0, 1), (1, 0)]))
                for n, part in enumerate(parts):
                    part.append((at + 2, n * shared, k_lacks, 0, shared))
            plan += [(chip_at + d, part) for d, part in zip(distances, parts)]
    else:
        full = lax.all_gather(out_weight, "seq", axis=1, tiled=True)
        pieces.append(lax.dynamic_slice(full, (core * half, 0), (half, width)))
        plan.append((None, [(0, 0, None, 0, half)]))

    state = jax.ShapeDtypeStruct((pair_heads, head_dim, head_dim), jnp.float32)
    state16 = jax.ShapeDtypeStruct(state.shape, jnp.bfloat16)
    total, send, even = call(
        state_kernel,
        (state, state16, state16),
        [SM] + [VM] * 3,
        2 * stretch * width * head_dim,
        1 << 21,
        info, keys, values, got,
    )
    buckets = [even]
    for bit in range(1, log_blocks):
        came = swap(send, bit, upward=bit == log_blocks - 1)
        buckets.append(came)
        if bit + 1 < log_blocks:
            total = total + came
            send = total.astype(jnp.bfloat16)

    mixed = jax.ShapeDtypeStruct((2 * stretch, half), jnp.float32)
    acc = call(
        functools.partial(local_kernel, log_stretch),
        mixed,
        [SM] + [VM] * 7,
        8 * stretch * stretch * half,
        1 << 23,
        info, queries, keys, values, got, index, table, even,
    )
    early = list(range(1, log_blocks - 1))
    if early:
        acc = call(
            functools.partial(far_kernel, early, False, log_stretch),
            mixed,
            [SM] + [VM] * (5 + len(early)),
            4 * stretch * half * head_dim * len(early),
            1 << 23,
            info, queries, got, index, table, acc, *[buckets[b] for b in early],
        )
    normed = call(
        functools.partial(far_kernel, [log_blocks - 1], True, log_stretch),
        jax.ShapeDtypeStruct(mixed.shape, jnp.bfloat16),
        [SM] + [VM] * 7,
        4 * stretch * half * head_dim,
        1 << 23,
        info, queries, got, index, table, acc, buckets[-1], norm_gain.reshape(1, width),
    )

    def project(side, dtype):
        return call(
            functools.partial(project_kernel, side, plan),
            jax.ShapeDtypeStruct((stretch, width), dtype),
            [SM] + [VM] * (1 + len(pieces)),
            2 * stretch * half * width,
            1 << 23,
            info, normed, *pieces,
        )

    came = swap(project(1, jnp.bfloat16), 0)
    return (project(0, jnp.float32) + came).astype(jnp.bfloat16)


def solution(mesh):
    placed = (
        P(("grp", "seq"), None),
        P(("grp", "seq"), None),
        P(("grp", "seq"), None),
        P(("grp", "seq")),
        P(),
        P(),
        P(None, "seq"),
    )
    return jax.shard_map(
        functools.partial(body, mesh.shape["grp"]),
        mesh=mesh,
        in_specs=placed,
        out_specs=P(("grp", "seq"), None),
        check_vma=False,
    )
```

time: 160 us -> 105 us (0.66)
  waiting for transfers between devices: 95.2 us -> 24.4 us
  Pallas kernels: 0 us -> 35.2 us
  matrix products: 25.7 us -> 0 us
  starting transfers between devices: 6.22 us -> 25.8 us
  between operations: 13.5 us -> 0.49 us
  other arithmetic: 12.5 us -> 7.08 us
  local copies, waits for them, and re-layouts: 6.56 us -> 11.3 us
    ppermute x4 -> x19, waiting for transfers between devices: 94.5 us -> 24.4 us  [the longest x4 10.5 us: body(): left = lax.ppermute(left, 'seq', counter)]
    pallas_call x0 -> x6, Pallas kernels: none -> 35.2 us  [call(): pl.pallas_call(kernel, out_shape=out_shape, in_specs=in_specs, out_specs=...]
    dot_general x8 -> x0, matrix products: 25.7 us -> none  [the longest x1 10.6 us: body(): jnp.einsum('hts,hsf->htf', weighted, v_heads, preferred_element_type=jnp....]
    ppermute x4 -> x19, starting transfers between devices: 6.22 us -> 25.8 us  [the longest x7 9.27 us: swap(): return lax.ppermute(block, 'seq', route)]
    concatenate x0 -> x6, other arithmetic: none -> 4.73 us  [the longest x3 2.46 us: body(): jnp.concatenate([lax.dynamic_slice(x, (first, 0), (shared, 2 * columns))...]
    dynamic_slice x0 -> x9, local copies, waits for them, and re-layouts: none -> 4.17 us  [the longest x2 2.35 us: body(): lax.dynamic_slice(x, (0, other), (stretch, half))]
    convert_element_type x1 -> x3, other arithmetic: 5.02 us -> 2.16 us  [the longest x1 1.3 us: body(): return (project(0, jnp.float32) + came).astype(jnp.bfloat16)]
    unnamed x28 -> x57, local copies, waits for them, and re-layouts: 3.69 us -> 6.13 us
  transfers between devices with their start and end apart: 5 -> 19, of which waited for: 4 -> 7; matrix products, arithmetic and copies ran while one was open for 24% -> 8% of each run, Pallas kernels for 0% -> 31%
where the time goes in v1:
time: 105 us; the launch traced here: 104 us
  Pallas kernels  35.2 us (34%)
  starting transfers between devices  25.8 us (25%)
  waiting for transfers between devices  24.4 us (23%)
  local copies, waits for them, and re-layouts  11.3 us (11%)
  other arithmetic  7.08 us (7%)
    pallas_call x6, Pallas kernels, call(): pl.pallas_call(kernel, out_shape=out_shape, in_specs=in_specs, out_specs=...  35.2 us
    ppermute x4, waiting for transfers between devices, body(): left = lax.ppermute(left, 'seq', counter)  10.5 us
    ppermute x7, starting transfers between devices, swap(): return lax.ppermute(block, 'seq', route)  9.27 us
    ppermute x7, waiting for transfers between devices, swap(): return lax.ppermute(block, 'seq', route)  7.57 us
    ppermute x4, starting transfers between devices, body(): pieces.append(lax.ppermute(wanted, 'grp', [(0, 1), (1, 0)]))  6.4 us
    ppermute x4, waiting for transfers between devices, body(): right = lax.ppermute(right, 'seq', clockwise)  6.33 us
    unnamed x57, local copies, waits for them, and re-layouts  6.13 us
    ppermute x4, starting transfers between devices, body(): left = lax.ppermute(left, 'seq', counter)  5.66 us
  transfers between devices with their start and end apart: 19, of which 7 were waited for; matrix products, arithmetic and copies ran while one was open for 8% of the time, Pallas kernels for 31%

profile of v1, /device:TPU:0, one launch (start us, length us, event | category | flops | bytes accessed | tf_op | source)
XLA Modules:
  0.0 104.3 jit_solution(15151533156696797228)
XLA Ops:
  0.0 1.1 %constant_dynamic-slice_fusion.11 = bf16[256,1024]{1,0:T(8,128)(2,1)S(1)} fusion(bf16[256,2048]{1,0:T(8,128)(2,1)} %k_ref.3, s32[]{:T(128)S(6)} %select_n.45), kind=kLoop, calls=%fused_computation.23 | loop fusion | bytes 1048580 | tf_op jit(solution)/shard_map/dynamic_slice | solution.py:214
  1.1 1.3 %constant_dynamic-slice_fusion.9 = (bf16[256,1024]{1,0:T(8,128)(2,1)S(1)}, bf16[256,1024]{1,0:T(8,128)(2,1)S(1)}) fusion(bf16[256,2048]{1,0:T(8,128)(2,1)} %refs_1_.3, s32[]{:T(128)S(6)} %select_n.45, bf16[256,2048]{1,0:T(8,128)(2,1)} %v_ref.3), kind=kLoop, calls=%fused_computation.21 | loop fusion | bytes 2097156 | tf_op jit(solution)/shard_map/dynamic_slice | solution.py:214
  2.4 0.0 copy-start.26
  2.4 1.3 %pad_maximum_fusion = bf16[768,1024]{1,0:T(8,128)(2,1)} fusion(bf16[256,1024]{1,0:T(8,128)(2,1)S(1)} %get-tuple-element.15, bf16[256,1024]{1,0:T(8,128)(2,1)S(1)} %get-tuple-element.16, bf16[256,1024]{1,0:T(8,128)(2,1)S(1)} %constant_dynamic-slice_fusion.11), kind=kLoop, calls=%fused_computation.1 | loop fusion | flops 4718592 | bytes 3145728 | tf_op jit(solution)/shard_map/concatenate | solution.py:213
  3.7 0.5 collective-permute-start
  4.2 0.0 copy-start.3
  4.2 0.1 collective-permute-start.5
  4.3 3.2 %collective-permute-done.5 = bf16[1024,128]{1,0:T(8,128)(2,1)S(1)} collective-permute-done((bf16[1024,128]{1,0:T(8,128)(2,1)S(1)}, bf16[1024,128]{1,0:T(8,128)(2,1)S(1)}, u32[]{:S(2)}, u32[]{:S(2)}) %collective-permute-start.5) | collective-permute-done | bytes 262176 | tf_op jit(solution)/shard_map/ppermute | solution.py:208
  7.5 0.2 maximum_select_fusion.refs_0_
  7.7 0.8 constant_dynamic-slice_fusion.6
  8.4 0.8 copy-done.1
  9.2 2.6 %collective-permute-start.7 = (bf16[640,256]{1,0:T(8,128)(2,1)}, bf16[640,256]{1,0:T(8,128)(2,1)S(1)}, u32[]{:S(2)}, u32[]{:S(2)}) collective-permute-start(bf16[640,256]{1,0:T(8,128)(2,1)} %constant_dynamic-slice_fusion.6), channel_id=1, source_target_pairs={{4,0},{5,1},{8,4},{9,5},{12,8},{13,9},{14,12},{15,13},{10,14},{11,... | collective-permute-start | bytes 983048 | tf_op jit(solution)/shard_map/ppermute | solution.py:244
  11.8 0.1 collective-permute-start.6
  11.9 1.1 %copy.10 = f32[64,18,16]{1,0,2:T(8,128)S(1)} copy(f32[64,18,16]{0,2,1:T(8,128)} %param.12) | data formatting | bytes 147456 | tf_op args[4]
  13.0 0.0 copy-start.5
  13.0 0.8 fusion.2.info.refs_0_
  13.8 6.5 %collective-permute-done.7.refs_2_ = bf16[640,256]{1,0:T(8,128)(2,1)S(1)} collective-permute-done((bf16[640,256]{1,0:T(8,128)(2,1)}, bf16[640,256]{1,0:T(8,128)(2,1)S(1)}, u32[]{:S(2)}, u32[]{:S(2)}) %collective-permute-start.7) | collective-permute-done | bytes 327712 | tf_op jit(solution)/shard_map/ppermute | solution.py:244
  20.3 1.7 %collective-permute-start.10 = (bf16[640,256]{1,0:T(8,128)(2,1)S(1)}, bf16[640,256]{1,0:T(8,128)(2,1)S(1)}, u32[]{:S(2)}, u32[]{:S(2)}) collective-permute-start(bf16[640,256]{1,0:T(8,128)(2,1)S(1)} %collective-permute-done.7.refs_2_), channel_id=1, source_target_pairs={{4,0},{5,1},{8,4},{9,5},{12,8},{13,9},{14,12},{15,13},{10,14},{11,... | collective-permute-start | bytes 983048 | tf_op jit(solution)/shard_map/ppermute | solution.py:244
  22.0 0.4 collective-permute-start.9
  22.4 1.0 constant_dynamic-slice_fusion.5
  23.3 0.8 pad_maximum_fusion.1
  24.1 1.7 %collective-permute-start.8 = (bf16[768,256]{1,0:T(8,128)(2,1)}, bf16[768,256]{1,0:T(8,128)(2,1)}, u32[]{:S(2)}, u32[]{:S(2)}) collective-permute-start(bf16[768,256]{1,0:T(8,128)(2,1)} %pad_maximum_fusion.1), channel_id=1, source_target_pairs={{0,16},{16,0},{1,17},{17,1},{2,18},{18,2},{3,19},{19,3},{4,20},{20... | collective-permute-start | bytes 1179656 | tf_op jit(solution)/shard_map/ppermute | solution.py:263
  25.8 4.0 %collective-permute-done.10.refs_5_ = bf16[640,256]{1,0:T(8,128)(2,1)S(1)} collective-permute-done((bf16[640,256]{1,0:T(8,128)(2,1)S(1)}, bf16[640,256]{1,0:T(8,128)(2,1)S(1)}, u32[]{:S(2)}, u32[]{:S(2)}) %collective-permute-start.10) | collective-permute-done | bytes 327712 | tf_op jit(solution)/shard_map/ppermute | solution.py:244
  29.8 1.4 %collective-permute-start.13 = (bf16[640,256]{1,0:T(8,128)(2,1)S(1)}, bf16[640,256]{1,0:T(8,128)(2,1)S(1)}, u32[]{:S(2)}, u32[]{:S(2)}) collective-permute-start(bf16[640,256]{1,0:T(8,128)(2,1)S(1)} %collective-permute-done.10.refs_5_), channel_id=1, source_target_pairs={{4,0},{5,1},{8,4},{9,5},{12,8},{13,9},{14,12},{15,13},{10,14},{11,... | collective-permute-start | bytes 983048 | tf_op jit(solution)/shard_map/ppermute | solution.py:244
  31.3 0.0 collective-permute-done.got_ref.refs_2_
  31.3 1.0 %shard_map.82 = (f32[8,128,128]{2,1,0:T(8,128)S(1)}, bf16[8,128,128]{2,1,0:T(8,128)(2,1)S(1)}, bf16[8,128,128]{2,1,0:T(8,128)(2,1)S(1)}) custom-call(s32[15]{0:T(128)S(1)} %fusion.2.info.refs_0_, bf16[256,2048]{1,0:T(8,128)(2,1)S(1)} %copy-done.5, bf16[256,2048]{1,0:T(8,128)(2,1)S(1)} %copy-done.3, bf16[768,1024]{1,0:T(8,128)(2,1)S(1)} %collective-permute-done.got_ref.refs_2_), custom_call_target="tpu_custom_call" | custom-call | flops 134217728 | bytes 2097152 | tf_op jit(solution)/shard_map/pallas_call | solution.py:21
  32.3 0.7 copy-done.23
  33.0 1.6 %collective-permute-start.2 = (bf16[8,128,128]{2,1,0:T(8,128)(2,1)S(1)}, bf16[8,128,128]{2,1,0:T(8,128)(2,1)S(1)}, u32[]{:S(2)}, u32[]{:S(2)}) collective-permute-start(bf16[8,128,128]{2,1,0:T(8,128)(2,1)S(1)} %get-tuple-element.9), channel_id=1, source_target_pairs={{0,2},{1,3},{2,0},{3,1},{4,6},{5,7},{6,4},{7,5},{8,10},{9,11},{10,... | collective-permute-start | bytes 786440 | tf_op jit(solution)/shard_map/ppermute | solution.py:208
  34.6 0.0 collective-permute-done.9.refs_4_
  34.7 0.8 pad_maximum_fusion.2
  35.5 1.5 %collective-permute-start.11 = (bf16[768,256]{1,0:T(8,128)(2,1)}, bf16[768,256]{1,0:T(8,128)(2,1)}, u32[]{:S(2)}, u32[]{:S(2)}) collective-permute-start(bf16[768,256]{1,0:T(8,128)(2,1)} %pad_maximum_fusion.2), channel_id=1, source_target_pairs={{0,16},{16,0},{1,17},{17,1},{2,18},{18,2},{3,19},{19,3},{4,20},{20... | collective-permute-start | bytes 1179656 | tf_op jit(solution)/shard_map/ppermute | solution.py:263
  37.0 1.6 %collective-permute-start.12 = (bf16[640,256]{1,0:T(8,128)(2,1)S(1)}, bf16[640,256]{1,0:T(8,128)(2,1)S(1)}, u32[]{:S(2)}, u32[]{:S(2)}) collective-permute-start(bf16[640,256]{1,0:T(8,128)(2,1)S(1)} %collective-permute-done.9.refs_4_), channel_id=1, source_target_pairs={{0,4},{1,5},{4,8},{5,9},{8,12},{9,13},{12,14},{13,15},{14,10},{15,... | collective-permute-start | bytes 983048 | tf_op jit(solution)/shard_map/ppermute | solution.py:243
  38.6 4.3 %collective-permute-done.2.refs_6_ = bf16[8,128,128]{2,1,0:T(8,128)(2,1)S(1)} collective-permute-done((bf16[8,128,128]{2,1,0:T(8,128)(2,1)S(1)}, bf16[8,128,128]{2,1,0:T(8,128)(2,1)S(1)}, u32[]{:S(2)}, u32[]{:S(2)}) %collective-permute-start.2) | collective-permute-done | bytes 262176 | tf_op jit(solution)/shard_map/ppermute | solution.py:208
  42.9 0.1 fusion
  42.9 0.0 copy-start
  43.0 0.1 collective-permute-start.3
  43.0 0.0 collective-permute-done.13.refs_8_
  43.1 3.8 %collective-permute-done.12.refs_7_ = bf16[640,256]{1,0:T(8,128)(2,1)S(1)} collective-permute-done((bf16[640,256]{1,0:T(8,128)(2,1)S(1)}, bf16[640,256]{1,0:T(8,128)(2,1)S(1)}, u32[]{:S(2)}, u32[]{:S(2)}) %collective-permute-start.12) | collective-permute-done | bytes 327712 | tf_op jit(solution)/shard_map/ppermute | solution.py:243
  46.9 0.8 pad_maximum_fusion.3
  47.7 1.5 %collective-permute-start.14 = (bf16[768,256]{1,0:T(8,128)(2,1)}, bf16[768,256]{1,0:T(8,128)(2,1)}, u32[]{:S(2)}, u32[]{:S(2)}) collective-permute-start(bf16[768,256]{1,0:T(8,128)(2,1)} %pad_maximum_fusion.3), channel_id=1, source_target_pairs={{0,16},{16,0},{1,17},{17,1},{2,18},{18,2},{3,19},{19,3},{4,20},{20... | collective-permute-start | bytes 1179656 | tf_op jit(solution)/shard_map/ppermute | solution.py:263
  49.2 0.0 collective-permute-start.16
  49.3 0.1 collective-permute-done.3.refs_7_
  49.4 2.5 %collective-permute-start.15 = (bf16[256,256]{1,0:T(8,128)(2,1)S(1)}, bf16[256,256]{1,0:T(8,128)(2,1)S(1)}, u32[]{:S(2)}, u32[]{:S(2)}) collective-permute-start(bf16[256,256]{1,0:T(8,128)(2,1)S(1)} %slice.8), channel_id=1, source_target_pairs={{0,4},{1,5},{4,8},{5,9},{8,12},{9,13},{12,14},{13,15},{14,10},{15,... | collective-permute-start | bytes 393224 | tf_op jit(solution)/shard_map/ppermute | solution.py:243
  51.9 0.8 add_convert_fusion.1
  52.7 2.6 %collective-permute-done.15.refs_10_ = bf16[256,256]{1,0:T(8,128)(2,1)S(1)} collective-permute-done((bf16[256,256]{1,0:T(8,128)(2,1)S(1)}, bf16[256,256]{1,0:T(8,128)(2,1)S(1)}, u32[]{:S(2)}, u32[]{:S(2)}) %collective-permute-start.15) | collective-permute-done | bytes 131104 | tf_op jit(solution)/shard_map/ppermute | solution.py:243
  55.3 0.0 collective-permute-start.1
  55.3 0.0 collective-permute-done.16.refs_11_
  55.3 7.0 %collective-permute-start.4 = (bf16[8,128,128]{2,1,0:T(8,128)(2,1)}, bf16[8,128,128]{2,1,0:T(8,128)(2,1)}, u32[]{:S(2)}, u32[]{:S(2)}) collective-permute-start(bf16[8,128,128]{2,1,0:T(8,128)(2,1)} %add_convert_fusion.1), channel_id=1, source_target_pairs={{0,8},{1,9},{2,10},{3,11},{4,12},{5,13},{6,14},{7,15},{16,24},{17,... | collective-permute-start | bytes 786440 | tf_op jit(solution)/shard_map/ppermute | solution.py:208
  62.2 1.0 fusion.1
  63.2 1.7 %collective-permute-start.17 = (bf16[384,256]{1,0:T(8,128)(2,1)}, bf16[384,256]{1,0:T(8,128)(2,1)}, u32[]{:S(2)}, u32[]{:S(2)}) collective-permute-start(bf16[384,256]{1,0:T(8,128)(2,1)} %fusion.1), channel_id=1, source_target_pairs={{0,16},{16,0},{1,17},{17,1},{2,18},{18,2},{3,19},{19,3},{4,20},{20... | collective-permute-start | bytes 589832 | tf_op jit(solution)/shard_map/ppermute | solution.py:263
  64.9 0.1 copy.13.index_ref.refs_3_
  65.1 0.0 copy-start.4
  65.1 1.2 %copy-done.4 = bf16[256,2048]{1,0:T(8,128)(2,1)S(1)} copy-done((bf16[256,2048]{1,0:T(8,128)(2,1)S(1)}, bf16[256,2048]{1,0:T(8,128)(2,1)}, u32[]{:S(2)}) %copy-start.4) | copy-done | bytes 1048600
  66.3 1.2 %copy-done.6 = bf16[256,2048]{1,0:T(8,128)(2,1)S(1)} copy-done((bf16[256,2048]{1,0:T(8,128)(2,1)S(1)}, bf16[256,2048]{1,0:T(8,128)(2,1)}, u32[]{:S(2)}) %copy-start.6) | copy-done | bytes 1048600
  67.6 0.9 copy-done.24
  68.5 16.6 %shard_map.83.refs_5_ = f32[512,1024]{1,0:T(8,128)S(1)} custom-call(s32[15]{0:T(128)S(1)} %fusion.2.info.refs_0_, bf16[256,2048]{1,0:T(8,128)(2,1)S(1)} %copy-done, bf16[256,2048]{1,0:T(8,128)(2,1)S(1)} %copy-done.6, bf16[256,2048]{1,0:T(8,128)(2,1)S(1)} %copy-done.4, bf16[768,1024]{1,0:T(8,128)(2,1)S(1)} %collective-permute-done.got_ref.refs_2_, ...), custom_call_target="tpu_custom_call" | custom-call | flops 536870912 | bytes 8388608 | tf_op jit(solution)/shard_map/pallas_call | solution.py:21
  85.1 0.0 copy-start.25
  85.1 5.4 %shard_map.84.refs_5_ = f32[512,1024]{1,0:T(8,128)S(1)} custom-call(s32[15]{0:T(128)S(1)} %fusion.2.info.refs_0_, bf16[256,2048]{1,0:T(8,128)(2,1)S(1)} %copy-done, bf16[768,1024]{1,0:T(8,128)(2,1)S(1)} %collective-permute-done.got_ref.refs_2_, s32[512,1]{1,0:T(8,128)S(1)} %copy.13.index_ref.refs_3_, f32[16,64,18]{2,1,0:T(8,128)S(1)} %bitcast.6, ...), custom_call_target="tpu_custom_call" | custom-call | flops 268435456 | bytes 8388608 | tf_op jit(solution)/shard_map/pallas_call | solution.py:21
  90.6 0.0 copy-start.2
  90.7 6.2 %shard_map.85.normed_ref = bf16[512,1024]{1,0:T(8,128)(2,1)S(1)} custom-call(s32[15]{0:T(128)S(1)} %fusion.2.info.refs_0_, bf16[256,2048]{1,0:T(8,128)(2,1)S(1)} %copy-done, bf16[768,1024]{1,0:T(8,128)(2,1)S(1)} %collective-permute-done.got_ref.refs_2_, s32[512,1]{1,0:T(8,128)S(1)} %copy.13.index_ref.refs_3_, f32[16,64,18]{2,1,0:T(8,128)S(1)} %bitcast.7, ...), custom_call_target="tpu_custom_call" | custom-call | flops 134217728 | bytes 8388608 | tf_op jit(solution)/shard_map/pallas_call | solution.py:21
  97.0 3.0 %shard_map.87 = bf16[256,2048]{1,0:T(8,128)(2,1)S(1)} custom-call(s32[15]{0:T(128)S(1)} %fusion.2.info.refs_0_, bf16[512,1024]{1,0:T(8,128)(2,1)S(1)} %shard_map.85.normed_ref, bf16[1024,256]{1,0:T(8,128)(2,1)S(1)} %copy-done.2, bf16[640,256]{1,0:T(8,128)(2,1)} %collective-permute-done.6.refs_1_, bf16[640,256]{1,0:T(8,128)(2,1)S(1)} %copy-done.14, ...), custom_call_target="tpu_custom_call" | custom-call | flops 1073741824 | bytes 8388608 | tf_op jit(solution)/shard_map/pallas_call | solution.py:21
  100.0 0.1 collective-permute-start.18
  100.1 2.9 %shard_map.86 = f32[256,2048]{1,0:T(8,128)S(1)} custom-call(s32[15]{0:T(128)S(1)} %fusion.2.info.refs_0_, bf16[512,1024]{1,0:T(8,128)(2,1)S(1)} %shard_map.85.normed_ref, bf16[1024,256]{1,0:T(8,128)(2,1)S(1)} %copy-done.2, bf16[640,256]{1,0:T(8,128)(2,1)} %collective-permute-done.6.refs_1_, bf16[640,256]{1,0:T(8,128)(2,1)S(1)} %copy-done.14, ...), custom_call_target="tpu_custom_call" | custom-call | flops 1073741824 | bytes 8388608 | tf_op jit(solution)/shard_map/pallas_call | solution.py:21
  103.0 1.3 %add_convert_fusion = bf16[256,2048]{1,0:T(8,128)(2,1)} fusion(f32[256,2048]{1,0:T(8,128)S(1)} %shard_map.86, bf16[256,2048]{1,0:T(8,128)(2,1)S(1)} %collective-permute-done.18), kind=kLoop, calls=%fused_computation | loop fusion | flops 1572864 | bytes 4194304 | tf_op jit(solution)/shard_map/convert_element_type | solution.py:329
  (60 shorter events, 0.3 us)
Async XLA Ops:
  2.4 1.8 %copy-start.26 = (bf16[2048,128]{1,0:T(8,128)(2,1)S(1)}, bf16[2048,128]{1,0:T(8,128)(2,1)}, u32[]{:S(2)}) copy-start(bf16[2048,128]{1,0:T(8,128)(2,1)} %param.14) | copy-start | bytes 1572868
  3.7 27.6 %collective-permute-start = (bf16[768,1024]{1,0:T(8,128)(2,1)}, bf16[768,1024]{1,0:T(8,128)(2,1)S(1)}, u32[]{:S(2)}, u32[]{:S(2)}) collective-permute-start(bf16[768,1024]{1,0:T(8,128)(2,1)} %pad_maximum_fusion), channel_id=1, source_target_pairs={{0,1},{1,0},{2,3},{3,2},{4,5},{5,4},{6,7},{7,6},{8,9},{9,8},{10,11... | collective-permute-start | bytes 4718600 | tf_op jit(solution)/shard_map/ppermute | solution.py:208
  4.2 27.1 %copy-start.3 = (bf16[256,2048]{1,0:T(8,128)(2,1)S(1)}, bf16[256,2048]{1,0:T(8,128)(2,1)}, u32[]{:S(2)}) copy-start(bf16[256,2048]{1,0:T(8,128)(2,1)} %v_ref.3) | copy-start | bytes 3145732
  4.2 3.3 %collective-permute-start.5 = (bf16[1024,128]{1,0:T(8,128)(2,1)S(1)}, bf16[1024,128]{1,0:T(8,128)(2,1)S(1)}, u32[]{:S(2)}, u32[]{:S(2)}) collective-permute-start(bf16[1024,128]{1,0:T(8,128)(2,1)S(1)} %get-tuple-element.12), channel_id=1, source_target_pairs={{0,1},{1,0},{2,3},{3,2},{4,5},{5,4},{6,7},{7,6},{8,9},{9,8},{10,11... | collective-permute-start | bytes 786440 | tf_op jit(solution)/shard_map/ppermute | solution.py:208
  8.4 0.8 copy-start.1
  9.2 11.1 %collective-permute-start.7 = (bf16[640,256]{1,0:T(8,128)(2,1)}, bf16[640,256]{1,0:T(8,128)(2,1)S(1)}, u32[]{:S(2)}, u32[]{:S(2)}) collective-permute-start(bf16[640,256]{1,0:T(8,128)(2,1)} %constant_dynamic-slice_fusion.6), channel_id=1, source_target_pairs={{4,0},{5,1},{8,4},{9,5},{12,8},{13,9},{14,12},{15,13},{10,14},{11,... | collective-permute-start | bytes 983048 | tf_op jit(solution)/shard_map/ppermute | solution.py:244
  11.8 10.2 %collective-permute-start.6 = (bf16[640,256]{1,0:T(8,128)(2,1)}, bf16[640,256]{1,0:T(8,128)(2,1)}, u32[]{:S(2)}, u32[]{:S(2)}) collective-permute-start(bf16[640,256]{1,0:T(8,128)(2,1)} %constant_dynamic-slice_fusion.6), channel_id=1, source_target_pairs={{0,4},{1,5},{4,8},{5,9},{8,12},{9,13},{12,14},{13,15},{14,10},{15,... | collective-permute-start | bytes 983048 | tf_op jit(solution)/shard_map/ppermute | solution.py:243
  13.0 18.2 %copy-start.5 = (bf16[256,2048]{1,0:T(8,128)(2,1)S(1)}, bf16[256,2048]{1,0:T(8,128)(2,1)}, u32[]{:S(2)}) copy-start(bf16[256,2048]{1,0:T(8,128)(2,1)} %k_ref.3) | copy-start | bytes 3145732
  20.3 12.0 %copy-start.13 = (bf16[640,256]{1,0:T(8,128)(2,1)}, bf16[640,256]{1,0:T(8,128)(2,1)S(1)}, u32[]{:S(2)}) copy-start(bf16[640,256]{1,0:T(8,128)(2,1)S(1)} %collective-permute-done.7.refs_2_) | copy-start | bytes 983044
  20.3 9.5 %collective-permute-start.10 = (bf16[640,256]{1,0:T(8,128)(2,1)S(1)}, bf16[640,256]{1,0:T(8,128)(2,1)S(1)}, u32[]{:S(2)}, u32[]{:S(2)}) collective-permute-start(bf16[640,256]{1,0:T(8,128)(2,1)S(1)} %collective-permute-done.7.refs_2_), channel_id=1, source_target_pairs={{4,0},{5,1},{8,4},{9,5},{12,8},{13,9},{14,12},{15,13},{10,14},{11,... | collective-permute-start | bytes 983048 | tf_op jit(solution)/shard_map/ppermute | solution.py:244
  22.0 12.6 %collective-permute-start.9 = (bf16[640,256]{1,0:T(8,128)(2,1)}, bf16[640,256]{1,0:T(8,128)(2,1)S(1)}, u32[]{:S(2)}, u32[]{:S(2)}) collective-permute-start(bf16[640,256]{1,0:T(8,128)(2,1)} %collective-permute-done.6.refs_1_), channel_id=1, source_target_pairs={{0,4},{1,5},{4,8},{5,9},{8,12},{9,13},{12,14},{13,15},{14,10},{15,... | collective-permute-start | bytes 983048 | tf_op jit(solution)/shard_map/ppermute | solution.py:243
  24.1 72.8 %collective-permute-start.8 = (bf16[768,256]{1,0:T(8,128)(2,1)}, bf16[768,256]{1,0:T(8,128)(2,1)}, u32[]{:S(2)}, u32[]{:S(2)}) collective-permute-start(bf16[768,256]{1,0:T(8,128)(2,1)} %pad_maximum_fusion.1), channel_id=1, source_target_pairs={{0,16},{16,0},{1,17},{17,1},{2,18},{18,2},{3,19},{19,3},{4,20},{20... | collective-permute-start | bytes 1179656 | tf_op jit(solution)/shard_map/ppermute | solution.py:263
  29.8 4.8 %copy-start.15 = (bf16[640,256]{1,0:T(8,128)(2,1)}, bf16[640,256]{1,0:T(8,128)(2,1)S(1)}, u32[]{:S(2)}) copy-start(bf16[640,256]{1,0:T(8,128)(2,1)S(1)} %collective-permute-done.10.refs_5_) | copy-start | bytes 983044
  29.8 13.2 %collective-permute-start.13 = (bf16[640,256]{1,0:T(8,128)(2,1)S(1)}, bf16[640,256]{1,0:T(8,128)(2,1)S(1)}, u32[]{:S(2)}, u32[]{:S(2)}) collective-permute-start(bf16[640,256]{1,0:T(8,128)(2,1)S(1)} %collective-permute-done.10.refs_5_), channel_id=1, source_target_pairs={{4,0},{5,1},{8,4},{9,5},{12,8},{13,9},{14,12},{15,13},{10,14},{11,... | collective-permute-start | bytes 983048 | tf_op jit(solution)/shard_map/ppermute | solution.py:244
  32.3 0.7 copy-start.23
  33.0 9.8 %collective-permute-start.2 = (bf16[8,128,128]{2,1,0:T(8,128)(2,1)S(1)}, bf16[8,128,128]{2,1,0:T(8,128)(2,1)S(1)}, u32[]{:S(2)}, u32[]{:S(2)}) collective-permute-start(bf16[8,128,128]{2,1,0:T(8,128)(2,1)S(1)} %get-tuple-element.9), channel_id=1, source_target_pairs={{0,2},{1,3},{2,0},{3,1},{4,6},{5,7},{6,4},{7,5},{8,10},{9,11},{10,... | collective-permute-start | bytes 786440 | tf_op jit(solution)/shard_map/ppermute | solution.py:208
  34.6 13.1 %copy-start.17 = (bf16[640,256]{1,0:T(8,128)(2,1)}, bf16[640,256]{1,0:T(8,128)(2,1)S(1)}, u32[]{:S(2)}) copy-start(bf16[640,256]{1,0:T(8,128)(2,1)S(1)} %collective-permute-done.9.refs_4_) | copy-start | bytes 983044
  35.5 61.4 %collective-permute-start.11 = (bf16[768,256]{1,0:T(8,128)(2,1)}, bf16[768,256]{1,0:T(8,128)(2,1)}, u32[]{:S(2)}, u32[]{:S(2)}) collective-permute-start(bf16[768,256]{1,0:T(8,128)(2,1)} %pad_maximum_fusion.2), channel_id=1, source_target_pairs={{0,16},{16,0},{1,17},{17,1},{2,18},{18,2},{3,19},{19,3},{4,20},{20... | collective-permute-start | bytes 1179656 | tf_op jit(solution)/shard_map/ppermute | solution.py:263
  37.0 9.8 %collective-permute-start.12 = (bf16[640,256]{1,0:T(8,128)(2,1)S(1)}, bf16[640,256]{1,0:T(8,128)(2,1)S(1)}, u32[]{:S(2)}, u32[]{:S(2)}) collective-permute-start(bf16[640,256]{1,0:T(8,128)(2,1)S(1)} %collective-permute-done.9.refs_4_), channel_id=1, source_target_pairs={{0,4},{1,5},{4,8},{5,9},{8,12},{9,13},{12,14},{13,15},{14,10},{15,... | collective-permute-start | bytes 983048 | tf_op jit(solution)/shard_map/ppermute | solution.py:243
  42.9 9.8 %copy-start.11 = (bf16[8,128,128]{2,1,0:T(8,128)(2,1)}, bf16[8,128,128]{2,1,0:T(8,128)(2,1)S(1)}, u32[]{:S(2)}) copy-start(bf16[8,128,128]{2,1,0:T(8,128)(2,1)S(1)} %collective-permute-done.2.refs_6_) | copy-start | bytes 786436
  42.9 12.4 %copy-start.27 = (s32[256]{0:T(256)S(1)}, s32[256]{0:T(256)}, u32[]{:S(2)}) copy-start(s32[256]{0:T(256)} %param.11) | copy-start | bytes 3076
  42.9 22.1 %copy-start = (bf16[256,2048]{1,0:T(8,128)(2,1)S(1)}, bf16[256,2048]{1,0:T(8,128)(2,1)}, u32[]{:S(2)}) copy-start(bf16[256,2048]{1,0:T(8,128)(2,1)} %refs_1_.3) | copy-start | bytes 3145732
  43.0 6.4 %collective-permute-start.3 = (bf16[8,128,128]{2,1,0:T(8,128)(2,1)S(1)}, bf16[8,128,128]{2,1,0:T(8,128)(2,1)S(1)}, u32[]{:S(2)}, u32[]{:S(2)}) collective-permute-start(bf16[8,128,128]{2,1,0:T(8,128)(2,1)S(1)} %fusion), channel_id=1, source_target_pairs={{0,4},{1,5},{2,6},{3,7},{4,0},{5,1},{6,2},{7,3},{8,12},{9,13},{10,... | collective-permute-start | bytes 786440 | tf_op jit(solution)/shard_map/ppermute | solution.py:208
  43.0 21.9 %copy-start.7 = (bf16[640,256]{1,0:T(8,128)(2,1)}, bf16[640,256]{1,0:T(8,128)(2,1)S(1)}, u32[]{:S(2)}) copy-start(bf16[640,256]{1,0:T(8,128)(2,1)S(1)} %collective-permute-done.13.refs_8_) | copy-start | bytes 983044
  46.9 18.1 %copy-start.9 = (bf16[640,256]{1,0:T(8,128)(2,1)}, bf16[640,256]{1,0:T(8,128)(2,1)S(1)}, u32[]{:S(2)}) copy-start(bf16[640,256]{1,0:T(8,128)(2,1)S(1)} %collective-permute-done.12.refs_7_) | copy-start | bytes 983044
  47.7 49.2 %collective-permute-start.14 = (bf16[768,256]{1,0:T(8,128)(2,1)}, bf16[768,256]{1,0:T(8,128)(2,1)}, u32[]{:S(2)}, u32[]{:S(2)}) collective-permute-start(bf16[768,256]{1,0:T(8,128)(2,1)} %pad_maximum_fusion.3), channel_id=1, source_target_pairs={{0,16},{16,0},{1,17},{17,1},{2,18},{18,2},{3,19},{19,3},{4,20},{20... | collective-permute-start | bytes 1179656 | tf_op jit(solution)/shard_map/ppermute | solution.py:263
  49.2 6.0 %collective-permute-start.16 = (bf16[384,256]{1,0:T(8,128)(2,1)S(1)}, bf16[384,256]{1,0:T(8,128)(2,1)S(1)}, u32[]{:S(2)}, u32[]{:S(2)}) collective-permute-start(bf16[384,256]{1,0:T(8,128)(2,1)S(1)} %get-tuple-element.13), channel_id=1, source_target_pairs={{4,0},{5,1},{8,4},{9,5},{12,8},{13,9},{14,12},{15,13},{10,14},{11,... | collective-permute-start | bytes 589832 | tf_op jit(solution)/shard_map/ppermute | solution.py:244
  49.4 15.5 %copy-start.21 = (bf16[8,128,128]{2,1,0:T(8,128)(2,1)}, bf16[8,128,128]{2,1,0:T(8,128)(2,1)S(1)}, u32[]{:S(2)}) copy-start(bf16[8,128,128]{2,1,0:T(8,128)(2,1)S(1)} %collective-permute-done.3.refs_7_) | copy-start | bytes 786436
  49.4 5.9 %collective-permute-start.15 = (bf16[256,256]{1,0:T(8,128)(2,1)S(1)}, bf16[256,256]{1,0:T(8,128)(2,1)S(1)}, u32[]{:S(2)}, u32[]{:S(2)}) collective-permute-start(bf16[256,256]{1,0:T(8,128)(2,1)S(1)} %slice.8), channel_id=1, source_target_pairs={{0,4},{1,5},{4,8},{5,9},{8,12},{9,13},{12,14},{13,15},{14,10},{15,... | collective-permute-start | bytes 393224 | tf_op jit(solution)/shard_map/ppermute | solution.py:243
  55.3 8.0 %collective-permute-start.1 = (s32[256]{0:T(256)S(1)}, s32[256]{0:T(256)S(1)}, u32[]{:S(2)}, u32[]{:S(2)}) collective-permute-start(s32[256]{0:T(256)S(1)} %copy-done.27), channel_id=1, source_target_pairs={{0,1},{1,0},{2,3},{3,2},{4,5},{5,4},{6,7},{7,6},{8,9},{9,8},{10,11... | collective-permute-start | bytes 3080 | tf_op jit(solution)/shard_map/ppermute | solution.py:208
  55.3 9.7 %copy-start.19 = (bf16[384,256]{1,0:T(8,128)(2,1)}, bf16[384,256]{1,0:T(8,128)(2,1)S(1)}, u32[]{:S(2)}) copy-start(bf16[384,256]{1,0:T(8,128)(2,1)S(1)} %collective-permute-done.16.refs_11_) | copy-start | bytes 589828
  55.3 35.3 %collective-permute-start.4 = (bf16[8,128,128]{2,1,0:T(8,128)(2,1)}, bf16[8,128,128]{2,1,0:T(8,128)(2,1)}, u32[]{:S(2)}, u32[]{:S(2)}) collective-permute-start(bf16[8,128,128]{2,1,0:T(8,128)(2,1)} %add_convert_fusion.1), channel_id=1, source_target_pairs={{0,8},{1,9},{2,10},{3,11},{4,12},{5,13},{6,14},{7,15},{16,24},{17,... | collective-permute-start | bytes 786440 | tf_op jit(solution)/shard_map/ppermute | solution.py:208
  63.2 33.7 %collective-permute-start.17 = (bf16[384,256]{1,0:T(8,128)(2,1)}, bf16[384,256]{1,0:T(8,128)(2,1)}, u32[]{:S(2)}, u32[]{:S(2)}) collective-permute-start(bf16[384,256]{1,0:T(8,128)(2,1)} %fusion.1), channel_id=1, source_target_pairs={{0,16},{16,0},{1,17},{17,1},{2,18},{18,2},{3,19},{19,3},{4,20},{20... | collective-permute-start | bytes 589832 | tf_op jit(solution)/shard_map/ppermute | solution.py:263
  65.1 1.2 %copy-start.4 = (bf16[256,2048]{1,0:T(8,128)(2,1)S(1)}, bf16[256,2048]{1,0:T(8,128)(2,1)}, u32[]{:S(2)}) copy-start(bf16[256,2048]{1,0:T(8,128)(2,1)} %v_ref.3) | copy-start | bytes 3145732
  66.3 1.2 %copy-start.6 = (bf16[256,2048]{1,0:T(8,128)(2,1)S(1)}, bf16[256,2048]{1,0:T(8,128)(2,1)}, u32[]{:S(2)}) copy-start(bf16[256,2048]{1,0:T(8,128)(2,1)} %k_ref.3) | copy-start | bytes 3145732
  67.5 0.9 copy-start.24
  68.5 16.6 %copy-start.12 = (bf16[8,128,128]{2,1,0:T(8,128)(2,1)S(1)}, bf16[8,128,128]{2,1,0:T(8,128)(2,1)}, u32[]{:S(2)}) copy-start(bf16[8,128,128]{2,1,0:T(8,128)(2,1)} %copy-done.11) | copy-start | bytes 786436
  68.5 16.6 %copy-start.22 = (bf16[8,128,128]{2,1,0:T(8,128)(2,1)S(1)}, bf16[8,128,128]{2,1,0:T(8,128)(2,1)}, u32[]{:S(2)}) copy-start(bf16[8,128,128]{2,1,0:T(8,128)(2,1)} %copy-done.21) | copy-start | bytes 786436
  85.1 5.5 %copy-start.25 = (f32[2048]{0:T(1024)S(1)}, f32[2048]{0:T(1024)}, u32[]{:S(2)}) copy-start(f32[2048]{0:T(1024)} %param.13) | copy-start | bytes 24580
  90.6 6.3 %copy-start.2 = (bf16[1024,256]{1,0:T(8,128)(2,1)S(1)}, bf16[1024,256]{1,0:T(8,128)(2,1)}, u32[]{:S(2)}) copy-start(bf16[1024,256]{1,0:T(8,128)(2,1)} %copy-done.1) | copy-start | bytes 1572868
  90.6 6.3 %copy-start.8 = (bf16[640,256]{1,0:T(8,128)(2,1)S(1)}, bf16[640,256]{1,0:T(8,128)(2,1)}, u32[]{:S(2)}) copy-start(bf16[640,256]{1,0:T(8,128)(2,1)} %copy-done.7) | copy-start | bytes 983044
  90.6 6.3 %copy-start.10 = (bf16[640,256]{1,0:T(8,128)(2,1)S(1)}, bf16[640,256]{1,0:T(8,128)(2,1)}, u32[]{:S(2)}) copy-start(bf16[640,256]{1,0:T(8,128)(2,1)} %copy-done.9) | copy-start | bytes 983044
  90.6 6.3 %copy-start.14 = (bf16[640,256]{1,0:T(8,128)(2,1)S(1)}, bf16[640,256]{1,0:T(8,128)(2,1)}, u32[]{:S(2)}) copy-start(bf16[640,256]{1,0:T(8,128)(2,1)} %copy-done.13) | copy-start | bytes 983044
  90.6 6.3 %copy-start.16 = (bf16[640,256]{1,0:T(8,128)(2,1)S(1)}, bf16[640,256]{1,0:T(8,128)(2,1)}, u32[]{:S(2)}) copy-start(bf16[640,256]{1,0:T(8,128)(2,1)} %copy-done.15) | copy-start | bytes 983044
  90.6 6.3 %copy-start.18 = (bf16[640,256]{1,0:T(8,128)(2,1)S(1)}, bf16[640,256]{1,0:T(8,128)(2,1)}, u32[]{:S(2)}) copy-start(bf16[640,256]{1,0:T(8,128)(2,1)} %copy-done.17) | copy-start | bytes 983044
  90.7 6.3 %copy-start.20 = (bf16[384,256]{1,0:T(8,128)(2,1)S(1)}, bf16[384,256]{1,0:T(8,128)(2,1)}, u32[]{:S(2)}) copy-start(bf16[384,256]{1,0:T(8,128)(2,1)} %copy-done.19) | copy-start | bytes 589828
  100.0 3.0 %collective-permute-start.18 = (bf16[256,2048]{1,0:T(8,128)(2,1)S(1)}, bf16[256,2048]{1,0:T(8,128)(2,1)S(1)}, u32[]{:S(2)}, u32[]{:S(2)}) collective-permute-start(bf16[256,2048]{1,0:T(8,128)(2,1)S(1)} %shard_map.87), channel_id=1, source_target_pairs={{0,1},{1,0},{2,3},{3,2},{4,5},{5,4},{6,7},{7,6},{8,9},{9,8},{10,11... | collective-permute-start | bytes 3145736 | tf_op jit(solution)/shard_map/ppermute | solution.py:208

commit v2 on v1

v2 whole, which is shorter than its diff:
```python
import functools
import math

import numpy as np

import jax
import jax.numpy as jnp
from jax import lax
from jax.experimental import pallas as pl
from jax.experimental.pallas import tpu as pltpu
from jax.sharding import PartitionSpec as P

TILE = 128
VM = pl.BlockSpec(memory_space=pltpu.VMEM)
SM = pl.BlockSpec(memory_space=pltpu.SMEM)
PARAMS = pltpu.CompilerParams(vmem_limit_bytes=8 * 1024 * 1024)


def call(kernel, out_shape, in_specs, flops, moved, *operands):
    outs = jax.tree.map(lambda _: VM, out_shape)
    return pl.pallas_call(
        kernel,
        out_shape=out_shape,
        in_specs=in_specs,
        out_specs=outs,
        compiler_params=PARAMS,
        cost_estimate=pl.CostEstimate(flops=flops, bytes_accessed=moved, transcendentals=0),
    )(*operands)


def us(microseconds):
    return int(microseconds * 1.15e9)


def lanes(start, size):
    return pl.ds(pl.multiple_of(start, TILE), size)


def dot(a, b, ca=1, cb=0):
    return lax.dot_general(a, b, (((ca,), (cb,)), ((), ())), preferred_element_type=jnp.float32)


def split_kernel(k_ref, v_ref, q_ref, w_ref, index_ref, sent_ref, mine_ref, w_sent_ref, w_mine_ref, sems):
    rows, half = mine_ref.shape[0] // 3, mine_ref.shape[1]
    deep = w_mine_ref.shape[0]
    core = lax.axis_index("seq") % 2
    copies = []
    for to_other, big, small in ((1, sent_ref, w_sent_ref), (0, mine_ref, w_mine_ref)):
        side = (core + to_other) % 2
        for at, ref in enumerate((k_ref, v_ref, q_ref)):
            copies.append((ref.at[:, lanes(side * half, half)], big.at[pl.ds(at * rows, rows), :]))
        copies.append((w_ref.at[pl.ds(pl.multiple_of(side * deep, 16), deep), :], small))
    copies = [pltpu.make_async_copy(a, b, sems.at[n]) for n, (a, b) in enumerate(copies)]
    for copy in copies:
        copy.start()
    if sent_ref.shape[0] > 3 * rows:
        tail = sent_ref.shape[0] - 3 * rows
        row = jnp.broadcast_to(index_ref[...].astype(jnp.float32), (tail, rows)).astype(jnp.bfloat16)
        sent_ref[pl.ds(3 * rows, tail), :] = jnp.zeros((tail, half), jnp.bfloat16)
        sent_ref[pl.ds(3 * rows, tail), pl.ds(0, rows)] = row
    for copy in copies:
        copy.wait()


def state_kernel(info, mine_ref, got_ref, sum_ref, send_ref, even_ref):
    heads, dim, _ = sum_ref.shape
    rows = mine_ref.shape[0] // 3
    core = info[0]
    for h in range(heads):
        far = pl.ds(h * dim, dim)
        mine = dot(mine_ref[pl.ds(rows, rows), far], mine_ref[pl.ds(0, rows), far], 0, 0)
        theirs = dot(got_ref[pl.ds(rows, rows), far], got_ref[pl.ds(0, rows), far], 0, 0)
        both = mine + theirs
        sum_ref[h] = both
        send_ref[h] = both.astype(jnp.bfloat16)
        even_ref[h] = jnp.where(core == 0, mine, theirs).astype(jnp.bfloat16)


def local_kernel(lam_ref, part_ref, out_ref):
    heads = lam_ref.shape[0]
    dim, rows = out_ref.shape[0] // heads, out_ref.shape[1]
    scale = 1.0 / math.sqrt(dim)
    step = min(TILE, rows)
    blocks = rows // step
    log_step = step.bit_length() - 1
    s_at = lax.broadcasted_iota(jnp.int32, (step, step), 0)
    t_at = lax.broadcasted_iota(jnp.int32, (step, step), 1)
    grid = jnp.zeros((step, step), jnp.int32)
    for bit in range(log_step):
        grid = grid + (jnp.right_shift(t_at, bit) != jnp.right_shift(s_at, bit)).astype(jnp.int32)
    grid = jnp.where(s_at <= t_at, grid, -1)
    for h in range(heads):

        def part(which, first, count):
            return part_ref[pl.ds(which * rows + first, count), pl.ds(h * dim, dim)]

        lam = lam_ref[h] * scale
        totals = [None] * blocks
        for s in range(blocks):
            scores = dot(part(0, s * step, step), part(2, s * step, rows - s * step), 1, 1)
            weighted = []
            for t in range(s, blocks):
                lam_t = lam[:, t * step : (t + 1) * step]
                if s == t:
                    picked = jnp.zeros((step, step), jnp.float32)
                    for level in range(log_step + 1):
                        picked = jnp.where(grid == level, lam_t[level : level + 1], picked)
                else:
                    level = log_step + (s ^ t).bit_length()
                    picked = lam_t[level : level + 1]
                weighted.append((picked * scores[:, (t - s) * step : (t - s + 1) * step]).astype(jnp.bfloat16))
            joined = weighted[0] if len(weighted) == 1 else jnp.concatenate(weighted, axis=1)
            add = dot(part(1, s * step, step), joined, 0, 0)
            for t in range(s, blocks):
                term = add[:, (t - s) * step : (t - s + 1) * step]
                totals[t] = term if totals[t] is None else totals[t] + term
        for t in range(blocks):
            out_ref[pl.ds(h * dim, dim), pl.ds(t * step, step)] = totals[t]


def early_kernel(levels, log_stretch, info, mine_ref, got_ref, lam0_ref, lam1_ref, base0_ref, base1_ref, *refs):
    buckets, out_ref = refs[:-1], refs[-1]
    heads = lam0_ref.shape[0]
    rows = mine_ref.shape[0] // 3
    dim = base0_ref.shape[0] // heads
    core = info[0]
    scale = 1.0 / math.sqrt(dim)
    for h in range(heads):
        far = pl.ds(h * dim, dim)
        for side in range(2):
            odd = core if side == 0 else 1 - core
            lam = (lam0_ref, lam1_ref)[side][h]
            q = (mine_ref, got_ref)[side][pl.ds(2 * rows, rows), far]
            total = (base0_ref, base1_ref)[side][far, :]
            for at, level in enumerate(levels):
                column = log_stretch + 1 + level
                on = odd if level == 0 else info[1 + level]
                weight = jnp.where(on == 1, lam[column : column + 1] * scale, 0.0)
                total = total + weight * dot(buckets[at][h], q, 1, 1)
            out_ref[far, pl.ds(side * rows, rows)] = total


def last_kernel(level, log_stretch, info, mine_ref, got_ref, lam0_ref, lam1_ref, base_ref, bucket_ref, gain_ref, out_ref):
    heads = lam0_ref.shape[0]
    rows = mine_ref.shape[0] // 3
    dim = base_ref.shape[0] // heads
    core = info[0]
    scale = 1.0 / math.sqrt(dim)
    column = log_stretch + 1 + level
    for h in range(heads):
        far = pl.ds(h * dim, dim)
        own = lanes(core * heads * dim + h * dim, dim)
        for side in range(2):
            at_rows = pl.ds(side * rows, rows)
            lam = (lam0_ref, lam1_ref)[side][h]
            q = (mine_ref, got_ref)[side][pl.ds(2 * rows, rows), far]
            weight = jnp.where(info[1 + level] == 1, lam[column : column + 1] * scale, 0.0)
            total = base_ref[far, at_rows] + weight * dot(bucket_ref[h], q, 1, 1)
            mean = jnp.mean(total * total, axis=0, keepdims=True)
            total = total * lax.rsqrt(mean + 1e-06)
            out_ref[at_rows, far] = (jnp.transpose(total) * gain_ref[:, own]).astype(out_ref.dtype)


def project_kernel(side, plan, info, normed_ref, *refs):
    out_ref = refs[-1]
    rows = out_ref.shape[0]
    for chip_slot, parts in plan:
        total = None
        for at, row0, k_slot, k_add, size in parts:
            piece = refs[at]
            start = k_add if k_slot is None else info[k_slot] + k_add
            a = normed_ref[pl.ds(side * rows, rows), lanes(start, size)]
            term = dot(a, piece[pl.ds(row0, size), :])
            total = term if total is None else total + term
        width = refs[parts[0][0]].shape[1]
        column = 0 if chip_slot is None else info[chip_slot] * width
        out_ref[:, lanes(column, width)] = total.astype(out_ref.dtype)


def ring_order(chips):
    return list(range(0, chips, 2)) + list(range(chips - 1, 0, -2))


def body(groups, queries, keys, values, level_index, level_table, norm_gain, out_weight):
    stretch, width = queries.shape
    table_rows, level_count, heads = level_table.shape
    head_dim = width // heads
    columns = out_weight.shape[1]
    log_stretch = stretch.bit_length() - 1
    devices = lax.axis_size("seq")
    log_blocks = devices.bit_length() - 1
    rank = lax.axis_index("seq")
    group = lax.axis_index("grp")
    core = rank % 2
    half = width // 2
    pair_heads = heads // 2
    chips = devices // 2
    ringed = (2 * columns) % TILE == 0 and chips >= 4
    shared = (3 * half // 8) // TILE * TILE if ringed and groups == 2 else 0
    kept = half - shared
    cut = kept // TILE // 2 * TILE

    order = ring_order(chips)
    facts = np.zeros((groups, devices, 1 + log_blocks + 2 + chips), np.int32)
    for g in range(groups):
        for r in range(devices):
            place = order.index(r // 2) if ringed else 0
            facts[g, r] = (
                [r % 2]
                + [r >> bit & 1 for bit in range(log_blocks)]
                + [g * shared, (1 - g) * kept]
                + [order[(place - d) % chips] if ringed else 0 for d in range(chips)]
            )
    k_mine, k_lacks, chip_at = 1 + log_blocks, 2 + log_blocks, 3 + log_blocks
    info = lax.dynamic_slice(jnp.asarray(facts), (group, rank, 0), (1, 1, facts.shape[2])).reshape(-1)

    def swap(block, bit, upward=False):
        route = [(r, r ^ 1 << bit) for r in range(devices) if not (upward and r >> bit & 1)]
        return lax.ppermute(block, "seq", route)

    packs = table_rows <= 256 and stretch <= half
    bf16 = functools.partial(jax.ShapeDtypeStruct, dtype=jnp.bfloat16)
    sent, mine, w_sent, w_own = pl.pallas_call(
        split_kernel,
        out_shape=(
            bf16(((3 * stretch + 16) if packs else 3 * stretch, half)),
            bf16((3 * stretch, half)),
            bf16((half, columns)),
            bf16((half, columns)),
        ),
        in_specs=[pl.BlockSpec(memory_space=pltpu.HBM)] * 4 + [VM],
        out_specs=(VM,) * 4,
        scratch_shapes=[pltpu.SemaphoreType.DMA((8,))],
        compiler_params=pltpu.CompilerParams(vmem_limit_bytes=56 * 1024 * 1024),
        cost_estimate=pl.CostEstimate(flops=us(1.5), bytes_accessed=1 << 21, transcendentals=0),
    )(keys, values, queries, out_weight, level_index.reshape(1, stretch))
    got = swap(sent, 0)
    if packs:
        index_got = got[3 * stretch, :stretch].astype(jnp.int32)
    else:
        index_got = swap(level_index, 0)

    w_got = swap(w_sent, 0)
    whole = jnp.where(
        core == 0,
        jnp.concatenate([w_own, w_got], axis=1),
        jnp.concatenate([w_got, w_own], axis=1),
    )

    table = jnp.transpose(level_table, (2, 1, 0))
    table = jnp.where(core == 0, table[:pair_heads], table[pair_heads:]).reshape(-1, table_rows)

    def level_weights(index):
        found = (index[None, :] == jnp.arange(table_rows, dtype=jnp.int32)[:, None]).astype(jnp.float32)
        lam = jnp.dot(table, found, precision=lax.Precision.HIGHEST)
        return lam.reshape(pair_heads, level_count, stretch)

    lam_own = level_weights(level_index)
    lam_got = level_weights(index_got)

    state = jax.ShapeDtypeStruct((pair_heads, head_dim, head_dim), jnp.float32)
    state16 = jax.ShapeDtypeStruct(state.shape, jnp.bfloat16)
    total, send, even = call(
        state_kernel,
        (state, state16, state16),
        [SM] + [VM] * 2,
        us(1.0),
        1 << 20,
        info, mine, got,
    )
    buckets = [even]
    reached = [send]
    upper = jnp.right_shift(rank, 1) % 2
    for bit in range(1, log_blocks):
        came = swap(send, bit, upward=bit == log_blocks - 1)
        if bit + 1 < log_blocks:
            total = total + came
            if bit == 1:
                total = jnp.where(upper == 0, total[: pair_heads // 2], total[pair_heads // 2 :])
            send = total.astype(jnp.bfloat16)
            reached.append(send)
        if bit > 1:
            rest = swap(came, 1)
            came = jnp.where(
                upper == 0, jnp.concatenate([came, rest], axis=0), jnp.concatenate([rest, came], axis=0)
            )
        buckets.append(came)

    pieces = []
    plan = []
    crossed = []
    if ringed:
        clockwise = []
        for at, chip in enumerate(order):
            follows = order[(at + 1) % chips]
            clockwise += [(2 * chip + c, 2 * follows + c) for c in range(2)]
        counter = [(b, a) for a, b in clockwise]
        pieces.append(whole)
        plan.append((chip_at, [(0, 0, None, 0, half)]))
        right = left = jnp.where(group % 2 == 0, whole[:kept], whole[shared:]) if shared else whole
        rounds = chips // 2
        for r in range(1, rounds + 1):
            last = r == rounds
            ahead = reached[r - 1 : r] + crossed[r - 3 : r - 2] * (r >= 3)
            right, left, *_ = lax.optimization_barrier((right, left, *ahead))
            if last:
                right, left = right[:cut], left[cut:]
            right = lax.ppermute(right, "seq", clockwise)
            left = lax.ppermute(left, "seq", counter)
            at = len(pieces)
            pieces += [right, left]
            if last:
                parts = [[(at, 0, k_mine, 0, cut), (at + 1, 0, k_mine, cut, kept - cut)]]
                distances = [r]
            else:
                parts = [[(at, 0, k_mine, 0, kept)], [(at + 1, 0, k_mine, 0, kept)]]
                distances = [r, chips - r]
            if shared:
                held = [jnp.concatenate([right, left], axis=0)] if last else [right, left]
                low, high = ([x[at:][:shared] for x in held] for at in (0, kept - shared))
                wanted = jnp.where(group == 0, jnp.concatenate(low, axis=0), jnp.concatenate(high, axis=0))
                crossed.append(lax.ppermute(wanted, "grp", [(0, 1), (1, 0)]))
                pieces.append(crossed[-1])
                for n, part in enumerate(parts):
                    part.append((at + 2, n * shared, k_lacks, 0, shared))
            plan += [(chip_at + d, part) for d, part in zip(distances, parts)]
    else:
        full = lax.all_gather(out_weight, "seq", axis=1, tiled=True)
        pieces.append(lax.dynamic_slice(full, (core * half, 0), (half, width)))
        plan.append((None, [(0, 0, None, 0, half)]))

    side_shape = jax.ShapeDtypeStruct((half, stretch), jnp.float32)
    acc_own = call(
        local_kernel, side_shape, [VM] * 2, us(2.9), 1 << 21, lam_own, mine,
    )
    acc_got = call(
        local_kernel, side_shape, [VM] * 2, us(2.9), 1 << 21, lam_got, got,
    )
    early = list(range(log_blocks - 1))
    acc = call(
        functools.partial(early_kernel, early, log_stretch),
        jax.ShapeDtypeStruct((half, 2 * stretch), jnp.float32),
        [SM] + [VM] * (6 + len(early)),
        us(3.5),
        1 << 21,
        info, mine, got, lam_own, lam_got, acc_own, acc_got, *buckets[:-1],
    )
    normed = call(
        functools.partial(last_kernel, log_blocks - 1, log_stretch),
        jax.ShapeDtypeStruct((2 * stretch, half), jnp.bfloat16),
        [SM] + [VM] * 7,
        us(2.5),
        1 << 21,
        info, mine, got, lam_own, lam_got, acc, buckets[-1], norm_gain.reshape(1, width),
    )

    def project(side, dtype):
        return call(
            functools.partial(project_kernel, side, plan),
            jax.ShapeDtypeStruct((stretch, width), dtype),
            [SM] + [VM] * (1 + len(pieces)),
            us(3.0),
            1 << 21,
            info, normed, *pieces,
        )

    came = swap(project(1, jnp.bfloat16), 0)
    return (project(0, jnp.float32) + came).astype(jnp.bfloat16)


def solution(mesh):
    placed = (
        P(("grp", "seq"), None),
        P(("grp", "seq"), None),
        P(("grp", "seq"), None),
        P(("grp", "seq")),
        P(),
        P(),
        P(None, "seq"),
    )
    return jax.shard_map(
        functools.partial(body, mesh.shape["grp"]),
        mesh=mesh,
        in_specs=placed,
        out_specs=P(("grp", "seq"), None),
        check_vma=False,
    )
```

time: 105 us -> 78.5 us (0.75)
  Pallas kernels: 35.2 us -> 17 us
  local copies, waits for them, and re-layouts: 11.3 us -> 3.19 us
  other arithmetic: 7.08 us -> 2.05 us
  waiting for transfers between devices: 24.4 us -> 27 us
  starting transfers between devices: 25.8 us -> 28.2 us
    pallas_call x6 -> x7, Pallas kernels: 35.2 us -> 12.4 us  [call(): pl.pallas_call(kernel, out_shape=out_shape, in_specs=in_specs, out_specs=...]
    ppermute x4, waiting for transfers between devices: 0.01 us -> 9.04 us  [body(): crossed.append(lax.ppermute(wanted, 'grp', [(0, 1), (1, 0)]))]
    ppermute x4, waiting for transfers between devices: 10.5 us -> 3.59 us  [body(): left = lax.ppermute(left, 'seq', counter)]
    concatenate x6 -> x0, other arithmetic: 4.73 us -> none  [the longest x3 2.46 us: body(): jnp.concatenate([lax.dynamic_slice(x, (first, 0), (shared, 2 * columns))...]
    pallas_call x0 -> x1, Pallas kernels: none -> 4.62 us  [body(): pl.pallas_call(split_kernel, out_shape=(bf16((3 * stretch + 16 if packs e...]
    ppermute x7 -> x8, starting transfers between devices: 9.27 us -> 13.7 us  [swap(): return lax.ppermute(block, 'seq', route)]
    ppermute x4, waiting for transfers between devices: 6.33 us -> 10.7 us  [body(): right = lax.ppermute(right, 'seq', clockwise)]
    dynamic_slice x9 -> x0, local copies, waits for them, and re-layouts: 4.17 us -> none  [the longest x2 2.35 us: body(): lax.dynamic_slice(x, (0, other), (stretch, half))]
  transfers between devices with their start and end apart: 19 -> 20, of which waited for: 7 -> 11; matrix products, arithmetic and copies ran while one was open for 8% -> 2% of each run, Pallas kernels for 31% -> 12%
where the time goes in v2:
time: 78.5 us; the launch traced here: 78.3 us
  starting transfers between devices  28.2 us (36%)
  waiting for transfers between devices  27 us (34%)
  Pallas kernels  17 us (22%)
  local copies, waits for them, and re-layouts  3.19 us (4%)
  other arithmetic  2.05 us (3%)
    ppermute x8, starting transfers between devices, swap(): return lax.ppermute(block, 'seq', route)  13.7 us
    pallas_call x7, Pallas kernels, call(): pl.pallas_call(kernel, out_shape=out_shape, in_specs=in_specs, out_specs=...  12.4 us
    ppermute x4, waiting for transfers between devices, body(): right = lax.ppermute(right, 'seq', clockwise)  10.7 us
    ppermute x4, waiting for transfers between devices, body(): crossed.append(lax.ppermute(wanted, 'grp', [(0, 1), (1, 0)]))  9.04 us
    ppermute x4, starting transfers between devices, body(): crossed.append(lax.ppermute(wanted, 'grp', [(0, 1), (1, 0)]))  6.32 us
    pallas_call x1, Pallas kernels, body(): pl.pallas_call(split_kernel, out_shape=(bf16((3 * stretch + 16 if packs e...  4.62 us
    ppermute x4, starting transfers between devices, body(): left = lax.ppermute(left, 'seq', counter)  4.53 us
    ppermute x8, waiting for transfers between devices, swap(): return lax.ppermute(block, 'seq', route)  3.69 us
  transfers between devices with their start and end apart: 20, of which 11 were waited for; matrix products, arithmetic and copies ran while one was open for 2% of the time, Pallas kernels for 12%

profile of v2, /device:TPU:0, one launch (start us, length us, event | category | flops | bytes accessed | tf_op | source)
XLA Modules:
  0.0 78.3 jit_solution(4936804252611280275)
XLA Ops:
  0.0 4.6 %shard_map.82 = (bf16[784,1024]{1,0:T(8,128)(2,1)}, bf16[768,1024]{1,0:T(8,128)(2,1)}, bf16[1024,128]{1,0:T(8,128)(2,1)}, bf16[1024,128]{1,0:T(8,128)(2,1)}) custom-call(bf16[256,2048]{1,0:T(8,128)(2,1)} %k_ref.1, bf16[256,2048]{1,0:T(8,128)(2,1)} %v_ref.1, bf16[256,2048]{1,0:T(8,128)(2,1)} %q_ref.1, bf16[2048,128]{1,0:T(8,128)(2,1)} %w_ref.1, s32[1,256]{1,0:T(1,128)} %bitcast.15), custom_call_target="tpu_custom_call" | custom-call | flops 1724999936 | bytes 2097152 | tf_op jit(solution)/shard_map/pallas_call | solution.py:223
  4.6 0.5 collective-permute-start
  5.2 0.1 collective-permute-start.6
  5.2 0.7 dynamic-slice_bitcast_fusion.info
  5.9 0.0 copy-done.4
  5.9 0.0 copy-done.5
  5.9 0.2 fusion.3.lam_ref.lam0_ref
  6.2 0.0 copy-start.1
  6.2 1.4 %copy-done.1 = bf16[768,1024]{1,0:T(8,128)(2,1)S(1)} copy-done((bf16[768,1024]{1,0:T(8,128)(2,1)S(1)}, bf16[768,1024]{1,0:T(8,128)(2,1)}, u32[]{:S(2)}) %copy-start.1) | copy-done | bytes 1572888
  7.6 2.1 %shard_map.83.base0_ref = f32[1024,256]{1,0:T(8,128)S(1)} custom-call(f32[8,18,256]{2,1,0:T(8,128)S(1)} %fusion.3.lam_ref.lam0_ref, bf16[768,1024]{1,0:T(8,128)(2,1)S(1)} %copy-done.1), custom_call_target="tpu_custom_call" | custom-call | flops 3335000064 | bytes 2097152 | tf_op jit(solution)/shard_map/pallas_call | solution.py:21
  9.7 0.0 copy-start.2
  9.7 0.0 collective-permute-done.6
  9.7 0.2 maximum_select_fusion.refs_0_
  9.9 0.0 collective-permute-done.part_ref.got_ref
  10.0 0.2 fusion.1.lam_ref.lam1_ref
  10.2 0.9 %copy-done.2 = bf16[768,1024]{1,0:T(8,128)(2,1)S(1)} copy-done((bf16[768,1024]{1,0:T(8,128)(2,1)S(1)}, bf16[768,1024]{1,0:T(8,128)(2,1)}, u32[]{:S(2)}) %copy-start.2) | copy-done | bytes 1572888
  11.1 1.0 %shard_map.85 = (f32[8,128,128]{2,1,0:T(8,128)S(1)}, bf16[8,128,128]{2,1,0:T(8,128)(2,1)S(1)}, bf16[8,128,128]{2,1,0:T(8,128)(2,1)S(1)}) custom-call(s32[15]{0:T(128)S(1)} %dynamic-slice_bitcast_fusion.info, bf16[768,1024]{1,0:T(8,128)(2,1)S(1)} %copy-done.2, bf16[784,1024]{1,0:T(8,128)(2,1)S(1)} %collective-permute-done.part_ref.got_ref), custom_call_target="tpu_custom_call" | custom-call | flops 1150000000 | bytes 1048576 | tf_op jit(solution)/shard_map/pallas_call | solution.py:21
  12.1 3.0 %collective-permute-start.1 = (bf16[8,128,128]{2,1,0:T(8,128)(2,1)S(1)}, bf16[8,128,128]{2,1,0:T(8,128)(2,1)S(1)}, u32[]{:S(2)}, u32[]{:S(2)}) collective-permute-start(bf16[8,128,128]{2,1,0:T(8,128)(2,1)S(1)} %get-tuple-element.23), channel_id=1, source_target_pairs={{0,2},{1,3},{2,0},{3,1},{4,6},{5,7},{6,4},{7,5},{8,10},{9,11},{10,... | collective-permute-start | bytes 786440 | tf_op jit(solution)/shard_map/ppermute | solution.py:219
  15.1 1.6 %collective-permute-start.7 = (bf16[640,256]{1,0:T(8,128)(2,1)S(1)}, bf16[640,256]{1,0:T(8,128)(2,1)S(1)}, u32[]{:S(2)}, u32[]{:S(2)}) collective-permute-start(bf16[640,256]{1,0:T(8,128)(2,1)S(1)} %slice_select_fusion), channel_id=1, source_target_pairs={{0,4},{1,5},{4,8},{5,9},{8,12},{9,13},{12,14},{13,15},{14,10},{15,... | collective-permute-start | bytes 983048 | tf_op jit(solution)/shard_map/ppermute | solution.py:308
  16.7 0.4 collective-permute-start.8
  17.1 2.1 %shard_map.84.base1_ref = f32[1024,256]{1,0:T(8,128)S(1)} custom-call(f32[8,18,256]{2,1,0:T(8,128)S(1)} %fusion.1.lam_ref.lam1_ref, bf16[784,1024]{1,0:T(8,128)(2,1)S(1)} %collective-permute-done.part_ref.got_ref), custom_call_target="tpu_custom_call" | custom-call | flops 3335000064 | bytes 2097152 | tf_op jit(solution)/shard_map/pallas_call | solution.py:21
  19.2 3.0 %collective-permute-done.1.refs_1_ = bf16[8,128,128]{2,1,0:T(8,128)(2,1)S(1)} collective-permute-done((bf16[8,128,128]{2,1,0:T(8,128)(2,1)S(1)}, bf16[8,128,128]{2,1,0:T(8,128)(2,1)S(1)}, u32[]{:S(2)}, u32[]{:S(2)}) %collective-permute-start.1) | collective-permute-done | bytes 262176 | tf_op jit(solution)/shard_map/ppermute | solution.py:219
  22.3 1.3 %collective-permute-start.2 = (bf16[4,128,128]{2,1,0:T(8,128)(2,1)S(1)}, bf16[4,128,128]{2,1,0:T(8,128)(2,1)S(1)}, u32[]{:S(2)}, u32[]{:S(2)}) collective-permute-start(bf16[4,128,128]{2,1,0:T(8,128)(2,1)S(1)} %fusion.5), channel_id=1, source_target_pairs={{0,4},{1,5},{2,6},{3,7},{4,0},{5,1},{6,2},{7,3},{8,12},{9,13},{10,... | collective-permute-start | bytes 393224 | tf_op jit(solution)/shard_map/ppermute | solution.py:219
  23.6 5.1 %collective-permute-done.7.refs_1_ = bf16[640,256]{1,0:T(8,128)(2,1)S(1)} collective-permute-done((bf16[640,256]{1,0:T(8,128)(2,1)S(1)}, bf16[640,256]{1,0:T(8,128)(2,1)S(1)}, u32[]{:S(2)}, u32[]{:S(2)}) %collective-permute-start.7) | collective-permute-done | bytes 327712 | tf_op jit(solution)/shard_map/ppermute | solution.py:308
  28.7 0.0 collective-permute-done.8.refs_2_
  28.7 0.0 collective-permute-start.10
  28.7 2.0 %collective-permute-start.11 = (bf16[640,256]{1,0:T(8,128)(2,1)S(1)}, bf16[640,256]{1,0:T(8,128)(2,1)S(1)}, u32[]{:S(2)}, u32[]{:S(2)}) collective-permute-start(bf16[640,256]{1,0:T(8,128)(2,1)S(1)} %collective-permute-done.8.refs_2_), channel_id=1, source_target_pairs={{4,0},{5,1},{8,4},{9,5},{12,8},{13,9},{14,12},{15,13},{10,14},{11,... | collective-permute-start | bytes 983048 | tf_op jit(solution)/shard_map/ppermute | solution.py:309
  30.8 0.0 collective-permute-done.2
  30.8 4.3 %collective-permute-start.4 = (bf16[4,128,128]{2,1,0:T(8,128)(2,1)S(1)}, bf16[4,128,128]{2,1,0:T(8,128)(2,1)S(1)}, u32[]{:S(2)}, u32[]{:S(2)}) collective-permute-start(bf16[4,128,128]{2,1,0:T(8,128)(2,1)S(1)} %add_convert_fusion.1), channel_id=1, source_target_pairs={{0,8},{1,9},{2,10},{3,11},{4,12},{5,13},{6,14},{7,15},{16,24},{17,... | collective-permute-start | bytes 393224 | tf_op jit(solution)/shard_map/ppermute | solution.py:219
  35.1 1.6 %collective-permute-start.3 = (bf16[4,128,128]{2,1,0:T(8,128)(2,1)S(1)}, bf16[4,128,128]{2,1,0:T(8,128)(2,1)S(1)}, u32[]{:S(2)}, u32[]{:S(2)}) collective-permute-start(bf16[4,128,128]{2,1,0:T(8,128)(2,1)S(1)} %collective-permute-done.2), channel_id=1, source_target_pairs={{0,2},{1,3},{2,0},{3,1},{4,6},{5,7},{6,4},{7,5},{8,10},{9,11},{10,... | collective-permute-start | bytes 393224 | tf_op jit(solution)/shard_map/ppermute | solution.py:219
  36.7 0.1 maximum_select_fusion.1
  36.8 1.6 %collective-permute-start.9 = (bf16[768,256]{1,0:T(8,128)(2,1)S(1)}, bf16[768,256]{1,0:T(8,128)(2,1)S(1)}, u32[]{:S(2)}, u32[]{:S(2)}) collective-permute-start(bf16[768,256]{1,0:T(8,128)(2,1)S(1)} %maximum_select_fusion.1), channel_id=1, source_target_pairs={{0,16},{16,0},{1,17},{17,1},{2,18},{18,2},{3,19},{19,3},{4,20},{20... | collective-permute-start | bytes 1179656 | tf_op jit(solution)/shard_map/ppermute | solution.py:322
  38.4 0.1 collective-permute-done.4
  38.5 2.9 %collective-permute-start.5 = (bf16[4,128,128]{2,1,0:T(8,128)(2,1)S(1)}, bf16[4,128,128]{2,1,0:T(8,128)(2,1)S(1)}, u32[]{:S(2)}, u32[]{:S(2)}) collective-permute-start(bf16[4,128,128]{2,1,0:T(8,128)(2,1)S(1)} %collective-permute-done.4), channel_id=1, source_target_pairs={{0,2},{1,3},{2,0},{3,1},{4,6},{5,7},{6,4},{7,5},{8,10},{9,11},{10,... | collective-permute-start | bytes 393224 | tf_op jit(solution)/shard_map/ppermute | solution.py:219
  41.4 0.0 collective-permute-done.3
  41.5 0.0 collective-permute-done.11.refs_5_
  41.5 0.0 collective-permute-done.10.refs_4_
  41.5 0.1 maximum_select_fusion.2
  41.7 1.6 %collective-permute-start.12 = (bf16[768,256]{1,0:T(8,128)(2,1)S(1)}, bf16[768,256]{1,0:T(8,128)(2,1)S(1)}, u32[]{:S(2)}, u32[]{:S(2)}) collective-permute-start(bf16[768,256]{1,0:T(8,128)(2,1)S(1)} %maximum_select_fusion.2), channel_id=1, source_target_pairs={{0,16},{16,0},{1,17},{17,1},{2,18},{18,2},{3,19},{19,3},{4,20},{20... | collective-permute-start | bytes 1179656 | tf_op jit(solution)/shard_map/ppermute | solution.py:322
  43.2 5.7 %collective-permute-done.9.refs_3_ = bf16[768,256]{1,0:T(8,128)(2,1)S(1)} collective-permute-done((bf16[768,256]{1,0:T(8,128)(2,1)S(1)}, bf16[768,256]{1,0:T(8,128)(2,1)S(1)}, u32[]{:S(2)}, u32[]{:S(2)}) %collective-permute-start.9) | collective-permute-done | bytes 393248 | tf_op jit(solution)/shard_map/ppermute | solution.py:322
  48.9 2.0 %collective-permute-start.13 = (bf16[640,256]{1,0:T(8,128)(2,1)S(1)}, bf16[640,256]{1,0:T(8,128)(2,1)S(1)}, u32[]{:S(2)}, u32[]{:S(2)}) collective-permute-start(bf16[640,256]{1,0:T(8,128)(2,1)S(1)} %collective-permute-done.10.refs_4_), channel_id=1, source_target_pairs={{0,4},{1,5},{4,8},{5,9},{8,12},{9,13},{12,14},{13,15},{14,10},{15,... | collective-permute-start | bytes 983048 | tf_op jit(solution)/shard_map/ppermute | solution.py:308
  51.0 0.0 collective-permute-start.14
  51.0 1.6 %shard_map.86.base_ref = f32[1024,512]{1,0:T(8,128)S(1)} custom-call(s32[15]{0:T(128)S(1)} %dynamic-slice_bitcast_fusion.info, bf16[768,1024]{1,0:T(8,128)(2,1)S(1)} %copy-done.2, bf16[784,1024]{1,0:T(8,128)(2,1)S(1)} %collective-permute-done.part_ref.got_ref, f32[8,18,256]{2,1,0:T(8,128)S(1)} %fusion.3.lam_ref.lam0_ref, ...), custom_call_target="tpu_custom_call" | custom-call | flops 4024999936 | bytes 2097152 | tf_op jit(solution)/shard_map/pallas_call | solution.py:21
  52.5 0.0 collective-permute-done.5
  52.6 0.0 copy-start
  52.6 4.5 %collective-permute-done.13.refs_7_ = bf16[640,256]{1,0:T(8,128)(2,1)S(1)} collective-permute-done((bf16[640,256]{1,0:T(8,128)(2,1)S(1)}, bf16[640,256]{1,0:T(8,128)(2,1)S(1)}, u32[]{:S(2)}, u32[]{:S(2)}) %collective-permute-start.13) | collective-permute-done | bytes 327712 | tf_op jit(solution)/shard_map/ppermute | solution.py:308
  57.1 2.8 %collective-permute-done.14.refs_8_ = bf16[640,256]{1,0:T(8,128)(2,1)S(1)} collective-permute-done((bf16[640,256]{1,0:T(8,128)(2,1)S(1)}, bf16[640,256]{1,0:T(8,128)(2,1)S(1)}, u32[]{:S(2)}, u32[]{:S(2)}) %collective-permute-start.14) | collective-permute-done | bytes 327712 | tf_op jit(solution)/shard_map/ppermute | solution.py:309
  59.9 0.0 collective-permute-done.12.refs_6_
  59.9 0.1 collective-permute-start.16
  60.0 2.1 %collective-permute-start.17 = (bf16[384,256]{1,0:T(8,128)(2,1)S(1)}, bf16[384,256]{1,0:T(8,128)(2,1)S(1)}, u32[]{:S(2)}, u32[]{:S(2)}) collective-permute-start(bf16[384,256]{1,0:T(8,128)(2,1)S(1)} %slice.86), channel_id=1, source_target_pairs={{4,0},{5,1},{8,4},{9,5},{12,8},{13,9},{14,12},{15,13},{10,14},{11,... | collective-permute-start | bytes 589832 | tf_op jit(solution)/shard_map/ppermute | solution.py:309
  62.1 0.1 maximum_select_fusion.3
  62.2 1.6 %collective-permute-start.15 = (bf16[768,256]{1,0:T(8,128)(2,1)S(1)}, bf16[768,256]{1,0:T(8,128)(2,1)S(1)}, u32[]{:S(2)}, u32[]{:S(2)}) collective-permute-start(bf16[768,256]{1,0:T(8,128)(2,1)S(1)} %maximum_select_fusion.3), channel_id=1, source_target_pairs={{0,16},{16,0},{1,17},{17,1},{2,18},{18,2},{3,19},{19,3},{4,20},{20... | collective-permute-start | bytes 1179656 | tf_op jit(solution)/shard_map/ppermute | solution.py:322
  63.8 1.1 %collective-permute-done.16.refs_10_ = bf16[256,256]{1,0:T(8,128)(2,1)S(1)} collective-permute-done((bf16[256,256]{1,0:T(8,128)(2,1)S(1)}, bf16[256,256]{1,0:T(8,128)(2,1)S(1)}, u32[]{:S(2)}, u32[]{:S(2)}) %collective-permute-start.16) | collective-permute-done | bytes 131104 | tf_op jit(solution)/shard_map/ppermute | solution.py:308
  64.9 0.8 %collective-permute-done.17.refs_11_ = bf16[384,256]{1,0:T(8,128)(2,1)S(1)} collective-permute-done((bf16[384,256]{1,0:T(8,128)(2,1)S(1)}, bf16[384,256]{1,0:T(8,128)(2,1)S(1)}, u32[]{:S(2)}, u32[]{:S(2)}) %collective-permute-start.17) | collective-permute-done | bytes 196640 | tf_op jit(solution)/shard_map/ppermute | solution.py:309
  65.7 0.1 fusion
  65.8 1.6 %collective-permute-start.18 = (bf16[384,256]{1,0:T(8,128)(2,1)S(1)}, bf16[384,256]{1,0:T(8,128)(2,1)S(1)}, u32[]{:S(2)}, u32[]{:S(2)}) collective-permute-start(bf16[384,256]{1,0:T(8,128)(2,1)S(1)} %fusion), channel_id=1, source_target_pairs={{0,16},{16,0},{1,17},{17,1},{2,18},{18,2},{3,19},{19,3},{4,20},{20... | collective-permute-start | bytes 589832 | tf_op jit(solution)/shard_map/ppermute | solution.py:322
  67.4 1.5 %shard_map.87.normed_ref = bf16[512,1024]{1,0:T(8,128)(2,1)S(1)} custom-call(s32[15]{0:T(128)S(1)} %dynamic-slice_bitcast_fusion.info, bf16[768,1024]{1,0:T(8,128)(2,1)S(1)} %copy-done.2, bf16[784,1024]{1,0:T(8,128)(2,1)S(1)} %collective-permute-done.part_ref.got_ref, f32[8,18,256]{2,1,0:T(8,128)S(1)} %fusion.3.lam_ref.lam0_ref, ...), custom_call_target="tpu_custom_call" | custom-call | flops 2875000064 | bytes 2097152 | tf_op jit(solution)/shard_map/pallas_call | solution.py:21
  68.8 1.2 %collective-permute-done.15.refs_9_ = bf16[768,256]{1,0:T(8,128)(2,1)S(1)} collective-permute-done((bf16[768,256]{1,0:T(8,128)(2,1)S(1)}, bf16[768,256]{1,0:T(8,128)(2,1)S(1)}, u32[]{:S(2)}, u32[]{:S(2)}) %collective-permute-start.15) | collective-permute-done | bytes 393248 | tf_op jit(solution)/shard_map/ppermute | solution.py:322
  70.1 2.1 %collective-permute-done.18.refs_12_ = bf16[384,256]{1,0:T(8,128)(2,1)S(1)} collective-permute-done((bf16[384,256]{1,0:T(8,128)(2,1)S(1)}, bf16[384,256]{1,0:T(8,128)(2,1)S(1)}, u32[]{:S(2)}, u32[]{:S(2)}) %collective-permute-start.18) | collective-permute-done | bytes 196640 | tf_op jit(solution)/shard_map/ppermute | solution.py:322
  72.2 2.1 %shard_map.89 = bf16[256,2048]{1,0:T(8,128)(2,1)S(1)} custom-call(s32[15]{0:T(128)S(1)} %dynamic-slice_bitcast_fusion.info, bf16[512,1024]{1,0:T(8,128)(2,1)S(1)} %shard_map.87.normed_ref, bf16[1024,256]{1,0:T(8,128)(2,1)S(1)} %maximum_select_fusion.refs_0_, bf16[640,256]{1,0:T(8,128)(2,1)S(1)} %collective-permute-done.7.refs_1_, ...), custom_call_target="tpu_custom_call" | custom-call | flops 3449999872 | bytes 2097152 | tf_op jit(solution)/shard_map/pallas_call | solution.py:21
  74.3 0.1 collective-permute-start.19
  74.4 2.1 %shard_map.88 = f32[256,2048]{1,0:T(8,128)S(1)} custom-call(s32[15]{0:T(128)S(1)} %dynamic-slice_bitcast_fusion.info, bf16[512,1024]{1,0:T(8,128)(2,1)S(1)} %shard_map.87.normed_ref, bf16[1024,256]{1,0:T(8,128)(2,1)S(1)} %maximum_select_fusion.refs_0_, bf16[640,256]{1,0:T(8,128)(2,1)S(1)} %collective-permute-done.7.refs_1_, ...), custom_call_target="tpu_custom_call" | custom-call | flops 3449999872 | bytes 2097152 | tf_op jit(solution)/shard_map/pallas_call | solution.py:21
  76.5 0.5 collective-permute-done.19
  77.0 1.3 %add_convert_fusion = bf16[256,2048]{1,0:T(8,128)(2,1)} fusion(f32[256,2048]{1,0:T(8,128)S(1)} %shard_map.88, bf16[256,2048]{1,0:T(8,128)(2,1)S(1)} %collective-permute-done.19), kind=kLoop, calls=%fused_computation | loop fusion | flops 1572864 | bytes 4194304 | tf_op jit(solution)/shard_map/convert_element_type | solution.py:368
  (21 shorter events, 0.4 us)
Async XLA Ops:
  0.0 5.9 %copy-start.4 = (f32[64,18,16]{0,2,1:T(8,128)S(1)}, f32[64,18,16]{0,2,1:T(8,128)}, u32[]{:S(2)}) copy-start(f32[64,18,16]{0,2,1:T(8,128)} %param.12) | copy-start | bytes 221188
  0.0 5.9 %copy-start.5 = (s32[256]{0:T(256)S(1)}, s32[256]{0:T(256)}, u32[]{:S(2)}) copy-start(s32[256]{0:T(256)} %param.11) | copy-start | bytes 3076
  4.6 5.3 %collective-permute-start = (bf16[784,1024]{1,0:T(8,128)(2,1)}, bf16[784,1024]{1,0:T(8,128)(2,1)S(1)}, u32[]{:S(2)}, u32[]{:S(2)}) collective-permute-start(bf16[784,1024]{1,0:T(8,128)(2,1)} %get-tuple-element.21), channel_id=1, source_target_pairs={{0,1},{1,0},{2,3},{3,2},{4,5},{5,4},{6,7},{7,6},{8,9},{9,8},{10,11... | collective-permute-start | bytes 4816904 | tf_op jit(solution)/shard_map/ppermute | solution.py:219
  5.2 4.5 %collective-permute-start.6 = (bf16[1024,128]{1,0:T(8,128)(2,1)}, bf16[1024,128]{1,0:T(8,128)(2,1)S(1)}, u32[]{:S(2)}, u32[]{:S(2)}) collective-permute-start(bf16[1024,128]{1,0:T(8,128)(2,1)} %get-tuple-element.26), channel_id=1, source_target_pairs={{0,1},{1,0},{2,3},{3,2},{4,5},{5,4},{6,7},{7,6},{8,9},{9,8},{10,11... | collective-permute-start | bytes 786440 | tf_op jit(solution)/shard_map/ppermute | solution.py:219
  6.2 1.4 %copy-start.1 = (bf16[768,1024]{1,0:T(8,128)(2,1)S(1)}, bf16[768,1024]{1,0:T(8,128)(2,1)}, u32[]{:S(2)}) copy-start(bf16[768,1024]{1,0:T(8,128)(2,1)} %get-tuple-element.20.part_ref.mine_ref) | copy-start | bytes 4718596
  7.6 2.1 %copy-start.3 = (bf16[1024,128]{1,0:T(8,128)(2,1)S(1)}, bf16[1024,128]{1,0:T(8,128)(2,1)}, u32[]{:S(2)}) copy-start(bf16[1024,128]{1,0:T(8,128)(2,1)} %get-tuple-element.25) | copy-start | bytes 786436
  9.7 1.4 %copy-start.2 = (bf16[768,1024]{1,0:T(8,128)(2,1)S(1)}, bf16[768,1024]{1,0:T(8,128)(2,1)}, u32[]{:S(2)}) copy-start(bf16[768,1024]{1,0:T(8,128)(2,1)} %get-tuple-element.20.part_ref.mine_ref) | copy-start | bytes 4718596
  12.1 10.1 %collective-permute-start.1 = (bf16[8,128,128]{2,1,0:T(8,128)(2,1)S(1)}, bf16[8,128,128]{2,1,0:T(8,128)(2,1)S(1)}, u32[]{:S(2)}, u32[]{:S(2)}) collective-permute-start(bf16[8,128,128]{2,1,0:T(8,128)(2,1)S(1)} %get-tuple-element.23), channel_id=1, source_target_pairs={{0,2},{1,3},{2,0},{3,1},{4,6},{5,7},{6,4},{7,5},{8,10},{9,11},{10,... | collective-permute-start | bytes 786440 | tf_op jit(solution)/shard_map/ppermute | solution.py:219
  15.1 13.6 %collective-permute-start.7 = (bf16[640,256]{1,0:T(8,128)(2,1)S(1)}, bf16[640,256]{1,0:T(8,128)(2,1)S(1)}, u32[]{:S(2)}, u32[]{:S(2)}) collective-permute-start(bf16[640,256]{1,0:T(8,128)(2,1)S(1)} %slice_select_fusion), channel_id=1, source_target_pairs={{0,4},{1,5},{4,8},{5,9},{8,12},{9,13},{12,14},{13,15},{14,10},{15,... | collective-permute-start | bytes 983048 | tf_op jit(solution)/shard_map/ppermute | solution.py:308
  16.7 12.0 %collective-permute-start.8 = (bf16[640,256]{1,0:T(8,128)(2,1)S(1)}, bf16[640,256]{1,0:T(8,128)(2,1)S(1)}, u32[]{:S(2)}, u32[]{:S(2)}) collective-permute-start(bf16[640,256]{1,0:T(8,128)(2,1)S(1)} %slice_select_fusion), channel_id=1, source_target_pairs={{4,0},{5,1},{8,4},{9,5},{12,8},{13,9},{14,12},{15,13},{10,14},{11,... | collective-permute-start | bytes 983048 | tf_op jit(solution)/shard_map/ppermute | solution.py:309
  22.3 8.5 %collective-permute-start.2 = (bf16[4,128,128]{2,1,0:T(8,128)(2,1)S(1)}, bf16[4,128,128]{2,1,0:T(8,128)(2,1)S(1)}, u32[]{:S(2)}, u32[]{:S(2)}) collective-permute-start(bf16[4,128,128]{2,1,0:T(8,128)(2,1)S(1)} %fusion.5), channel_id=1, source_target_pairs={{0,4},{1,5},{2,6},{3,7},{4,0},{5,1},{6,2},{7,3},{8,12},{9,13},{10,... | collective-permute-start | bytes 393224 | tf_op jit(solution)/shard_map/ppermute | solution.py:219
  28.7 12.8 %collective-permute-start.10 = (bf16[640,256]{1,0:T(8,128)(2,1)S(1)}, bf16[640,256]{1,0:T(8,128)(2,1)S(1)}, u32[]{:S(2)}, u32[]{:S(2)}) collective-permute-start(bf16[640,256]{1,0:T(8,128)(2,1)S(1)} %collective-permute-done.7.refs_1_), channel_id=1, source_target_pairs={{0,4},{1,5},{4,8},{5,9},{8,12},{9,13},{12,14},{13,15},{14,10},{15,... | collective-permute-start | bytes 983048 | tf_op jit(solution)/shard_map/ppermute | solution.py:308
  28.7 12.8 %collective-permute-start.11 = (bf16[640,256]{1,0:T(8,128)(2,1)S(1)}, bf16[640,256]{1,0:T(8,128)(2,1)S(1)}, u32[]{:S(2)}, u32[]{:S(2)}) collective-permute-start(bf16[640,256]{1,0:T(8,128)(2,1)S(1)} %collective-permute-done.8.refs_2_), channel_id=1, source_target_pairs={{4,0},{5,1},{8,4},{9,5},{12,8},{13,9},{14,12},{15,13},{10,14},{11,... | collective-permute-start | bytes 983048 | tf_op jit(solution)/shard_map/ppermute | solution.py:309
  30.8 7.7 %collective-permute-start.4 = (bf16[4,128,128]{2,1,0:T(8,128)(2,1)S(1)}, bf16[4,128,128]{2,1,0:T(8,128)(2,1)S(1)}, u32[]{:S(2)}, u32[]{:S(2)}) collective-permute-start(bf16[4,128,128]{2,1,0:T(8,128)(2,1)S(1)} %add_convert_fusion.1), channel_id=1, source_target_pairs={{0,8},{1,9},{2,10},{3,11},{4,12},{5,13},{6,14},{7,15},{16,24},{17,... | collective-permute-start | bytes 393224 | tf_op jit(solution)/shard_map/ppermute | solution.py:219
  35.1 6.3 %collective-permute-start.3 = (bf16[4,128,128]{2,1,0:T(8,128)(2,1)S(1)}, bf16[4,128,128]{2,1,0:T(8,128)(2,1)S(1)}, u32[]{:S(2)}, u32[]{:S(2)}) collective-permute-start(bf16[4,128,128]{2,1,0:T(8,128)(2,1)S(1)} %collective-permute-done.2), channel_id=1, source_target_pairs={{0,2},{1,3},{2,0},{3,1},{4,6},{5,7},{6,4},{7,5},{8,10},{9,11},{10,... | collective-permute-start | bytes 393224 | tf_op jit(solution)/shard_map/ppermute | solution.py:219
  36.8 12.1 %collective-permute-start.9 = (bf16[768,256]{1,0:T(8,128)(2,1)S(1)}, bf16[768,256]{1,0:T(8,128)(2,1)S(1)}, u32[]{:S(2)}, u32[]{:S(2)}) collective-permute-start(bf16[768,256]{1,0:T(8,128)(2,1)S(1)} %maximum_select_fusion.1), channel_id=1, source_target_pairs={{0,16},{16,0},{1,17},{17,1},{2,18},{18,2},{3,19},{19,3},{4,20},{20... | collective-permute-start | bytes 1179656 | tf_op jit(solution)/shard_map/ppermute | solution.py:322
  38.5 14.0 %collective-permute-start.5 = (bf16[4,128,128]{2,1,0:T(8,128)(2,1)S(1)}, bf16[4,128,128]{2,1,0:T(8,128)(2,1)S(1)}, u32[]{:S(2)}, u32[]{:S(2)}) collective-permute-start(bf16[4,128,128]{2,1,0:T(8,128)(2,1)S(1)} %collective-permute-done.4), channel_id=1, source_target_pairs={{0,2},{1,3},{2,0},{3,1},{4,6},{5,7},{6,4},{7,5},{8,10},{9,11},{10,... | collective-permute-start | bytes 393224 | tf_op jit(solution)/shard_map/ppermute | solution.py:219
  41.7 18.2 %collective-permute-start.12 = (bf16[768,256]{1,0:T(8,128)(2,1)S(1)}, bf16[768,256]{1,0:T(8,128)(2,1)S(1)}, u32[]{:S(2)}, u32[]{:S(2)}) collective-permute-start(bf16[768,256]{1,0:T(8,128)(2,1)S(1)} %maximum_select_fusion.2), channel_id=1, source_target_pairs={{0,16},{16,0},{1,17},{17,1},{2,18},{18,2},{3,19},{19,3},{4,20},{20... | collective-permute-start | bytes 1179656 | tf_op jit(solution)/shard_map/ppermute | solution.py:322
  48.9 8.2 %collective-permute-start.13 = (bf16[640,256]{1,0:T(8,128)(2,1)S(1)}, bf16[640,256]{1,0:T(8,128)(2,1)S(1)}, u32[]{:S(2)}, u32[]{:S(2)}) collective-permute-start(bf16[640,256]{1,0:T(8,128)(2,1)S(1)} %collective-permute-done.10.refs_4_), channel_id=1, source_target_pairs={{0,4},{1,5},{4,8},{5,9},{8,12},{9,13},{12,14},{13,15},{14,10},{15,... | collective-permute-start | bytes 983048 | tf_op jit(solution)/shard_map/ppermute | solution.py:308
  51.0 8.9 %collective-permute-start.14 = (bf16[640,256]{1,0:T(8,128)(2,1)S(1)}, bf16[640,256]{1,0:T(8,128)(2,1)S(1)}, u32[]{:S(2)}, u32[]{:S(2)}) collective-permute-start(bf16[640,256]{1,0:T(8,128)(2,1)S(1)} %collective-permute-done.11.refs_5_), channel_id=1, source_target_pairs={{4,0},{5,1},{8,4},{9,5},{12,8},{13,9},{14,12},{15,13},{10,14},{11,... | collective-permute-start | bytes 983048 | tf_op jit(solution)/shard_map/ppermute | solution.py:309
  52.6 14.8 %copy-start = (f32[2048]{0:T(1024)S(1)}, f32[2048]{0:T(1024)}, u32[]{:S(2)}) copy-start(f32[2048]{0:T(1024)} %param.13) | copy-start | bytes 24580
  59.9 5.0 %collective-permute-start.16 = (bf16[256,256]{1,0:T(8,128)(2,1)S(1)}, bf16[256,256]{1,0:T(8,128)(2,1)S(1)}, u32[]{:S(2)}, u32[]{:S(2)}) collective-permute-start(bf16[256,256]{1,0:T(8,128)(2,1)S(1)} %slice.85), channel_id=1, source_target_pairs={{0,4},{1,5},{4,8},{5,9},{8,12},{9,13},{12,14},{13,15},{14,10},{15,... | collective-permute-start | bytes 393224 | tf_op jit(solution)/shard_map/ppermute | solution.py:308
  60.0 5.7 %collective-permute-start.17 = (bf16[384,256]{1,0:T(8,128)(2,1)S(1)}, bf16[384,256]{1,0:T(8,128)(2,1)S(1)}, u32[]{:S(2)}, u32[]{:S(2)}) collective-permute-start(bf16[384,256]{1,0:T(8,128)(2,1)S(1)} %slice.86), channel_id=1, source_target_pairs={{4,0},{5,1},{8,4},{9,5},{12,8},{13,9},{14,12},{15,13},{10,14},{11,... | collective-permute-start | bytes 589832 | tf_op jit(solution)/shard_map/ppermute | solution.py:309
  62.2 7.8 %collective-permute-start.15 = (bf16[768,256]{1,0:T(8,128)(2,1)S(1)}, bf16[768,256]{1,0:T(8,128)(2,1)S(1)}, u32[]{:S(2)}, u32[]{:S(2)}) collective-permute-start(bf16[768,256]{1,0:T(8,128)(2,1)S(1)} %maximum_select_fusion.3), channel_id=1, source_target_pairs={{0,16},{16,0},{1,17},{17,1},{2,18},{18,2},{3,19},{19,3},{4,20},{20... | collective-permute-start | bytes 1179656 | tf_op jit(solution)/shard_map/ppermute | solution.py:322
  65.8 6.4 %collective-permute-start.18 = (bf16[384,256]{1,0:T(8,128)(2,1)S(1)}, bf16[384,256]{1,0:T(8,128)(2,1)S(1)}, u32[]{:S(2)}, u32[]{:S(2)}) collective-permute-start(bf16[384,256]{1,0:T(8,128)(2,1)S(1)} %fusion), channel_id=1, source_target_pairs={{0,16},{16,0},{1,17},{17,1},{2,18},{18,2},{3,19},{19,3},{4,20},{20... | collective-permute-start | bytes 589832 | tf_op jit(solution)/shard_map/ppermute | solution.py:322
  74.3 2.7 %collective-permute-start.19 = (bf16[256,2048]{1,0:T(8,128)(2,1)S(1)}, bf16[256,2048]{1,0:T(8,128)(2,1)S(1)}, u32[]{:S(2)}, u32[]{:S(2)}) collective-permute-start(bf16[256,2048]{1,0:T(8,128)(2,1)S(1)} %shard_map.89), channel_id=1, source_target_pairs={{0,1},{1,0},{2,3},{3,2},{4,5},{5,4},{6,7},{7,6},{8,9},{9,8},{10,11... | collective-permute-start | bytes 3145736 | tf_op jit(solution)/shard_map/ppermute | solution.py:219

commit v3 on v2

--- a/solution.py
+++ b/solution.py
@@ -11,6 +11,7 @@
 from jax.sharding import PartitionSpec as P
 
 TILE = 128
+LATE = 1
 VM = pl.BlockSpec(memory_space=pltpu.VMEM)
 SM = pl.BlockSpec(memory_space=pltpu.SMEM)
 PARAMS = pltpu.CompilerParams(vmem_limit_bytes=8 * 1024 * 1024)
@@ -40,24 +41,21 @@
     return lax.dot_general(a, b, (((ca,), (cb,)), ((), ())), preferred_element_type=jnp.float32)
 
 
-def split_kernel(k_ref, v_ref, q_ref, w_ref, index_ref, sent_ref, mine_ref, w_sent_ref, w_mine_ref, sems):
-    rows, half = mine_ref.shape[0] // 3, mine_ref.shape[1]
-    deep = w_mine_ref.shape[0]
-    core = lax.axis_index("seq") % 2
+def split_kernel(to_other, k_ref, v_ref, q_ref, index_ref, after_ref, out_ref, sems):
+    half = out_ref.shape[1]
+    rows = k_ref.shape[0]
+    side = (lax.axis_index("seq") + to_other) % 2
     copies = []
-    for to_other, big, small in ((1, sent_ref, w_sent_ref), (0, mine_ref, w_mine_ref)):
-        side = (core + to_other) % 2
-        for at, ref in enumerate((k_ref, v_ref, q_ref)):
-            copies.append((ref.at[:, lanes(side * half, half)], big.at[pl.ds(at * rows, rows), :]))
-        copies.append((w_ref.at[pl.ds(pl.multiple_of(side * deep, 16), deep), :], small))
+    for at, ref in enumerate((k_ref, v_ref, q_ref)):
+        copies.append((ref.at[:, lanes(side * half, half)], out_ref.at[pl.ds(at * rows, rows), :]))
     copies = [pltpu.make_async_copy(a, b, sems.at[n]) for n, (a, b) in enumerate(copies)]
     for copy in copies:
         copy.start()
-    if sent_ref.shape[0] > 3 * rows:
-        tail = sent_ref.shape[0] - 3 * rows
+    tail = out_ref.shape[0] - 3 * rows
+    if tail:
         row = jnp.broadcast_to(index_ref[...].astype(jnp.float32), (tail, rows)).astype(jnp.bfloat16)
-        sent_ref[pl.ds(3 * rows, tail), :] = jnp.zeros((tail, half), jnp.bfloat16)
-        sent_ref[pl.ds(3 * rows, tail), pl.ds(0, rows)] = row
+        out_ref[pl.ds(3 * rows, tail), :] = jnp.zeros((tail, half), jnp.bfloat16)
+        out_ref[pl.ds(3 * rows, tail), pl.ds(0, rows)] = row
     for copy in copies:
         copy.wait()
 
@@ -140,13 +138,13 @@
             out_ref[far, pl.ds(side * rows, rows)] = total
 
 
-def last_kernel(level, log_stretch, info, mine_ref, got_ref, lam0_ref, lam1_ref, base_ref, bucket_ref, gain_ref, out_ref):
+def last_kernel(levels, log_stretch, info, mine_ref, got_ref, lam0_ref, lam1_ref, base_ref, gain_ref, *refs):
+    buckets, out_ref = refs[:-1], refs[-1]
     heads = lam0_ref.shape[0]
     rows = mine_ref.shape[0] // 3
     dim = base_ref.shape[0] // heads
     core = info[0]
     scale = 1.0 / math.sqrt(dim)
-    column = log_stretch + 1 + level
     for h in range(heads):
         far = pl.ds(h * dim, dim)
         own = lanes(core * heads * dim + h * dim, dim)
@@ -154,27 +152,47 @@
             at_rows = pl.ds(side * rows, rows)
             lam = (lam0_ref, lam1_ref)[side][h]
             q = (mine_ref, got_ref)[side][pl.ds(2 * rows, rows), far]
-            weight = jnp.where(info[1 + level] == 1, lam[column : column + 1] * scale, 0.0)
-            total = base_ref[far, at_rows] + weight * dot(bucket_ref[h], q, 1, 1)
+            total = base_ref[far, at_rows]
+            for at, level in enumerate(levels):
+                column = log_stretch + 1 + level
+                weight = jnp.where(info[1 + level] == 1, lam[column : column + 1] * scale, 0.0)
+                total = total + weight * dot(buckets[at][h], q, 1, 1)
             mean = jnp.mean(total * total, axis=0, keepdims=True)
             total = total * lax.rsqrt(mean + 1e-06)
             out_ref[at_rows, far] = (jnp.transpose(total) * gain_ref[:, own]).astype(out_ref.dtype)
 
 
-def project_kernel(side, plan, info, normed_ref, *refs):
-    out_ref = refs[-1]
-    rows = out_ref.shape[0]
-    for chip_slot, parts in plan:
+def project_kernel(plan, info, normed_ref, *refs):
+    pieces, own_ref, other_ref = refs[:-2], refs[-2], refs[-1]
+    rows = own_ref.shape[0]
+    for slot, (_, parts) in enumerate(plan):
         total = None
         for at, row0, k_slot, k_add, size in parts:
-            piece = refs[at]
             start = k_add if k_slot is None else info[k_slot] + k_add
-            a = normed_ref[pl.ds(side * rows, rows), lanes(start, size)]
-            term = dot(a, piece[pl.ds(row0, size), :])
+            term = dot(normed_ref[:, lanes(start, size)], pieces[at][pl.ds(row0, size), :])
             total = term if total is None else total + term
-        width = refs[parts[0][0]].shape[1]
-        column = 0 if chip_slot is None else info[chip_slot] * width
-        out_ref[:, lanes(column, width)] = total.astype(out_ref.dtype)
+        width = pieces[parts[0][0]].shape[1]
+        own_ref[:, pl.ds(slot * width, width)] = total[:rows]
+        other_ref[:, pl.ds(slot * width, width)] = total[rows:].astype(other_ref.dtype)
+
+
+def combine_kernel(plans, info, *refs):
+    out_ref, held, sems = refs[-3:]
+    copies = []
+    for n, plan in enumerate(plans):
+        own_ref, came_ref = refs[2 * n], refs[2 * n + 1]
+        width = own_ref.shape[1] // len(plan)
+        for slot, (chip_slot, _) in enumerate(plan):
+            at = pl.ds(slot * width, width)
+            column = 0 if chip_slot is None else info[chip_slot] * width
+            total = own_ref[:, at] + came_ref[:, at].astype(jnp.float32)
+            to = pl.ds(len(copies) * width, width)
+            held[:, to] = total.astype(out_ref.dtype)
+            copy = pltpu.make_async_copy(held.at[:, to], out_ref.at[:, lanes(column, width)], sems.at[len(copies)])
+            copy.start()
+            copies.append(copy)
+    for copy in copies:
+        copy.wait()
 
 
 def ring_order(chips):
@@ -220,33 +238,34 @@
 
     packs = table_rows <= 256 and stretch <= half
     bf16 = functools.partial(jax.ShapeDtypeStruct, dtype=jnp.bfloat16)
-    sent, mine, w_sent, w_own = pl.pallas_call(
-        split_kernel,
-        out_shape=(
-            bf16(((3 * stretch + 16) if packs else 3 * stretch, half)),
-            bf16((3 * stretch, half)),
-            bf16((half, columns)),
-            bf16((half, columns)),
-        ),
-        in_specs=[pl.BlockSpec(memory_space=pltpu.HBM)] * 4 + [VM],
-        out_specs=(VM,) * 4,
-        scratch_shapes=[pltpu.SemaphoreType.DMA((8,))],
-        compiler_params=pltpu.CompilerParams(vmem_limit_bytes=56 * 1024 * 1024),
-        cost_estimate=pl.CostEstimate(flops=us(1.5), bytes_accessed=1 << 21, transcendentals=0),
-    )(keys, values, queries, out_weight, level_index.reshape(1, stretch))
+
+    def split(to_other, rows, after):
+        hbm = pl.BlockSpec(memory_space=pltpu.HBM)
+        return pl.pallas_call(
+            functools.partial(split_kernel, to_other),
+            out_shape=bf16((rows, half)),
+            in_specs=[hbm] * 3 + [VM, pl.BlockSpec(memory_space=pl.ANY)],
+            out_specs=VM,
+            scratch_shapes=[pltpu.SemaphoreType.DMA((3,))],
+            compiler_params=pltpu.CompilerParams(vmem_limit_bytes=56 * 1024 * 1024),
+            cost_estimate=pl.CostEstimate(flops=us(2.5), bytes_accessed=1 << 21, transcendentals=0),
+        )(keys, values, queries, level_index.reshape(1, stretch), after)
+
+    w_got = swap(out_weight, 0)
+    sent = split(1, (3 * stretch + 16) if packs else 3 * stretch, level_index)
     got = swap(sent, 0)
     if packs:
         index_got = got[3 * stretch, :stretch].astype(jnp.int32)
     else:
         index_got = swap(level_index, 0)
 
-    w_got = swap(w_sent, 0)
     whole = jnp.where(
         core == 0,
-        jnp.concatenate([w_own, w_got], axis=1),
-        jnp.concatenate([w_got, w_own], axis=1),
-    )
-
+        jnp.concatenate([out_weight[:half], w_got[:half]], axis=1),
+        jnp.concatenate([w_got[half:], out_weight[half:]], axis=1),
+    )
+
+    mine = split(0, 3 * stretch, whole)
     table = jnp.transpose(level_table, (2, 1, 0))
     table = jnp.where(core == 0, table[:pair_heads], table[pair_heads:]).reshape(-1, table_rows)
 
@@ -268,10 +287,18 @@
         1 << 20,
         info, mine, got,
     )
+    send_first = send
     buckets = [even]
+    quarters = []
     reached = [send]
     upper = jnp.right_shift(rank, 1) % 2
-    for bit in range(1, log_blocks):
+    crossed = []
+
+    def tie(x, *others):
+        return lax.optimization_barrier((x, *others))[0]
+
+    def level(bit):
+        nonlocal total, send
         came = swap(send, bit, upward=bit == log_blocks - 1)
         if bit + 1 < log_blocks:
             total = total + came
@@ -280,15 +307,17 @@
             send = total.astype(jnp.bfloat16)
             reached.append(send)
         if bit > 1:
-            rest = swap(came, 1)
-            came = jnp.where(
-                upper == 0, jnp.concatenate([came, rest], axis=0), jnp.concatenate([rest, came], axis=0)
-            )
-        buckets.append(came)
+            quarters.append(came)
+        else:
+            buckets.append(came)
+
+    for bit in range(1, min(3, log_blocks)):
+        level(bit)
 
     pieces = []
     plan = []
-    crossed = []
+    late = []
+    landed = ()
     if ringed:
         clockwise = []
         for at, chip in enumerate(order):
@@ -299,16 +328,26 @@
         plan.append((chip_at, [(0, 0, None, 0, half)]))
         right = left = jnp.where(group % 2 == 0, whole[:kept], whole[shared:]) if shared else whole
         rounds = chips // 2
+
+        def ring_after(r):
+            if r == 3:
+                return reached[2:3] + crossed[:1]
+            return []
+
         for r in range(1, rounds + 1):
             last = r == rounds
-            ahead = reached[r - 1 : r] + crossed[r - 3 : r - 2] * (r >= 3)
-            right, left, *_ = lax.optimization_barrier((right, left, *ahead))
+            right, left, *_ = lax.optimization_barrier((right, left, *ring_after(r)))
             if last:
                 right, left = right[:cut], left[cut:]
             right = lax.ppermute(right, "seq", clockwise)
             left = lax.ppermute(left, "seq", counter)
+            if r == 1:
+                right, left, _ = lax.optimization_barrier((right, left, send_first))
+            if r == 3:
+                send = tie(send, right, left)
             at = len(pieces)
             pieces += [right, left]
+            landed = (right, left)
             if last:
                 parts = [[(at, 0, k_mine, 0, cut), (at + 1, 0, k_mine, cut, kept - cut)]]
                 distances = [r]
@@ -323,49 +362,77 @@
                 pieces.append(crossed[-1])
                 for n, part in enumerate(parts):
                     part.append((at + 2, n * shared, k_lacks, 0, shared))
-            plan += [(chip_at + d, part) for d, part in zip(distances, parts)]
+            (late if r >= rounds - LATE else plan).extend(
+                (chip_at + d, part) for d, part in zip(distances, parts)
+            )
     else:
         full = lax.all_gather(out_weight, "seq", axis=1, tiled=True)
         pieces.append(lax.dynamic_slice(full, (core * half, 0), (half, width)))
         plan.append((None, [(0, 0, None, 0, half)]))
 
+    while len(quarters) + 2 < log_blocks:
+        level(len(quarters) + 2)
+    joined = jnp.stack(quarters)
+    rest = swap(joined, 1)
+    both = jnp.where(
+        upper == 0, jnp.concatenate([joined, rest], axis=1), jnp.concatenate([rest, joined], axis=1)
+    )
+    buckets += [both[n] for n in range(len(quarters))]
+
     side_shape = jax.ShapeDtypeStruct((half, stretch), jnp.float32)
     acc_own = call(
-        local_kernel, side_shape, [VM] * 2, us(2.9), 1 << 21, lam_own, mine,
+        local_kernel, side_shape, [VM] * 2, us(2.1), 1 << 20, tie(lam_own, reached[0]), mine,
     )
     acc_got = call(
-        local_kernel, side_shape, [VM] * 2, us(2.9), 1 << 21, lam_got, got,
-    )
-    early = list(range(log_blocks - 1))
+        local_kernel, side_shape, [VM] * 2, us(2.1), 1 << 20, lam_got, got,
+    )
     acc = call(
-        functools.partial(early_kernel, early, log_stretch),
+        functools.partial(early_kernel, [0, 1], log_stretch),
         jax.ShapeDtypeStruct((half, 2 * stretch), jnp.float32),
-        [SM] + [VM] * (6 + len(early)),
-        us(3.5),
-        1 << 21,
-        info, mine, got, lam_own, lam_got, acc_own, acc_got, *buckets[:-1],
+        [SM] + [VM] * 8,
+        us(1.6),
+        1 << 20,
+        info, mine, got, lam_own, lam_got, acc_own, acc_got, *buckets[:2],
     )
     normed = call(
-        functools.partial(last_kernel, log_blocks - 1, log_stretch),
+        functools.partial(last_kernel, list(range(2, log_blocks)), log_stretch),
         jax.ShapeDtypeStruct((2 * stretch, half), jnp.bfloat16),
-        [SM] + [VM] * 7,
-        us(2.5),
-        1 << 21,
-        info, mine, got, lam_own, lam_got, acc, buckets[-1], norm_gain.reshape(1, width),
-    )
-
-    def project(side, dtype):
-        return call(
-            functools.partial(project_kernel, side, plan),
-            jax.ShapeDtypeStruct((stretch, width), dtype),
-            [SM] + [VM] * (1 + len(pieces)),
-            us(3.0),
-            1 << 21,
-            info, normed, *pieces,
+        [SM] + [VM] * (6 + len(quarters)),
+        us(2.0),
+        1 << 20,
+        info, mine, got, lam_own, lam_got, acc, norm_gain.reshape(1, width), *buckets[2:],
+    )
+
+    plans = [p for p in (plan, late) if p]
+    shares = []
+    for p in plans:
+        used = sorted({part[0] for _, parts in p for part in parts})
+        local = [(c, [(used.index(part[0]), *part[1:]) for part in parts]) for c, parts in p]
+        wide = len(p) * pieces[used[0]].shape[1]
+        own, other = call(
+            functools.partial(project_kernel, local),
+            (
+                jax.ShapeDtypeStruct((stretch, wide), jnp.float32),
+                jax.ShapeDtypeStruct((stretch, wide), jnp.bfloat16),
+            ),
+            [SM] + [VM] * (1 + len(used)),
+            us(4.0 * wide / width),
+            1 << 20,
+            info, normed, *[pieces[n] for n in used],
         )
-
-    came = swap(project(1, jnp.bfloat16), 0)
-    return (project(0, jnp.float32) + came).astype(jnp.bfloat16)
+        shares += [own, swap(other, 0)]
+    return pl.pallas_call(
+        functools.partial(combine_kernel, plans),
+        out_shape=jax.ShapeDtypeStruct((stretch, width), jnp.bfloat16),
+        in_specs=[SM] + [VM] * len(shares),
+        out_specs=pl.BlockSpec(memory_space=pltpu.HBM),
+        scratch_shapes=[
+            pltpu.VMEM((stretch, width), jnp.bfloat16),
+            pltpu.SemaphoreType.DMA((sum(len(p) for p in plans),)),
+        ],
+        compiler_params=PARAMS,
+        cost_estimate=pl.CostEstimate(flops=us(1.0), bytes_accessed=1 << 20, transcendentals=0),
+    )(info, *shares)
 
 
 def solution(mesh):

time: 78.5 us -> 64.7 us (0.82)
  waiting for transfers between devices: 27 us -> 16 us
  starting transfers between devices: 28.2 us -> 23.6 us
  Pallas kernels: 17 us -> 20.4 us
  other arithmetic: 2.05 us -> 0.75 us
    ppermute x4, waiting for transfers between devices: 9.04 us -> 0.49 us  [body(): crossed.append(lax.ppermute(wanted, 'grp', [(0, 1), (1, 0)]))]
    ppermute x4, waiting for transfers between devices: 10.7 us -> 4.94 us  [body(): right = lax.ppermute(right, 'seq', clockwise)]
    ppermute x8, starting transfers between devices: 13.7 us -> 8.63 us  [swap(): return lax.ppermute(block, 'seq', route)]
    pallas_call x1 -> x3, Pallas kernels: 4.62 us -> 8.12 us  [the longest x2 6.53 us: split(): pl.pallas_call(functools.partial(split_kernel, to_other), out_shape=bf16(...]
    ppermute x4, waiting for transfers between devices: 3.59 us -> 5.99 us  [body(): left = lax.ppermute(left, 'seq', counter)]
    ppermute x4, starting transfers between devices: 3.67 us -> 5.78 us  [body(): right = lax.ppermute(right, 'seq', clockwise)]
    convert_element_type x3 -> x2, other arithmetic: 1.33 us -> 0.07 us  [level(): send = total.astype(jnp.bfloat16)]
    ppermute x4, starting transfers between devices: 4.53 us -> 3.58 us  [body(): left = lax.ppermute(left, 'seq', counter)]
  transfers between devices with their start and end apart: 20 -> 20, of which waited for: 11 -> 12; matrix products, arithmetic and copies ran while one was open for 2% -> 3% of each run, Pallas kernels for 12% -> 29%
where the time goes in v3:
time: 64.7 us; the launch traced here: 64 us
  starting transfers between devices  23.6 us (36%)
  Pallas kernels  20.4 us (32%)
  waiting for transfers between devices  16 us (25%)
  local copies, waits for them, and re-layouts  2.43 us (4%)
  other arithmetic  0.75 us (1%)
    pallas_call x7, Pallas kernels, call(): pl.pallas_call(kernel, out_shape=out_shape, in_specs=in_specs, out_specs=...  12.2 us
    ppermute x8, starting transfers between devices, swap(): return lax.ppermute(block, 'seq', route)  8.63 us
    pallas_call x2, Pallas kernels, split(): pl.pallas_call(functools.partial(split_kernel, to_other), out_shape=bf16(...  6.53 us
    ppermute x4, waiting for transfers between devices, body(): left = lax.ppermute(left, 'seq', counter)  5.99 us
    ppermute x4, starting transfers between devices, body(): right = lax.ppermute(right, 'seq', clockwise)  5.78 us
    ppermute x4, starting transfers between devices, body(): crossed.append(lax.ppermute(wanted, 'grp', [(0, 1), (1, 0)]))  5.62 us
    ppermute x4, waiting for transfers between devices, body(): right = lax.ppermute(right, 'seq', clockwise)  4.94 us
    ppermute x8, waiting for transfers between devices, swap(): return lax.ppermute(block, 'seq', route)  4.58 us
  transfers between devices with their start and end apart: 20, of which 12 were waited for; matrix products, arithmetic and copies ran while one was open for 3% of the time, Pallas kernels for 29%

profile of v3, /device:TPU:0, one launch (start us, length us, event | category | flops | bytes accessed | tf_op | source)
XLA Modules:
  0.0 64.0 jit_solution(13864837053798423175)
XLA Ops:
  0.0 0.5 collective-permute-start
  0.5 3.3 %shard_map.83 = bf16[784,1024]{1,0:T(8,128)(2,1)} custom-call(bf16[256,2048]{1,0:T(8,128)(2,1)} %k_ref.3, bf16[256,2048]{1,0:T(8,128)(2,1)} %v_ref.3, bf16[256,2048]{1,0:T(8,128)(2,1)} %q_ref.3, s32[1,256]{1,0:T(1,128)} %bitcast.25, s32[256]{0:T(256)} %after_ref.1), custom_call_target="tpu_custom_call" | custom-call | flops 2875000064 | bytes 2097152 | tf_op jit(solution)/shard_map/pallas_call | solution.py:244
  3.8 0.1 collective-permute-start.1
  3.9 0.7 %dynamic-slice_bitcast_fusion.info = s32[15]{0:T(128)S(1)} fusion(s32[2,16,15]{2,1,0:T(8,128)} %constant.36.clone, s32[]{:T(128)S(6)} %select_n.85, s32[]{:T(128)S(6)} %select_n.86), kind=kLoop, calls=%fused_computation.27 | loop fusion | bytes 128 | tf_op jit(solution)/shard_map/reshape | solution.py:233
  4.6 0.2 fusion.3.lam_ref.lam0_ref
  4.9 0.0 collective-permute-done
  5.0 0.2 maximum_select_fusion.after_ref.refs_0_
  5.1 0.0 copy-start
  5.2 3.1 %collective-permute-start.4 = (bf16[640,256]{1,0:T(8,128)(2,1)S(1)}, bf16[640,256]{1,0:T(8,128)(2,1)S(1)}, u32[]{:S(2)}, u32[]{:S(2)}) collective-permute-start(bf16[640,256]{1,0:T(8,128)(2,1)S(1)} %slice_select_fusion), channel_id=1, source_target_pairs={{0,4},{1,5},{4,8},{5,9},{8,12},{9,13},{12,14},{13,15},{14,10},{15,... | collective-permute-start | bytes 983048 | tf_op jit(solution)/shard_map/ppermute | solution.py:342
  8.3 0.0 collective-permute-start.5
  8.3 3.2 %shard_map.82.mine_ref.part_ref = bf16[768,1024]{1,0:T(8,128)(2,1)} custom-call(bf16[256,2048]{1,0:T(8,128)(2,1)} %k_ref.3, bf16[256,2048]{1,0:T(8,128)(2,1)} %v_ref.3, bf16[256,2048]{1,0:T(8,128)(2,1)} %q_ref.3, s32[1,256]{1,0:T(1,128)} %bitcast.26, bf16[1024,256]{1,0:T(8,128)(2,1)} %copy-done), custom_call_target="tpu_custom_call" | custom-call | flops 2875000064 | bytes 2097152 | tf_op jit(solution)/shard_map/pallas_call | solution.py:244
  11.5 0.0 collective-permute-done.1.got_ref.part_ref
  11.5 1.4 %copy-done.2 = bf16[768,1024]{1,0:T(8,128)(2,1)S(1)} copy-done((bf16[768,1024]{1,0:T(8,128)(2,1)S(1)}, bf16[768,1024]{1,0:T(8,128)(2,1)}, u32[]{:S(2)}) %copy-start.2) | copy-done | bytes 1572888
  12.9 1.0 %shard_map.84 = (f32[8,128,128]{2,1,0:T(8,128)S(1)}, bf16[8,128,128]{2,1,0:T(8,128)(2,1)S(1)}, bf16[8,128,128]{2,1,0:T(8,128)(2,1)S(1)}) custom-call(s32[15]{0:T(128)S(1)} %dynamic-slice_bitcast_fusion.info, bf16[768,1024]{1,0:T(8,128)(2,1)S(1)} %copy-done.2, bf16[784,1024]{1,0:T(8,128)(2,1)S(1)} %collective-permute-done.1.got_ref.part_ref), custom_call_target="tpu_custom_call" | custom-call | flops 1150000000 | bytes 1048576 | tf_op jit(solution)/shard_map/pallas_call | solution.py:22
  14.0 2.0 %collective-permute-start.2 = (bf16[8,128,128]{2,1,0:T(8,128)(2,1)S(1)}, bf16[8,128,128]{2,1,0:T(8,128)(2,1)S(1)}, u32[]{:S(2)}, u32[]{:S(2)}) collective-permute-start(bf16[8,128,128]{2,1,0:T(8,128)(2,1)S(1)} %get-tuple-element.24), channel_id=1, source_target_pairs={{0,2},{1,3},{2,0},{3,1},{4,6},{5,7},{6,4},{7,5},{8,10},{9,11},{10,... | collective-permute-start | bytes 786440 | tf_op jit(solution)/shard_map/ppermute | solution.py:237
  16.0 0.1 collective-permute-done.4.refs_1_
  16.1 1.5 %collective-permute-done.5.refs_2_ = bf16[640,256]{1,0:T(8,128)(2,1)S(1)} collective-permute-done((bf16[640,256]{1,0:T(8,128)(2,1)S(1)}, bf16[640,256]{1,0:T(8,128)(2,1)S(1)}, u32[]{:S(2)}, u32[]{:S(2)}) %collective-permute-start.5) | collective-permute-done | bytes 327712 | tf_op jit(solution)/shard_map/ppermute | solution.py:343
  17.6 0.1 fusion.18
  17.7 0.2 fusion.1.lam_ref.lam1_ref
  18.0 2.1 %shard_map.85.base0_ref = f32[1024,256]{1,0:T(8,128)S(1)} custom-call(f32[8,18,256]{2,1,0:T(8,128)S(1)} %fusion.3.lam_ref.lam0_ref, bf16[768,1024]{1,0:T(8,128)(2,1)S(1)} %copy-done.3), custom_call_target="tpu_custom_call" | custom-call | flops 2415000064 | bytes 1048576 | tf_op jit(solution)/shard_map/pallas_call | solution.py:22
  20.0 1.6 %collective-permute-start.6 = (bf16[640,256]{1,0:T(8,128)(2,1)S(1)}, bf16[640,256]{1,0:T(8,128)(2,1)S(1)}, u32[]{:S(2)}, u32[]{:S(2)}) collective-permute-start(bf16[640,256]{1,0:T(8,128)(2,1)S(1)} %collective-permute-done.4.refs_1_), channel_id=1, source_target_pairs={{0,4},{1,5},{4,8},{5,9},{8,12},{9,13},{12,14},{13,15},{14,10},{15,... | collective-permute-start | bytes 983048 | tf_op jit(solution)/shard_map/ppermute | solution.py:342
  21.7 0.5 collective-permute-start.7
  22.1 0.1 maximum_select_fusion.2
  22.2 1.6 %collective-permute-start.8 = (bf16[768,256]{1,0:T(8,128)(2,1)S(1)}, bf16[768,256]{1,0:T(8,128)(2,1)S(1)}, u32[]{:S(2)}, u32[]{:S(2)}) collective-permute-start(bf16[768,256]{1,0:T(8,128)(2,1)S(1)} %maximum_select_fusion.2), channel_id=1, source_target_pairs={{0,16},{16,0},{1,17},{17,1},{2,18},{18,2},{3,19},{19,3},{4,20},{20... | collective-permute-start | bytes 1179656 | tf_op jit(solution)/shard_map/ppermute | solution.py:361
  23.8 2.1 %shard_map.86.base1_ref = f32[1024,256]{1,0:T(8,128)S(1)} custom-call(f32[8,18,256]{2,1,0:T(8,128)S(1)} %fusion.1.lam_ref.lam1_ref, bf16[784,1024]{1,0:T(8,128)(2,1)S(1)} %collective-permute-done.1.got_ref.part_ref), custom_call_target="tpu_custom_call" | custom-call | flops 2415000064 | bytes 1048576 | tf_op jit(solution)/shard_map/pallas_call | solution.py:22
  25.9 0.0 collective-permute-done.2.refs_1_
  26.0 1.6 %collective-permute-start.3 = (bf16[4,128,128]{2,1,0:T(8,128)(2,1)S(1)}, bf16[4,128,128]{2,1,0:T(8,128)(2,1)S(1)}, u32[]{:S(2)}, u32[]{:S(2)}) collective-permute-start(bf16[4,128,128]{2,1,0:T(8,128)(2,1)S(1)} %fusion.5), channel_id=1, source_target_pairs={{0,4},{1,5},{2,6},{3,7},{4,0},{5,1},{6,2},{7,3},{8,12},{9,13},{10,... | collective-permute-start | bytes 393224 | tf_op jit(solution)/shard_map/ppermute | solution.py:237
  27.6 1.3 %shard_map.87.base_ref = f32[1024,512]{1,0:T(8,128)S(1)} custom-call(s32[15]{0:T(128)S(1)} %dynamic-slice_bitcast_fusion.info, bf16[768,1024]{1,0:T(8,128)(2,1)S(1)} %copy-done.3, bf16[784,1024]{1,0:T(8,128)(2,1)S(1)} %collective-permute-done.1.got_ref.part_ref, f32[8,18,256]{2,1,0:T(8,128)S(1)} %fusion.3.lam_ref.lam0_ref, ...), custom_call_target="tpu_custom_call" | custom-call | flops 1840000000 | bytes 1048576 | tf_op jit(solution)/shard_map/pallas_call | solution.py:22
  28.9 2.4 %collective-permute-done.7.refs_5_ = bf16[640,256]{1,0:T(8,128)(2,1)S(1)} collective-permute-done((bf16[640,256]{1,0:T(8,128)(2,1)S(1)}, bf16[640,256]{1,0:T(8,128)(2,1)S(1)}, u32[]{:S(2)}, u32[]{:S(2)}) %collective-permute-start.7) | collective-permute-done | bytes 327712 | tf_op jit(solution)/shard_map/ppermute | solution.py:343
  31.3 1.4 %collective-permute-done.3 = bf16[4,128,128]{2,1,0:T(8,128)(2,1)S(1)} collective-permute-done((bf16[4,128,128]{2,1,0:T(8,128)(2,1)S(1)}, bf16[4,128,128]{2,1,0:T(8,128)(2,1)S(1)}, u32[]{:S(2)}, u32[]{:S(2)}) %collective-permute-start.3) | collective-permute-done | bytes 131104 | tf_op jit(solution)/shard_map/ppermute | solution.py:237
  32.7 0.0 collective-permute-done.6.refs_4_
  32.7 0.0 collective-permute-done.8.refs_3_
  32.7 0.4 collective-permute-start.9
  33.2 1.6 %collective-permute-start.10 = (bf16[640,256]{1,0:T(8,128)(2,1)S(1)}, bf16[640,256]{1,0:T(8,128)(2,1)S(1)}, u32[]{:S(2)}, u32[]{:S(2)}) collective-permute-start(bf16[640,256]{1,0:T(8,128)(2,1)S(1)} %collective-permute-done.7.refs_5_), channel_id=1, source_target_pairs={{4,0},{5,1},{8,4},{9,5},{12,8},{13,9},{14,12},{15,13},{10,14},{11,... | collective-permute-start | bytes 983048 | tf_op jit(solution)/shard_map/ppermute | solution.py:343
  34.9 0.1 maximum_select_fusion.3
  35.0 1.6 %collective-permute-start.13 = (bf16[768,256]{1,0:T(8,128)(2,1)S(1)}, bf16[768,256]{1,0:T(8,128)(2,1)S(1)}, u32[]{:S(2)}, u32[]{:S(2)}) collective-permute-start(bf16[768,256]{1,0:T(8,128)(2,1)S(1)} %maximum_select_fusion.3), channel_id=1, source_target_pairs={{0,16},{16,0},{1,17},{17,1},{2,18},{18,2},{3,19},{19,3},{4,20},{20... | collective-permute-start | bytes 1179656 | tf_op jit(solution)/shard_map/ppermute | solution.py:361
  36.5 3.5 %collective-permute-done.9.refs_0_ = bf16[640,256]{1,0:T(8,128)(2,1)S(1)} collective-permute-done((bf16[640,256]{1,0:T(8,128)(2,1)S(1)}, bf16[640,256]{1,0:T(8,128)(2,1)S(1)}, u32[]{:S(2)}, u32[]{:S(2)}) %collective-permute-start.9) | collective-permute-done | bytes 327712 | tf_op jit(solution)/shard_map/ppermute | solution.py:342
  40.1 0.8 %collective-permute-done.10.refs_1_ = bf16[640,256]{1,0:T(8,128)(2,1)S(1)} collective-permute-done((bf16[640,256]{1,0:T(8,128)(2,1)S(1)}, bf16[640,256]{1,0:T(8,128)(2,1)S(1)}, u32[]{:S(2)}, u32[]{:S(2)}) %collective-permute-start.10) | collective-permute-done | bytes 327712 | tf_op jit(solution)/shard_map/ppermute | solution.py:343
  40.9 4.2 %collective-permute-start.11 = (bf16[4,128,128]{2,1,0:T(8,128)(2,1)S(1)}, bf16[4,128,128]{2,1,0:T(8,128)(2,1)S(1)}, u32[]{:S(2)}, u32[]{:S(2)}) collective-permute-start(bf16[4,128,128]{2,1,0:T(8,128)(2,1)S(1)} %add_convert_fusion), channel_id=1, source_target_pairs={{0,8},{1,9},{2,10},{3,11},{4,12},{5,13},{6,14},{7,15},{16,24},{17,... | collective-permute-start | bytes 393224 | tf_op jit(solution)/shard_map/ppermute | solution.py:237
  45.1 0.6 collective-permute-start.16
  45.8 1.5 %collective-permute-start.17 = (bf16[384,256]{1,0:T(8,128)(2,1)S(1)}, bf16[384,256]{1,0:T(8,128)(2,1)S(1)}, u32[]{:S(2)}, u32[]{:S(2)}) collective-permute-start(bf16[384,256]{1,0:T(8,128)(2,1)S(1)} %slice.110), channel_id=1, source_target_pairs={{4,0},{5,1},{8,4},{9,5},{12,8},{13,9},{14,12},{15,13},{10,14},{11,... | collective-permute-start | bytes 589832 | tf_op jit(solution)/shard_map/ppermute | solution.py:343
  47.3 0.3 collective-permute-done.11
  47.6 0.1 collective-permute-start.12
  47.7 0.1 maximum_select_fusion.4
  47.8 0.0 copy-start.4
  47.8 1.1 %collective-permute-start.15 = (bf16[768,256]{1,0:T(8,128)(2,1)S(1)}, bf16[768,256]{1,0:T(8,128)(2,1)S(1)}, u32[]{:S(2)}, u32[]{:S(2)}) collective-permute-start(bf16[768,256]{1,0:T(8,128)(2,1)S(1)} %maximum_select_fusion.4), channel_id=1, source_target_pairs={{0,16},{16,0},{1,17},{17,1},{2,18},{18,2},{3,19},{19,3},{4,20},{20... | collective-permute-start | bytes 1179656 | tf_op jit(solution)/shard_map/ppermute | solution.py:361
  49.0 1.3 %collective-permute-done.16.refs_3_ = bf16[256,256]{1,0:T(8,128)(2,1)S(1)} collective-permute-done((bf16[256,256]{1,0:T(8,128)(2,1)S(1)}, bf16[256,256]{1,0:T(8,128)(2,1)S(1)}, u32[]{:S(2)}, u32[]{:S(2)}) %collective-permute-start.16) | collective-permute-done | bytes 131104 | tf_op jit(solution)/shard_map/ppermute | solution.py:342
  50.3 1.3 %collective-permute-done.17.refs_4_ = bf16[384,256]{1,0:T(8,128)(2,1)S(1)} collective-permute-done((bf16[384,256]{1,0:T(8,128)(2,1)S(1)}, bf16[384,256]{1,0:T(8,128)(2,1)S(1)}, u32[]{:S(2)}, u32[]{:S(2)}) %collective-permute-start.17) | collective-permute-done | bytes 196640 | tf_op jit(solution)/shard_map/ppermute | solution.py:343
  51.5 0.1 fusion
  51.6 1.3 %collective-permute-start.18 = (bf16[384,256]{1,0:T(8,128)(2,1)S(1)}, bf16[384,256]{1,0:T(8,128)(2,1)S(1)}, u32[]{:S(2)}, u32[]{:S(2)}) collective-permute-start(bf16[384,256]{1,0:T(8,128)(2,1)S(1)} %fusion), channel_id=1, source_target_pairs={{0,16},{16,0},{1,17},{17,1},{2,18},{18,2},{3,19},{19,3},{4,20},{20... | collective-permute-start | bytes 589832 | tf_op jit(solution)/shard_map/ppermute | solution.py:361
  52.9 1.2 %collective-permute-done.12 = bf16[2,4,128,128]{3,2,1,0:T(8,128)(2,1)S(1)} collective-permute-done((bf16[2,4,128,128]{3,2,1,0:T(8,128)(2,1)S(1)}, bf16[2,4,128,128]{3,2,1,0:T(8,128)(2,1)S(1)}, u32[]{:S(2)}, u32[]{:S(2)}) %collective-permute-start.12) | collective-permute-done | bytes 262176 | tf_op jit(solution)/shard_map/ppermute | solution.py:237
  54.1 0.1 maximum_select_fusion.1
  54.2 0.0 copy-start.1
  54.2 1.7 %shard_map.88.normed_ref = bf16[512,1024]{1,0:T(8,128)(2,1)S(1)} custom-call(s32[15]{0:T(128)S(1)} %dynamic-slice_bitcast_fusion.info, bf16[768,1024]{1,0:T(8,128)(2,1)S(1)} %copy-done.3, bf16[784,1024]{1,0:T(8,128)(2,1)S(1)} %collective-permute-done.1.got_ref.part_ref, f32[8,18,256]{2,1,0:T(8,128)S(1)} %fusion.3.lam_ref.lam0_ref, ...), custom_call_target="tpu_custom_call" | custom-call | flops 2300000000 | bytes 1048576 | tf_op jit(solution)/shard_map/pallas_call | solution.py:22
  55.9 0.0 collective-permute-done.13.refs_6_
  55.9 2.4 %shard_map.89 = (f32[256,1280]{1,0:T(8,128)S(1)}, bf16[256,1280]{1,0:T(8,128)(2,1)S(1)}) custom-call(s32[15]{0:T(128)S(1)} %dynamic-slice_bitcast_fusion.info, bf16[512,1024]{1,0:T(8,128)(2,1)S(1)} %shard_map.88.normed_ref, bf16[1024,256]{1,0:T(8,128)(2,1)S(1)} %copy-done.1, bf16[640,256]{1,0:T(8,128)(2,1)S(1)} %collective-permute-done.4.refs_1_, ...), custom_call_target="tpu_custom_call" | custom-call | flops 2875000064 | bytes 1048576 | tf_op jit(solution)/shard_map/pallas_call | solution.py:22
  58.3 0.1 collective-permute-start.14
  58.4 0.0 collective-permute-done.15.refs_2_
  58.4 0.5 collective-permute-done.18.refs_5_
  58.9 1.7 %shard_map.90 = (f32[256,768]{1,0:T(8,128)S(1)}, bf16[256,768]{1,0:T(8,128)(2,1)S(1)}) custom-call(s32[15]{0:T(128)S(1)} %dynamic-slice_bitcast_fusion.info, bf16[512,1024]{1,0:T(8,128)(2,1)S(1)} %shard_map.88.normed_ref, bf16[640,256]{1,0:T(8,128)(2,1)S(1)} %collective-permute-done.9.refs_0_, bf16[640,256]{1,0:T(8,128)(2,1)S(1)} %collective-permute-done.10.refs_1_, ...), custom_call_target="tpu_custom_call" | custom-call | flops 1724999936 | bytes 1048576 | tf_op jit(solution)/shard_map/pallas_call | solution.py:22
  60.6 0.1 collective-permute-start.19
  60.7 1.7 %collective-permute-done.19.refs_3_ = bf16[256,768]{1,0:T(8,128)(2,1)S(1)} collective-permute-done((bf16[256,768]{1,0:T(8,128)(2,1)S(1)}, bf16[256,768]{1,0:T(8,128)(2,1)S(1)}, u32[]{:S(2)}, u32[]{:S(2)}) %collective-permute-start.19) | collective-permute-done | bytes 393248 | tf_op jit(solution)/shard_map/ppermute | solution.py:237
  62.4 0.0 collective-permute-done.14.refs_1_
  62.4 1.6 %shard_map.91 = bf16[256,2048]{1,0:T(8,128)(2,1)} custom-call(s32[15]{0:T(128)S(1)} %dynamic-slice_bitcast_fusion.info, f32[256,1280]{1,0:T(8,128)S(1)} %get-tuple-element.37.refs_0_, bf16[256,1280]{1,0:T(8,128)(2,1)S(1)} %collective-permute-done.14.refs_1_, f32[256,768]{1,0:T(8,128)S(1)} %get-tuple-element.41.refs_2_, ...), custom_call_target="tpu_custom_call" | custom-call | flops 1150000000 | bytes 1048576 | tf_op jit(solution)/shard_map/pallas_call | solution.py:424
  (28 shorter events, 0.5 us)
Async XLA Ops:
  0.0 4.9 %collective-permute-start = (bf16[2048,128]{1,0:T(8,128)(2,1)}, bf16[2048,128]{1,0:T(8,128)(2,1)S(1)}, u32[]{:S(2)}, u32[]{:S(2)}) collective-permute-start(bf16[2048,128]{1,0:T(8,128)(2,1)} %param.14), channel_id=1, source_target_pairs={{0,1},{1,0},{2,3},{3,2},{4,5},{5,4},{6,7},{7,6},{8,9},{9,8},{10,11... | collective-permute-start | bytes 1572872 | tf_op jit(solution)/shard_map/ppermute | solution.py:237
  0.5 3.5 %copy-start.6 = (f32[64,18,16]{0,2,1:T(8,128)S(1)}, f32[64,18,16]{0,2,1:T(8,128)}, u32[]{:S(2)}) copy-start(f32[64,18,16]{0,2,1:T(8,128)} %param.12) | copy-start | bytes 221188
  0.5 4.2 %copy-start.7 = (s32[256]{0:T(256)S(1)}, s32[256]{0:T(256)}, u32[]{:S(2)}) copy-start(s32[256]{0:T(256)} %after_ref.1) | copy-start | bytes 3076
  0.5 4.4 %copy-start.5 = (bf16[2048,128]{1,0:T(8,128)(2,1)S(1)}, bf16[2048,128]{1,0:T(8,128)(2,1)}, u32[]{:S(2)}) copy-start(bf16[2048,128]{1,0:T(8,128)(2,1)} %param.14) | copy-start | bytes 1572868
  3.8 7.7 %collective-permute-start.1 = (bf16[784,1024]{1,0:T(8,128)(2,1)}, bf16[784,1024]{1,0:T(8,128)(2,1)S(1)}, u32[]{:S(2)}, u32[]{:S(2)}) collective-permute-start(bf16[784,1024]{1,0:T(8,128)(2,1)} %shard_map.83), channel_id=1, source_target_pairs={{0,1},{1,0},{2,3},{3,2},{4,5},{5,4},{6,7},{7,6},{8,9},{9,8},{10,11... | collective-permute-start | bytes 4816904 | tf_op jit(solution)/shard_map/ppermute | solution.py:237
  5.1 3.1 %copy-start = (bf16[1024,256]{1,0:T(8,128)(2,1)}, bf16[1024,256]{1,0:T(8,128)(2,1)S(1)}, u32[]{:S(2)}) copy-start(bf16[1024,256]{1,0:T(8,128)(2,1)S(1)} %maximum_select_fusion.after_ref.refs_0_) | copy-start | bytes 1572868
  5.2 10.9 %collective-permute-start.4 = (bf16[640,256]{1,0:T(8,128)(2,1)S(1)}, bf16[640,256]{1,0:T(8,128)(2,1)S(1)}, u32[]{:S(2)}, u32[]{:S(2)}) collective-permute-start(bf16[640,256]{1,0:T(8,128)(2,1)S(1)} %slice_select_fusion), channel_id=1, source_target_pairs={{0,4},{1,5},{4,8},{5,9},{8,12},{9,13},{12,14},{13,15},{14,10},{15,... | collective-permute-start | bytes 983048 | tf_op jit(solution)/shard_map/ppermute | solution.py:342
  8.3 9.4 %collective-permute-start.5 = (bf16[640,256]{1,0:T(8,128)(2,1)S(1)}, bf16[640,256]{1,0:T(8,128)(2,1)S(1)}, u32[]{:S(2)}, u32[]{:S(2)}) collective-permute-start(bf16[640,256]{1,0:T(8,128)(2,1)S(1)} %slice_select_fusion), channel_id=1, source_target_pairs={{4,0},{5,1},{8,4},{9,5},{12,8},{13,9},{14,12},{15,13},{10,14},{11,... | collective-permute-start | bytes 983048 | tf_op jit(solution)/shard_map/ppermute | solution.py:343
  11.5 1.4 %copy-start.2 = (bf16[768,1024]{1,0:T(8,128)(2,1)S(1)}, bf16[768,1024]{1,0:T(8,128)(2,1)}, u32[]{:S(2)}) copy-start(bf16[768,1024]{1,0:T(8,128)(2,1)} %shard_map.82.mine_ref.part_ref) | copy-start | bytes 4718596
  14.0 4.0 %copy-start.3 = (bf16[768,1024]{1,0:T(8,128)(2,1)S(1)}, bf16[768,1024]{1,0:T(8,128)(2,1)}, u32[]{:S(2)}) copy-start(bf16[768,1024]{1,0:T(8,128)(2,1)} %shard_map.82.mine_ref.part_ref) | copy-start | bytes 4718596
  14.0 11.9 %collective-permute-start.2 = (bf16[8,128,128]{2,1,0:T(8,128)(2,1)S(1)}, bf16[8,128,128]{2,1,0:T(8,128)(2,1)S(1)}, u32[]{:S(2)}, u32[]{:S(2)}) collective-permute-start(bf16[8,128,128]{2,1,0:T(8,128)(2,1)S(1)} %get-tuple-element.24), channel_id=1, source_target_pairs={{0,2},{1,3},{2,0},{3,1},{4,6},{5,7},{6,4},{7,5},{8,10},{9,11},{10,... | collective-permute-start | bytes 786440 | tf_op jit(solution)/shard_map/ppermute | solution.py:237
  20.0 12.7 %collective-permute-start.6 = (bf16[640,256]{1,0:T(8,128)(2,1)S(1)}, bf16[640,256]{1,0:T(8,128)(2,1)S(1)}, u32[]{:S(2)}, u32[]{:S(2)}) collective-permute-start(bf16[640,256]{1,0:T(8,128)(2,1)S(1)} %collective-permute-done.4.refs_1_), channel_id=1, source_target_pairs={{0,4},{1,5},{4,8},{5,9},{8,12},{9,13},{12,14},{13,15},{14,10},{15,... | collective-permute-start | bytes 983048 | tf_op jit(solution)/shard_map/ppermute | solution.py:342
  21.7 9.6 %collective-permute-start.7 = (bf16[640,256]{1,0:T(8,128)(2,1)S(1)}, bf16[640,256]{1,0:T(8,128)(2,1)S(1)}, u32[]{:S(2)}, u32[]{:S(2)}) collective-permute-start(bf16[640,256]{1,0:T(8,128)(2,1)S(1)} %collective-permute-done.5.refs_2_), channel_id=1, source_target_pairs={{4,0},{5,1},{8,4},{9,5},{12,8},{13,9},{14,12},{15,13},{10,14},{11,... | collective-permute-start | bytes 983048 | tf_op jit(solution)/shard_map/ppermute | solution.py:343
  22.2 10.5 %collective-permute-start.8 = (bf16[768,256]{1,0:T(8,128)(2,1)S(1)}, bf16[768,256]{1,0:T(8,128)(2,1)S(1)}, u32[]{:S(2)}, u32[]{:S(2)}) collective-permute-start(bf16[768,256]{1,0:T(8,128)(2,1)S(1)} %maximum_select_fusion.2), channel_id=1, source_target_pairs={{0,16},{16,0},{1,17},{17,1},{2,18},{18,2},{3,19},{19,3},{4,20},{20... | collective-permute-start | bytes 1179656 | tf_op jit(solution)/shard_map/ppermute | solution.py:361
  26.0 6.7 %collective-permute-start.3 = (bf16[4,128,128]{2,1,0:T(8,128)(2,1)S(1)}, bf16[4,128,128]{2,1,0:T(8,128)(2,1)S(1)}, u32[]{:S(2)}, u32[]{:S(2)}) collective-permute-start(bf16[4,128,128]{2,1,0:T(8,128)(2,1)S(1)} %fusion.5), channel_id=1, source_target_pairs={{0,4},{1,5},{2,6},{3,7},{4,0},{5,1},{6,2},{7,3},{8,12},{9,13},{10,... | collective-permute-start | bytes 393224 | tf_op jit(solution)/shard_map/ppermute | solution.py:237
  32.7 7.3 %collective-permute-start.9 = (bf16[640,256]{1,0:T(8,128)(2,1)S(1)}, bf16[640,256]{1,0:T(8,128)(2,1)S(1)}, u32[]{:S(2)}, u32[]{:S(2)}) collective-permute-start(bf16[640,256]{1,0:T(8,128)(2,1)S(1)} %collective-permute-done.6.refs_4_), channel_id=1, source_target_pairs={{0,4},{1,5},{4,8},{5,9},{8,12},{9,13},{12,14},{13,15},{14,10},{15,... | collective-permute-start | bytes 983048 | tf_op jit(solution)/shard_map/ppermute | solution.py:342
  33.2 7.7 %collective-permute-start.10 = (bf16[640,256]{1,0:T(8,128)(2,1)S(1)}, bf16[640,256]{1,0:T(8,128)(2,1)S(1)}, u32[]{:S(2)}, u32[]{:S(2)}) collective-permute-start(bf16[640,256]{1,0:T(8,128)(2,1)S(1)} %collective-permute-done.7.refs_5_), channel_id=1, source_target_pairs={{4,0},{5,1},{8,4},{9,5},{12,8},{13,9},{14,12},{15,13},{10,14},{11,... | collective-permute-start | bytes 983048 | tf_op jit(solution)/shard_map/ppermute | solution.py:343
  35.0 21.0 %collective-permute-start.13 = (bf16[768,256]{1,0:T(8,128)(2,1)S(1)}, bf16[768,256]{1,0:T(8,128)(2,1)S(1)}, u32[]{:S(2)}, u32[]{:S(2)}) collective-permute-start(bf16[768,256]{1,0:T(8,128)(2,1)S(1)} %maximum_select_fusion.3), channel_id=1, source_target_pairs={{0,16},{16,0},{1,17},{17,1},{2,18},{18,2},{3,19},{19,3},{4,20},{20... | collective-permute-start | bytes 1179656 | tf_op jit(solution)/shard_map/ppermute | solution.py:361
  40.9 6.7 %collective-permute-start.11 = (bf16[4,128,128]{2,1,0:T(8,128)(2,1)S(1)}, bf16[4,128,128]{2,1,0:T(8,128)(2,1)S(1)}, u32[]{:S(2)}, u32[]{:S(2)}) collective-permute-start(bf16[4,128,128]{2,1,0:T(8,128)(2,1)S(1)} %add_convert_fusion), channel_id=1, source_target_pairs={{0,8},{1,9},{2,10},{3,11},{4,12},{5,13},{6,14},{7,15},{16,24},{17,... | collective-permute-start | bytes 393224 | tf_op jit(solution)/shard_map/ppermute | solution.py:237
  45.1 5.1 %collective-permute-start.16 = (bf16[256,256]{1,0:T(8,128)(2,1)S(1)}, bf16[256,256]{1,0:T(8,128)(2,1)S(1)}, u32[]{:S(2)}, u32[]{:S(2)}) collective-permute-start(bf16[256,256]{1,0:T(8,128)(2,1)S(1)} %slice.109), channel_id=1, source_target_pairs={{0,4},{1,5},{4,8},{5,9},{8,12},{9,13},{12,14},{13,15},{14,10},{15,... | collective-permute-start | bytes 393224 | tf_op jit(solution)/shard_map/ppermute | solution.py:342
  45.8 5.7 %collective-permute-start.17 = (bf16[384,256]{1,0:T(8,128)(2,1)S(1)}, bf16[384,256]{1,0:T(8,128)(2,1)S(1)}, u32[]{:S(2)}, u32[]{:S(2)}) collective-permute-start(bf16[384,256]{1,0:T(8,128)(2,1)S(1)} %slice.110), channel_id=1, source_target_pairs={{4,0},{5,1},{8,4},{9,5},{12,8},{13,9},{14,12},{15,13},{10,14},{11,... | collective-permute-start | bytes 589832 | tf_op jit(solution)/shard_map/ppermute | solution.py:343
  47.6 6.4 %collective-permute-start.12 = (bf16[2,4,128,128]{3,2,1,0:T(8,128)(2,1)S(1)}, bf16[2,4,128,128]{3,2,1,0:T(8,128)(2,1)S(1)}, u32[]{:S(2)}, u32[]{:S(2)}) collective-permute-start(bf16[2,4,128,128]{3,2,1,0:T(8,128)(2,1)S(1)} %pad_maximum_fusion), channel_id=1, source_target_pairs={{0,2},{1,3},{2,0},{3,1},{4,6},{5,7},{6,4},{7,5},{8,10},{9,11},{10,... | collective-permute-start | bytes 786440 | tf_op jit(solution)/shard_map/ppermute | solution.py:237
  47.8 6.4 %copy-start.4 = (f32[2048]{0:T(1024)S(1)}, f32[2048]{0:T(1024)}, u32[]{:S(2)}) copy-start(f32[2048]{0:T(1024)} %param.13) | copy-start | bytes 24580
  47.8 10.5 %collective-permute-start.15 = (bf16[768,256]{1,0:T(8,128)(2,1)S(1)}, bf16[768,256]{1,0:T(8,128)(2,1)S(1)}, u32[]{:S(2)}, u32[]{:S(2)}) collective-permute-start(bf16[768,256]{1,0:T(8,128)(2,1)S(1)} %maximum_select_fusion.4), channel_id=1, source_target_pairs={{0,16},{16,0},{1,17},{17,1},{2,18},{18,2},{3,19},{19,3},{4,20},{20... | collective-permute-start | bytes 1179656 | tf_op jit(solution)/shard_map/ppermute | solution.py:361
  51.6 7.3 %collective-permute-start.18 = (bf16[384,256]{1,0:T(8,128)(2,1)S(1)}, bf16[384,256]{1,0:T(8,128)(2,1)S(1)}, u32[]{:S(2)}, u32[]{:S(2)}) collective-permute-start(bf16[384,256]{1,0:T(8,128)(2,1)S(1)} %fusion), channel_id=1, source_target_pairs={{0,16},{16,0},{1,17},{17,1},{2,18},{18,2},{3,19},{19,3},{4,20},{20... | collective-permute-start | bytes 589832 | tf_op jit(solution)/shard_map/ppermute | solution.py:361
  54.2 1.7 %copy-start.1 = (bf16[1024,256]{1,0:T(8,128)(2,1)S(1)}, bf16[1024,256]{1,0:T(8,128)(2,1)}, u32[]{:S(2)}) copy-start(bf16[1024,256]{1,0:T(8,128)(2,1)} %copy-done) | copy-start | bytes 1572868
  58.3 4.1 %collective-permute-start.14 = (bf16[256,1280]{1,0:T(8,128)(2,1)S(1)}, bf16[256,1280]{1,0:T(8,128)(2,1)S(1)}, u32[]{:S(2)}, u32[]{:S(2)}) collective-permute-start(bf16[256,1280]{1,0:T(8,128)(2,1)S(1)} %get-tuple-element.38), channel_id=1, source_target_pairs={{0,1},{1,0},{2,3},{3,2},{4,5},{5,4},{6,7},{7,6},{8,9},{9,8},{10,11... | collective-permute-start | bytes 1966088 | tf_op jit(solution)/shard_map/ppermute | solution.py:237
  60.6 1.8 %collective-permute-start.19 = (bf16[256,768]{1,0:T(8,128)(2,1)S(1)}, bf16[256,768]{1,0:T(8,128)(2,1)S(1)}, u32[]{:S(2)}, u32[]{:S(2)}) collective-permute-start(bf16[256,768]{1,0:T(8,128)(2,1)S(1)} %get-tuple-element.42), channel_id=1, source_target_pairs={{0,1},{1,0},{2,3},{3,2},{4,5},{5,4},{6,7},{7,6},{8,9},{9,8},{10,11... | collective-permute-start | bytes 1179656 | tf_op jit(solution)/shard_map/ppermute | solution.py:237

commit v4 on v3

--- a/solution.py
+++ b/solution.py
@@ -11,7 +11,6 @@
 from jax.sharding import PartitionSpec as P
 
 TILE = 128
-LATE = 1
 VM = pl.BlockSpec(memory_space=pltpu.VMEM)
 SM = pl.BlockSpec(memory_space=pltpu.SMEM)
 PARAMS = pltpu.CompilerParams(vmem_limit_bytes=8 * 1024 * 1024)
@@ -41,32 +40,34 @@
     return lax.dot_general(a, b, (((ca,), (cb,)), ((), ())), preferred_element_type=jnp.float32)
 
 
-def split_kernel(to_other, k_ref, v_ref, q_ref, index_ref, after_ref, out_ref, sems):
+def split_kernel(count, *refs):
+    index_ref, out_ref, sems = refs[count], refs[-2], refs[-1]
     half = out_ref.shape[1]
-    rows = k_ref.shape[0]
-    side = (lax.axis_index("seq") + to_other) % 2
+    rows = refs[0].shape[0]
+    side = (lax.axis_index("seq") + 1) % 2
     copies = []
-    for at, ref in enumerate((k_ref, v_ref, q_ref)):
-        copies.append((ref.at[:, lanes(side * half, half)], out_ref.at[pl.ds(at * rows, rows), :]))
-    copies = [pltpu.make_async_copy(a, b, sems.at[n]) for n, (a, b) in enumerate(copies)]
+    for at, ref in enumerate(refs[:count]):
+        source = ref.at[:, lanes(side * half, half)]
+        copies.append(pltpu.make_async_copy(source, out_ref.at[pl.ds(at * rows, rows), :], sems.at[at]))
     for copy in copies:
         copy.start()
-    tail = out_ref.shape[0] - 3 * rows
+    tail = out_ref.shape[0] - count * rows
     if tail:
         row = jnp.broadcast_to(index_ref[...].astype(jnp.float32), (tail, rows)).astype(jnp.bfloat16)
-        out_ref[pl.ds(3 * rows, tail), :] = jnp.zeros((tail, half), jnp.bfloat16)
-        out_ref[pl.ds(3 * rows, tail), pl.ds(0, rows)] = row
+        out_ref[pl.ds(count * rows, tail), :] = jnp.zeros((tail, half), jnp.bfloat16)
+        out_ref[pl.ds(count * rows, tail), pl.ds(0, rows)] = row
     for copy in copies:
         copy.wait()
 
 
-def state_kernel(info, mine_ref, got_ref, sum_ref, send_ref, even_ref):
+def state_kernel(info, k_ref, v_ref, got_ref, sum_ref, send_ref, even_ref):
     heads, dim, _ = sum_ref.shape
-    rows = mine_ref.shape[0] // 3
+    rows = k_ref.shape[0]
     core = info[0]
     for h in range(heads):
         far = pl.ds(h * dim, dim)
-        mine = dot(mine_ref[pl.ds(rows, rows), far], mine_ref[pl.ds(0, rows), far], 0, 0)
+        own = lanes(core * heads * dim + h * dim, dim)
+        mine = dot(v_ref[:, own], k_ref[:, own], 0, 0)
         theirs = dot(got_ref[pl.ds(rows, rows), far], got_ref[pl.ds(0, rows), far], 0, 0)
         both = mine + theirs
         sum_ref[h] = both
@@ -74,7 +75,8 @@
         even_ref[h] = jnp.where(core == 0, mine, theirs).astype(jnp.bfloat16)
 
 
-def local_kernel(lam_ref, part_ref, out_ref):
+def local_kernel(own_side, info, lam_ref, *refs):
+    out_ref = refs[-1]
     heads = lam_ref.shape[0]
     dim, rows = out_ref.shape[0] // heads, out_ref.shape[1]
     scale = 1.0 / math.sqrt(dim)
@@ -90,7 +92,10 @@
     for h in range(heads):
 
         def part(which, first, count):
-            return part_ref[pl.ds(which * rows + first, count), pl.ds(h * dim, dim)]
+            if own_side:
+                return refs[which][pl.ds(first, count), lanes(info[0] * heads * dim + h * dim, dim)]
+            ref, at = (refs[0], which * rows) if which < 2 else (refs[1], 0)
+            return ref[pl.ds(at + first, count), pl.ds(h * dim, dim)]
 
         lam = lam_ref[h] * scale
         totals = [None] * blocks
@@ -116,10 +121,10 @@
             out_ref[pl.ds(h * dim, dim), pl.ds(t * step, step)] = totals[t]
 
 
-def early_kernel(levels, log_stretch, info, mine_ref, got_ref, lam0_ref, lam1_ref, base0_ref, base1_ref, *refs):
+def early_kernel(levels, log_stretch, info, q_ref, got_ref, lam0_ref, lam1_ref, base0_ref, base1_ref, *refs):
     buckets, out_ref = refs[:-1], refs[-1]
     heads = lam0_ref.shape[0]
-    rows = mine_ref.shape[0] // 3
+    rows = q_ref.shape[0]
     dim = base0_ref.shape[0] // heads
     core = info[0]
     scale = 1.0 / math.sqrt(dim)
@@ -128,7 +133,10 @@
         for side in range(2):
             odd = core if side == 0 else 1 - core
             lam = (lam0_ref, lam1_ref)[side][h]
-            q = (mine_ref, got_ref)[side][pl.ds(2 * rows, rows), far]
+            if side == 0:
+                q = q_ref[:, lanes(core * heads * dim + h * dim, dim)]
+            else:
+                q = got_ref[pl.ds(0, rows), far]
             total = (base0_ref, base1_ref)[side][far, :]
             for at, level in enumerate(levels):
                 column = log_stretch + 1 + level
@@ -138,10 +146,10 @@
             out_ref[far, pl.ds(side * rows, rows)] = total
 
 
-def last_kernel(levels, log_stretch, info, mine_ref, got_ref, lam0_ref, lam1_ref, base_ref, gain_ref, *refs):
+def last_kernel(levels, log_stretch, info, q_ref, got_ref, lam0_ref, lam1_ref, base_ref, gain_ref, *refs):
     buckets, out_ref = refs[:-1], refs[-1]
     heads = lam0_ref.shape[0]
-    rows = mine_ref.shape[0] // 3
+    rows = q_ref.shape[0]
     dim = base_ref.shape[0] // heads
     core = info[0]
     scale = 1.0 / math.sqrt(dim)
@@ -151,7 +159,10 @@
         for side in range(2):
             at_rows = pl.ds(side * rows, rows)
             lam = (lam0_ref, lam1_ref)[side][h]
-            q = (mine_ref, got_ref)[side][pl.ds(2 * rows, rows), far]
+            if side == 0:
+                q = q_ref[:, lanes(core * heads * dim + h * dim, dim)]
+            else:
+                q = got_ref[pl.ds(0, rows), far]
             total = base_ref[far, at_rows]
             for at, level in enumerate(levels):
                 column = log_stretch + 1 + level
@@ -239,33 +250,32 @@
     packs = table_rows <= 256 and stretch <= half
     bf16 = functools.partial(jax.ShapeDtypeStruct, dtype=jnp.bfloat16)
 
-    def split(to_other, rows, after):
+    def split(arrays, tail, after):
         hbm = pl.BlockSpec(memory_space=pltpu.HBM)
         return pl.pallas_call(
-            functools.partial(split_kernel, to_other),
-            out_shape=bf16((rows, half)),
-            in_specs=[hbm] * 3 + [VM, pl.BlockSpec(memory_space=pl.ANY)],
+            functools.partial(split_kernel, len(arrays)),
+            out_shape=bf16((len(arrays) * stretch + tail, half)),
+            in_specs=[hbm] * len(arrays) + [VM, pl.BlockSpec(memory_space=pl.ANY)],
             out_specs=VM,
-            scratch_shapes=[pltpu.SemaphoreType.DMA((3,))],
+            scratch_shapes=[pltpu.SemaphoreType.DMA((len(arrays),))],
             compiler_params=pltpu.CompilerParams(vmem_limit_bytes=56 * 1024 * 1024),
-            cost_estimate=pl.CostEstimate(flops=us(2.5), bytes_accessed=1 << 21, transcendentals=0),
-        )(keys, values, queries, level_index.reshape(1, stretch), after)
+            cost_estimate=pl.CostEstimate(flops=us(2.0), bytes_accessed=1 << 20, transcendentals=0),
+        )(*arrays, level_index.reshape(1, stretch), after)
 
     w_got = swap(out_weight, 0)
-    sent = split(1, (3 * stretch + 16) if packs else 3 * stretch, level_index)
-    got = swap(sent, 0)
-    if packs:
-        index_got = got[3 * stretch, :stretch].astype(jnp.int32)
-    else:
-        index_got = swap(level_index, 0)
-
+    got_kv = swap(split([keys, values], 0, level_index), 0)
     whole = jnp.where(
         core == 0,
         jnp.concatenate([out_weight[:half], w_got[:half]], axis=1),
         jnp.concatenate([w_got[half:], out_weight[half:]], axis=1),
     )
 
-    mine = split(0, 3 * stretch, whole)
+    got_q = swap(split([queries], 16 if packs else 0, whole), 0)
+    if packs:
+        index_got = got_q[stretch, :stretch].astype(jnp.int32)
+    else:
+        index_got = swap(level_index, 0)
+
     table = jnp.transpose(level_table, (2, 1, 0))
     table = jnp.where(core == 0, table[:pair_heads], table[pair_heads:]).reshape(-1, table_rows)
 
@@ -282,10 +292,10 @@
     total, send, even = call(
         state_kernel,
         (state, state16, state16),
-        [SM] + [VM] * 2,
+        [SM] + [VM] * 3,
         us(1.0),
         1 << 20,
-        info, mine, got,
+        info, keys, values, got_kv,
     )
     send_first = send
     buckets = [even]
@@ -299,7 +309,7 @@
 
     def level(bit):
         nonlocal total, send
-        came = swap(send, bit, upward=bit == log_blocks - 1)
+        came = swap(send, bit)
         if bit + 1 < log_blocks:
             total = total + came
             if bit == 1:
@@ -316,7 +326,7 @@
 
     pieces = []
     plan = []
-    late = []
+    middle, late = [], []
     landed = ()
     if ringed:
         clockwise = []
@@ -343,7 +353,7 @@
             left = lax.ppermute(left, "seq", counter)
             if r == 1:
                 right, left, _ = lax.optimization_barrier((right, left, send_first))
-            if r == 3:
+            if r == 2:
                 send = tie(send, right, left)
             at = len(pieces)
             pieces += [right, left]
@@ -362,7 +372,7 @@
                 pieces.append(crossed[-1])
                 for n, part in enumerate(parts):
                     part.append((at + 2, n * shared, k_lacks, 0, shared))
-            (late if r >= rounds - LATE else plan).extend(
+            (plan if r < rounds - 1 else late if last else middle).extend(
                 (chip_at + d, part) for d, part in zip(distances, parts)
             )
     else:
@@ -381,10 +391,12 @@
 
     side_shape = jax.ShapeDtypeStruct((half, stretch), jnp.float32)
     acc_own = call(
-        local_kernel, side_shape, [VM] * 2, us(2.1), 1 << 20, tie(lam_own, reached[0]), mine,
+        functools.partial(local_kernel, True), side_shape, [SM] + [VM] * 4, us(2.1), 1 << 20,
+        info, tie(lam_own, reached[0]), keys, values, queries,
     )
     acc_got = call(
-        local_kernel, side_shape, [VM] * 2, us(2.1), 1 << 20, lam_got, got,
+        functools.partial(local_kernel, False), side_shape, [SM] + [VM] * 3, us(2.1), 1 << 20,
+        info, tie(lam_got, reached[min(2, len(reached) - 1)]), got_kv, got_q,
     )
     acc = call(
         functools.partial(early_kernel, [0, 1], log_stretch),
@@ -392,7 +404,7 @@
         [SM] + [VM] * 8,
         us(1.6),
         1 << 20,
-        info, mine, got, lam_own, lam_got, acc_own, acc_got, *buckets[:2],
+        info, queries, got_q, lam_own, lam_got, acc_own, acc_got, *buckets[:2],
     )
     normed = call(
         functools.partial(last_kernel, list(range(2, log_blocks)), log_stretch),
@@ -400,10 +412,10 @@
         [SM] + [VM] * (6 + len(quarters)),
         us(2.0),
         1 << 20,
-        info, mine, got, lam_own, lam_got, acc, norm_gain.reshape(1, width), *buckets[2:],
-    )
-
-    plans = [p for p in (plan, late) if p]
+        info, queries, got_q, lam_own, lam_got, acc, norm_gain.reshape(1, width), *buckets[2:],
+    )
+
+    plans = [p for p in (plan, middle, late) if p]
     shares = []
     for p in plans:
         used = sorted({part[0] for _, parts in p for part in parts})

time: 64.7 us -> 63.3 us (0.978)
  local copies, waits for them, and re-layouts: 2.43 us -> 1.03 us
  Pallas kernels: 20.4 us -> 21.4 us
  waiting for transfers between devices: 16 us -> 15.2 us
    ppermute x4, starting transfers between devices: 5.78 us -> 9.57 us  [body(): right = lax.ppermute(right, 'seq', clockwise)]
    ppermute x4, waiting for transfers between devices: 4.94 us -> 1.21 us  [body(): right = lax.ppermute(right, 'seq', clockwise)]
    ppermute x4, starting transfers between devices: 3.58 us -> 0.69 us  [body(): left = lax.ppermute(left, 'seq', counter)]
    ppermute x4, waiting for transfers between devices: 0.49 us -> 3.26 us  [body(): crossed.append(lax.ppermute(wanted, 'grp', [(0, 1), (1, 0)]))]
    ppermute x4, waiting for transfers between devices: 5.99 us -> 8.51 us  [body(): left = lax.ppermute(left, 'seq', counter)]
    ppermute x8 -> x10, waiting for transfers between devices: 4.58 us -> 2.22 us  [swap(): return lax.ppermute(block, 'seq', route)]
    pallas_call x7 -> x8, Pallas kernels: 12.2 us -> 14.2 us  [call(): pl.pallas_call(kernel, out_shape=out_shape, in_specs=in_specs, out_specs=...]
    unnamed x16 -> x18, local copies, waits for them, and re-layouts: 1.44 us -> 0.04 us
  transfers between devices with their start and end apart: 20 -> 22, of which waited for: 12 -> 10; matrix products, arithmetic and copies ran while one was open for 3% -> 3% of each run, Pallas kernels for 29% -> 31%
where the time goes in v4:
time: 63.3 us; the launch traced here: 63.1 us
  starting transfers between devices  23.9 us (38%)
  Pallas kernels  21.4 us (34%)
  waiting for transfers between devices  15.2 us (24%)
  local copies, waits for them, and re-layouts  1.03 us (2%)
  other arithmetic  0.75 us (1%)
    pallas_call x8, Pallas kernels, call(): pl.pallas_call(kernel, out_shape=out_shape, in_specs=in_specs, out_specs=...  14.2 us
    ppermute x4, starting transfers between devices, body(): right = lax.ppermute(right, 'seq', clockwise)  9.57 us
    ppermute x4, waiting for transfers between devices, body(): left = lax.ppermute(left, 'seq', counter)  8.51 us
    ppermute x10, starting transfers between devices, swap(): return lax.ppermute(block, 'seq', route)  8.07 us
    pallas_call x2, Pallas kernels, split(): pl.pallas_call(functools.partial(split_kernel, len(arrays)), out_shape=bf...  5.63 us
    ppermute x4, starting transfers between devices, body(): crossed.append(lax.ppermute(wanted, 'grp', [(0, 1), (1, 0)]))  5.57 us
    ppermute x4, waiting for transfers between devices, body(): crossed.append(lax.ppermute(wanted, 'grp', [(0, 1), (1, 0)]))  3.26 us
    ppermute x10, waiting for transfers between devices, swap(): return lax.ppermute(block, 'seq', route)  2.22 us
  transfers between devices with their start and end apart: 22, of which 10 were waited for; matrix products, arithmetic and copies ran while one was open for 3% of the time, Pallas kernels for 31%

profile of v4, /device:TPU:0, one launch (start us, length us, event | category | flops | bytes accessed | tf_op | source)
XLA Modules:
  0.0 63.1 jit_solution(13216631947837486821)
XLA Ops:
  0.0 0.5 collective-permute-start
  0.5 2.9 %shard_map.83 = bf16[512,1024]{1,0:T(8,128)(2,1)} custom-call(bf16[256,2048]{1,0:T(8,128)(2,1)} %refs_0_.5, bf16[256,2048]{1,0:T(8,128)(2,1)} %refs_1_.3, s32[1,256]{1,0:T(1,128)} %bitcast.25, s32[256]{0:T(256)} %refs_3_.1), custom_call_target="tpu_custom_call" | custom-call | flops 2300000000 | bytes 1048576 | tf_op jit(solution)/shard_map/pallas_call | solution.py:255
  3.4 0.1 collective-permute-start.2
  3.6 0.2 fusion.3.lam_ref.lam0_ref
  3.9 0.0 collective-permute-done
  3.9 0.2 maximum_select_fusion.refs_2_.refs_0_
  4.1 3.1 %collective-permute-start.5 = (bf16[640,256]{1,0:T(8,128)(2,1)S(1)}, bf16[640,256]{1,0:T(8,128)(2,1)S(1)}, u32[]{:S(2)}, u32[]{:S(2)}) collective-permute-start(bf16[640,256]{1,0:T(8,128)(2,1)S(1)} %slice_select_fusion), channel_id=1, source_target_pairs={{0,4},{1,5},{4,8},{5,9},{8,12},{9,13},{12,14},{13,15},{14,10},{15,... | collective-permute-start | bytes 983048 | tf_op jit(solution)/shard_map/ppermute | solution.py:352
  7.2 0.0 collective-permute-start.6
  7.2 0.7 %dynamic-slice_bitcast_fusion.info = s32[15]{0:T(128)S(1)} fusion(s32[2,16,15]{2,1,0:T(8,128)} %constant.36.clone, s32[]{:T(128)S(6)} %select_n.85, s32[]{:T(128)S(6)} %select_n.86), kind=kLoop, calls=%fused_computation.27 | loop fusion | bytes 128 | tf_op jit(solution)/shard_map/reshape | solution.py:244
  7.9 2.7 %shard_map.82 = bf16[272,1024]{1,0:T(8,128)(2,1)} custom-call(bf16[256,2048]{1,0:T(8,128)(2,1)} %q_ref.3, s32[1,256]{1,0:T(1,128)} %bitcast.26, bf16[1024,256]{1,0:T(8,128)(2,1)} %copy-done), custom_call_target="tpu_custom_call" | custom-call | flops 2300000000 | bytes 1048576 | tf_op jit(solution)/shard_map/pallas_call | solution.py:255
  10.6 0.1 collective-permute-start.1
  10.7 0.0 collective-permute-done.2.got_ref.refs_0_
  10.7 1.1 %shard_map.84 = (f32[8,128,128]{2,1,0:T(8,128)S(1)}, bf16[8,128,128]{2,1,0:T(8,128)(2,1)S(1)}, bf16[8,128,128]{2,1,0:T(8,128)(2,1)S(1)}) custom-call(s32[15]{0:T(128)S(1)} %dynamic-slice_bitcast_fusion.info, bf16[256,2048]{1,0:T(8,128)(2,1)S(1)} %copy-done.2, bf16[256,2048]{1,0:T(8,128)(2,1)S(1)} %copy-done.3, ...), custom_call_target="tpu_custom_call" | custom-call | flops 1150000000 | bytes 1048576 | tf_op jit(solution)/shard_map/pallas_call | solution.py:21
  11.9 0.0 copy-start.4
  11.9 2.0 %collective-permute-start.3 = (bf16[8,128,128]{2,1,0:T(8,128)(2,1)S(1)}, bf16[8,128,128]{2,1,0:T(8,128)(2,1)S(1)}, u32[]{:S(2)}, u32[]{:S(2)}) collective-permute-start(bf16[8,128,128]{2,1,0:T(8,128)(2,1)S(1)} %get-tuple-element.27), channel_id=1, source_target_pairs={{0,2},{1,3},{2,0},{3,1},{4,6},{5,7},{6,4},{7,5},{8,10},{9,11},{10,... | collective-permute-start | bytes 786440 | tf_op jit(solution)/shard_map/ppermute | solution.py:248
  13.9 1.1 %collective-permute-done.5.refs_1_ = bf16[640,256]{1,0:T(8,128)(2,1)S(1)} collective-permute-done((bf16[640,256]{1,0:T(8,128)(2,1)S(1)}, bf16[640,256]{1,0:T(8,128)(2,1)S(1)}, u32[]{:S(2)}, u32[]{:S(2)}) %collective-permute-start.5) | collective-permute-done | bytes 327712 | tf_op jit(solution)/shard_map/ppermute | solution.py:352
  15.0 1.5 %collective-permute-done.6.refs_2_ = bf16[640,256]{1,0:T(8,128)(2,1)S(1)} collective-permute-done((bf16[640,256]{1,0:T(8,128)(2,1)S(1)}, bf16[640,256]{1,0:T(8,128)(2,1)S(1)}, u32[]{:S(2)}, u32[]{:S(2)}) %collective-permute-start.6) | collective-permute-done | bytes 327712 | tf_op jit(solution)/shard_map/ppermute | solution.py:353
  16.6 1.6 %collective-permute-start.7 = (bf16[640,256]{1,0:T(8,128)(2,1)S(1)}, bf16[640,256]{1,0:T(8,128)(2,1)S(1)}, u32[]{:S(2)}, u32[]{:S(2)}) collective-permute-start(bf16[640,256]{1,0:T(8,128)(2,1)S(1)} %collective-permute-done.5.refs_1_), channel_id=1, source_target_pairs={{0,4},{1,5},{4,8},{5,9},{8,12},{9,13},{12,14},{13,15},{14,10},{15,... | collective-permute-start | bytes 983048 | tf_op jit(solution)/shard_map/ppermute | solution.py:352
  18.1 0.5 collective-permute-start.8
  18.6 0.1 fusion.18
  18.7 0.1 maximum_select_fusion.2
  18.8 1.6 %collective-permute-start.11 = (bf16[768,256]{1,0:T(8,128)(2,1)S(1)}, bf16[768,256]{1,0:T(8,128)(2,1)S(1)}, u32[]{:S(2)}, u32[]{:S(2)}) collective-permute-start(bf16[768,256]{1,0:T(8,128)(2,1)S(1)} %maximum_select_fusion.2), channel_id=1, source_target_pairs={{0,16},{16,0},{1,17},{17,1},{2,18},{18,2},{3,19},{19,3},{4,20},{20... | collective-permute-start | bytes 1179656 | tf_op jit(solution)/shard_map/ppermute | solution.py:371
  20.3 2.6 %shard_map.85.base0_ref = f32[1024,256]{1,0:T(8,128)S(1)} custom-call(s32[15]{0:T(128)S(1)} %dynamic-slice_bitcast_fusion.info, f32[8,18,256]{2,1,0:T(8,128)S(1)} %fusion.3.lam_ref.lam0_ref, bf16[256,2048]{1,0:T(8,128)(2,1)S(1)} %copy-done.2, bf16[256,2048]{1,0:T(8,128)(2,1)S(1)} %copy-done.3, bf16[256,2048]{1,0:T(8,128)(2,1)S(1)} %copy-done.4), custom_call_target="tpu_custom_call" | custom-call | flops 2415000064 | bytes 1048576 | tf_op jit(solution)/shard_map/pallas_call | solution.py:21
  23.0 0.0 collective-permute-done.1.refs_1_.got_ref
  23.0 0.2 fusion.1.lam_ref.lam1_ref
  23.2 0.0 collective-permute-done.3.refs_1_
  23.3 1.6 %collective-permute-start.4 = (bf16[4,128,128]{2,1,0:T(8,128)(2,1)S(1)}, bf16[4,128,128]{2,1,0:T(8,128)(2,1)S(1)}, u32[]{:S(2)}, u32[]{:S(2)}) collective-permute-start(bf16[4,128,128]{2,1,0:T(8,128)(2,1)S(1)} %fusion.5), channel_id=1, source_target_pairs={{0,4},{1,5},{2,6},{3,7},{4,0},{5,1},{6,2},{7,3},{8,12},{9,13},{10,... | collective-permute-start | bytes 393224 | tf_op jit(solution)/shard_map/ppermute | solution.py:248
  25.0 2.8 %collective-permute-done.8.refs_5_ = bf16[640,256]{1,0:T(8,128)(2,1)S(1)} collective-permute-done((bf16[640,256]{1,0:T(8,128)(2,1)S(1)}, bf16[640,256]{1,0:T(8,128)(2,1)S(1)}, u32[]{:S(2)}, u32[]{:S(2)}) %collective-permute-start.8) | collective-permute-done | bytes 327712 | tf_op jit(solution)/shard_map/ppermute | solution.py:353
  27.8 0.1 collective-permute-done.7.refs_4_
  27.9 0.1 maximum_select_fusion.3
  28.0 1.8 %collective-permute-start.12 = (bf16[768,256]{1,0:T(8,128)(2,1)S(1)}, bf16[768,256]{1,0:T(8,128)(2,1)S(1)}, u32[]{:S(2)}, u32[]{:S(2)}) collective-permute-start(bf16[768,256]{1,0:T(8,128)(2,1)S(1)} %maximum_select_fusion.3), channel_id=1, source_target_pairs={{0,16},{16,0},{1,17},{17,1},{2,18},{18,2},{3,19},{19,3},{4,20},{20... | collective-permute-start | bytes 1179656 | tf_op jit(solution)/shard_map/ppermute | solution.py:371
  29.8 0.0 collective-permute-done.4
  29.9 2.3 %collective-permute-start.9 = (bf16[4,128,128]{2,1,0:T(8,128)(2,1)S(1)}, bf16[4,128,128]{2,1,0:T(8,128)(2,1)S(1)}, u32[]{:S(2)}, u32[]{:S(2)}) collective-permute-start(bf16[4,128,128]{2,1,0:T(8,128)(2,1)S(1)} %add_convert_fusion), channel_id=1, source_target_pairs={{0,8},{1,9},{2,10},{3,11},{4,12},{5,13},{6,14},{7,15},{8,0},{9,1},... | collective-permute-start | bytes 393224 | tf_op jit(solution)/shard_map/ppermute | solution.py:248
  32.1 0.0 collective-permute-done.11.refs_3_
  32.1 3.0 %collective-permute-start.14 = (bf16[640,256]{1,0:T(8,128)(2,1)S(1)}, bf16[640,256]{1,0:T(8,128)(2,1)S(1)}, u32[]{:S(2)}, u32[]{:S(2)}) collective-permute-start(bf16[640,256]{1,0:T(8,128)(2,1)S(1)} %collective-permute-done.7.refs_4_), channel_id=1, source_target_pairs={{0,4},{1,5},{4,8},{5,9},{8,12},{9,13},{12,14},{13,15},{14,10},{15,... | collective-permute-start | bytes 983048 | tf_op jit(solution)/shard_map/ppermute | solution.py:352
  35.2 2.6 %shard_map.86.base1_ref = f32[1024,256]{1,0:T(8,128)S(1)} custom-call(s32[15]{0:T(128)S(1)} %dynamic-slice_bitcast_fusion.info, f32[8,18,256]{2,1,0:T(8,128)S(1)} %fusion.1.lam_ref.lam1_ref, bf16[512,1024]{1,0:T(8,128)(2,1)S(1)} %collective-permute-done.2.got_ref.refs_0_, bf16[272,1024]{1,0:T(8,128)(2,1)S(1)} %collective-permute-done.1.refs_1_.got_ref), custom_call_target="tpu_custom_call" | custom-call | flops 2415000064 | bytes 1048576 | tf_op jit(solution)/shard_map/pallas_call | solution.py:21
  37.8 1.3 %shard_map.87.base_ref = f32[1024,512]{1,0:T(8,128)S(1)} custom-call(s32[15]{0:T(128)S(1)} %dynamic-slice_bitcast_fusion.info, bf16[256,2048]{1,0:T(8,128)(2,1)S(1)} %copy-done.4, bf16[272,1024]{1,0:T(8,128)(2,1)S(1)} %collective-permute-done.1.refs_1_.got_ref, f32[8,18,256]{2,1,0:T(8,128)S(1)} %fusion.3.lam_ref.lam0_ref, ...), custom_call_target="tpu_custom_call" | custom-call | flops 1840000000 | bytes 1048576 | tf_op jit(solution)/shard_map/pallas_call | solution.py:21
  39.1 0.8 %collective-permute-done.9 = bf16[4,128,128]{2,1,0:T(8,128)(2,1)S(1)} collective-permute-done((bf16[4,128,128]{2,1,0:T(8,128)(2,1)S(1)}, bf16[4,128,128]{2,1,0:T(8,128)(2,1)S(1)}, u32[]{:S(2)}, u32[]{:S(2)}) %collective-permute-start.9) | collective-permute-done | bytes 131104 | tf_op jit(solution)/shard_map/ppermute | solution.py:248
  39.9 1.3 %collective-permute-start.10 = (bf16[2,4,128,128]{3,2,1,0:T(8,128)(2,1)S(1)}, bf16[2,4,128,128]{3,2,1,0:T(8,128)(2,1)S(1)}, u32[]{:S(2)}, u32[]{:S(2)}) collective-permute-start(bf16[2,4,128,128]{3,2,1,0:T(8,128)(2,1)S(1)} %pad_maximum_fusion), channel_id=1, source_target_pairs={{0,2},{1,3},{2,0},{3,1},{4,6},{5,7},{6,4},{7,5},{8,10},{9,11},{10,... | collective-permute-start | bytes 786440 | tf_op jit(solution)/shard_map/ppermute | solution.py:248
  41.2 3.1 %collective-permute-done.15.refs_1_ = bf16[640,256]{1,0:T(8,128)(2,1)S(1)} collective-permute-done((bf16[640,256]{1,0:T(8,128)(2,1)S(1)}, bf16[640,256]{1,0:T(8,128)(2,1)S(1)}, u32[]{:S(2)}, u32[]{:S(2)}) %collective-permute-start.15) | collective-permute-done | bytes 327712 | tf_op jit(solution)/shard_map/ppermute | solution.py:353
  44.3 0.0 collective-permute-done.14.refs_0_
  44.4 0.0 copy-start.5
  44.4 0.1 maximum_select_fusion.4
  44.5 0.6 collective-permute-start.16
  45.1 1.9 %collective-permute-start.18 = (bf16[256,256]{1,0:T(8,128)(2,1)S(1)}, bf16[256,256]{1,0:T(8,128)(2,1)S(1)}, u32[]{:S(2)}, u32[]{:S(2)}) collective-permute-start(bf16[256,256]{1,0:T(8,128)(2,1)S(1)} %slice.109), channel_id=1, source_target_pairs={{0,4},{1,5},{4,8},{5,9},{8,12},{9,13},{12,14},{13,15},{14,10},{15,... | collective-permute-start | bytes 393224 | tf_op jit(solution)/shard_map/ppermute | solution.py:352
  47.0 0.2 collective-permute-start.19
  47.2 0.1 collective-permute-done.10
  47.3 0.1 maximum_select_fusion.1
  47.4 1.7 %shard_map.88.normed_ref = bf16[512,1024]{1,0:T(8,128)(2,1)S(1)} custom-call(s32[15]{0:T(128)S(1)} %dynamic-slice_bitcast_fusion.info, bf16[256,2048]{1,0:T(8,128)(2,1)S(1)} %copy-done.4, bf16[272,1024]{1,0:T(8,128)(2,1)S(1)} %collective-permute-done.1.refs_1_.got_ref, f32[8,18,256]{2,1,0:T(8,128)S(1)} %fusion.3.lam_ref.lam0_ref, ...), custom_call_target="tpu_custom_call" | custom-call | flops 2300000000 | bytes 1048576 | tf_op jit(solution)/shard_map/pallas_call | solution.py:21
  49.2 0.0 collective-permute-done.12.refs_6_
  49.2 2.3 %shard_map.89 = (f32[256,1280]{1,0:T(8,128)S(1)}, bf16[256,1280]{1,0:T(8,128)(2,1)S(1)}) custom-call(s32[15]{0:T(128)S(1)} %dynamic-slice_bitcast_fusion.info, bf16[512,1024]{1,0:T(8,128)(2,1)S(1)} %shard_map.88.normed_ref, bf16[1024,256]{1,0:T(8,128)(2,1)S(1)} %copy-done.1, bf16[640,256]{1,0:T(8,128)(2,1)S(1)} %collective-permute-done.5.refs_1_, ...), custom_call_target="tpu_custom_call" | custom-call | flops 2875000064 | bytes 1048576 | tf_op jit(solution)/shard_map/pallas_call | solution.py:21
  51.5 0.1 collective-permute-start.13
  51.6 1.1 %collective-permute-done.19.refs_1_ = bf16[384,256]{1,0:T(8,128)(2,1)S(1)} collective-permute-done((bf16[384,256]{1,0:T(8,128)(2,1)S(1)}, bf16[384,256]{1,0:T(8,128)(2,1)S(1)}, u32[]{:S(2)}, u32[]{:S(2)}) %collective-permute-start.19) | collective-permute-done | bytes 196640 | tf_op jit(solution)/shard_map/ppermute | solution.py:353
  52.7 0.1 fusion
  52.8 1.6 %collective-permute-start.20 = (bf16[384,256]{1,0:T(8,128)(2,1)S(1)}, bf16[384,256]{1,0:T(8,128)(2,1)S(1)}, u32[]{:S(2)}, u32[]{:S(2)}) collective-permute-start(bf16[384,256]{1,0:T(8,128)(2,1)S(1)} %fusion), channel_id=1, source_target_pairs={{0,16},{16,0},{1,17},{17,1},{2,18},{18,2},{3,19},{19,3},{4,20},{20... | collective-permute-start | bytes 589832 | tf_op jit(solution)/shard_map/ppermute | solution.py:371
  54.3 0.0 collective-permute-done.16.refs_2_
  54.3 1.4 %shard_map.90 = (f32[256,512]{1,0:T(8,128)S(1)}, bf16[256,512]{1,0:T(8,128)(2,1)S(1)}) custom-call(s32[15]{0:T(128)S(1)} %dynamic-slice_bitcast_fusion.info, bf16[512,1024]{1,0:T(8,128)(2,1)S(1)} %shard_map.88.normed_ref, bf16[640,256]{1,0:T(8,128)(2,1)S(1)} %collective-permute-done.14.refs_0_, bf16[640,256]{1,0:T(8,128)(2,1)S(1)} %collective-permute-done.15.refs_1_, ...), custom_call_target="tpu_custom_call" | custom-call | flops 1150000000 | bytes 1048576 | tf_op jit(solution)/shard_map/pallas_call | solution.py:21
  55.7 0.1 collective-permute-start.17
  55.8 3.3 %collective-permute-done.20.refs_2_ = bf16[384,256]{1,0:T(8,128)(2,1)S(1)} collective-permute-done((bf16[384,256]{1,0:T(8,128)(2,1)S(1)}, bf16[384,256]{1,0:T(8,128)(2,1)S(1)}, u32[]{:S(2)}, u32[]{:S(2)}) %collective-permute-start.20) | collective-permute-done | bytes 196640 | tf_op jit(solution)/shard_map/ppermute | solution.py:371
  59.1 1.0 %shard_map.91 = (f32[256,256]{1,0:T(8,128)S(1)}, bf16[256,256]{1,0:T(8,128)(2,1)S(1)}) custom-call(s32[15]{0:T(128)S(1)} %dynamic-slice_bitcast_fusion.info, bf16[512,1024]{1,0:T(8,128)(2,1)S(1)} %shard_map.88.normed_ref, bf16[256,256]{1,0:T(8,128)(2,1)S(1)} %collective-permute-done.18.refs_0_, bf16[384,256]{1,0:T(8,128)(2,1)S(1)} %collective-permute-done.19.refs_1_, ...), custom_call_target="tpu_custom_call" | custom-call | flops 575000000 | bytes 1048576 | tf_op jit(solution)/shard_map/pallas_call | solution.py:21
  60.1 0.1 collective-permute-start.21
  60.2 1.3 %collective-permute-done.21.refs_5_ = bf16[256,256]{1,0:T(8,128)(2,1)S(1)} collective-permute-done((bf16[256,256]{1,0:T(8,128)(2,1)S(1)}, bf16[256,256]{1,0:T(8,128)(2,1)S(1)}, u32[]{:S(2)}, u32[]{:S(2)}) %collective-permute-start.21) | collective-permute-done | bytes 131104 | tf_op jit(solution)/shard_map/ppermute | solution.py:248
  61.5 0.0 collective-permute-done.13.refs_1_
  61.5 1.6 %shard_map.92 = bf16[256,2048]{1,0:T(8,128)(2,1)} custom-call(s32[15]{0:T(128)S(1)} %dynamic-slice_bitcast_fusion.info, f32[256,1280]{1,0:T(8,128)S(1)} %get-tuple-element.39.refs_0_, bf16[256,1280]{1,0:T(8,128)(2,1)S(1)} %collective-permute-done.13.refs_1_, f32[256,512]{1,0:T(8,128)S(1)} %get-tuple-element.43.refs_2_, ...), custom_call_target="tpu_custom_call" | custom-call | flops 1150000000 | bytes 1048576 | tf_op jit(solution)/shard_map/pallas_call | solution.py:436
  (35 shorter events, 0.5 us)
Async XLA Ops:
  0.0 3.9 %collective-permute-start = (bf16[2048,128]{1,0:T(8,128)(2,1)}, bf16[2048,128]{1,0:T(8,128)(2,1)S(1)}, u32[]{:S(2)}, u32[]{:S(2)}) collective-permute-start(bf16[2048,128]{1,0:T(8,128)(2,1)} %param.14), channel_id=1, source_target_pairs={{0,1},{1,0},{2,3},{3,2},{4,5},{5,4},{6,7},{7,6},{8,9},{9,8},{10,11... | collective-permute-start | bytes 1572872 | tf_op jit(solution)/shard_map/ppermute | solution.py:248
  0.5 3.1 %copy-start.7 = (f32[64,18,16]{0,2,1:T(8,128)S(1)}, f32[64,18,16]{0,2,1:T(8,128)}, u32[]{:S(2)}) copy-start(f32[64,18,16]{0,2,1:T(8,128)} %param.12) | copy-start | bytes 221188
  0.5 3.1 %copy-start.6 = (bf16[2048,128]{1,0:T(8,128)(2,1)S(1)}, bf16[2048,128]{1,0:T(8,128)(2,1)}, u32[]{:S(2)}) copy-start(bf16[2048,128]{1,0:T(8,128)(2,1)} %param.14) | copy-start | bytes 1572868
  0.5 3.1 %copy-start.8 = (s32[256]{0:T(256)S(1)}, s32[256]{0:T(256)}, u32[]{:S(2)}) copy-start(s32[256]{0:T(256)} %refs_3_.1) | copy-start | bytes 3076
  3.4 7.3 %collective-permute-start.2 = (bf16[512,1024]{1,0:T(8,128)(2,1)}, bf16[512,1024]{1,0:T(8,128)(2,1)S(1)}, u32[]{:S(2)}, u32[]{:S(2)}) collective-permute-start(bf16[512,1024]{1,0:T(8,128)(2,1)} %shard_map.83), channel_id=1, source_target_pairs={{0,1},{1,0},{2,3},{3,2},{4,5},{5,4},{6,7},{7,6},{8,9},{9,8},{10,11... | collective-permute-start | bytes 3145736 | tf_op jit(solution)/shard_map/ppermute | solution.py:248
  4.1 3.8 %copy-start = (bf16[1024,256]{1,0:T(8,128)(2,1)}, bf16[1024,256]{1,0:T(8,128)(2,1)S(1)}, u32[]{:S(2)}) copy-start(bf16[1024,256]{1,0:T(8,128)(2,1)S(1)} %maximum_select_fusion.refs_2_.refs_0_) | copy-start | bytes 1572868
  4.1 10.9 %collective-permute-start.5 = (bf16[640,256]{1,0:T(8,128)(2,1)S(1)}, bf16[640,256]{1,0:T(8,128)(2,1)S(1)}, u32[]{:S(2)}, u32[]{:S(2)}) collective-permute-start(bf16[640,256]{1,0:T(8,128)(2,1)S(1)} %slice_select_fusion), channel_id=1, source_target_pairs={{0,4},{1,5},{4,8},{5,9},{8,12},{9,13},{12,14},{13,15},{14,10},{15,... | collective-permute-start | bytes 983048 | tf_op jit(solution)/shard_map/ppermute | solution.py:352
  7.2 9.4 %collective-permute-start.6 = (bf16[640,256]{1,0:T(8,128)(2,1)S(1)}, bf16[640,256]{1,0:T(8,128)(2,1)S(1)}, u32[]{:S(2)}, u32[]{:S(2)}) collective-permute-start(bf16[640,256]{1,0:T(8,128)(2,1)S(1)} %slice_select_fusion), channel_id=1, source_target_pairs={{4,0},{5,1},{8,4},{9,5},{12,8},{13,9},{14,12},{15,13},{10,14},{11,... | collective-permute-start | bytes 983048 | tf_op jit(solution)/shard_map/ppermute | solution.py:353
  7.9 2.8 %copy-start.2 = (bf16[256,2048]{1,0:T(8,128)(2,1)S(1)}, bf16[256,2048]{1,0:T(8,128)(2,1)}, u32[]{:S(2)}) copy-start(bf16[256,2048]{1,0:T(8,128)(2,1)} %refs_0_.5) | copy-start | bytes 3145732
  7.9 2.8 %copy-start.3 = (bf16[256,2048]{1,0:T(8,128)(2,1)S(1)}, bf16[256,2048]{1,0:T(8,128)(2,1)}, u32[]{:S(2)}) copy-start(bf16[256,2048]{1,0:T(8,128)(2,1)} %refs_1_.3) | copy-start | bytes 3145732
  10.6 12.4 %collective-permute-start.1 = (bf16[272,1024]{1,0:T(8,128)(2,1)}, bf16[272,1024]{1,0:T(8,128)(2,1)S(1)}, u32[]{:S(2)}, u32[]{:S(2)}) collective-permute-start(bf16[272,1024]{1,0:T(8,128)(2,1)} %shard_map.82), channel_id=1, source_target_pairs={{0,1},{1,0},{2,3},{3,2},{4,5},{5,4},{6,7},{7,6},{8,9},{9,8},{10,11... | collective-permute-start | bytes 1671176 | tf_op jit(solution)/shard_map/ppermute | solution.py:248
  11.9 8.5 %copy-start.4 = (bf16[256,2048]{1,0:T(8,128)(2,1)S(1)}, bf16[256,2048]{1,0:T(8,128)(2,1)}, u32[]{:S(2)}) copy-start(bf16[256,2048]{1,0:T(8,128)(2,1)} %q_ref.3) | copy-start | bytes 3145732
  11.9 11.3 %collective-permute-start.3 = (bf16[8,128,128]{2,1,0:T(8,128)(2,1)S(1)}, bf16[8,128,128]{2,1,0:T(8,128)(2,1)S(1)}, u32[]{:S(2)}, u32[]{:S(2)}) collective-permute-start(bf16[8,128,128]{2,1,0:T(8,128)(2,1)S(1)} %get-tuple-element.27), channel_id=1, source_target_pairs={{0,2},{1,3},{2,0},{3,1},{4,6},{5,7},{6,4},{7,5},{8,10},{9,11},{10,... | collective-permute-start | bytes 786440 | tf_op jit(solution)/shard_map/ppermute | solution.py:248
  16.6 11.3 %collective-permute-start.7 = (bf16[640,256]{1,0:T(8,128)(2,1)S(1)}, bf16[640,256]{1,0:T(8,128)(2,1)S(1)}, u32[]{:S(2)}, u32[]{:S(2)}) collective-permute-start(bf16[640,256]{1,0:T(8,128)(2,1)S(1)} %collective-permute-done.5.refs_1_), channel_id=1, source_target_pairs={{0,4},{1,5},{4,8},{5,9},{8,12},{9,13},{12,14},{13,15},{14,10},{15,... | collective-permute-start | bytes 983048 | tf_op jit(solution)/shard_map/ppermute | solution.py:352
  18.1 9.6 %collective-permute-start.8 = (bf16[640,256]{1,0:T(8,128)(2,1)S(1)}, bf16[640,256]{1,0:T(8,128)(2,1)S(1)}, u32[]{:S(2)}, u32[]{:S(2)}) collective-permute-start(bf16[640,256]{1,0:T(8,128)(2,1)S(1)} %collective-permute-done.6.refs_2_), channel_id=1, source_target_pairs={{4,0},{5,1},{8,4},{9,5},{12,8},{13,9},{14,12},{15,13},{10,14},{11,... | collective-permute-start | bytes 983048 | tf_op jit(solution)/shard_map/ppermute | solution.py:353
  18.8 13.4 %collective-permute-start.11 = (bf16[768,256]{1,0:T(8,128)(2,1)S(1)}, bf16[768,256]{1,0:T(8,128)(2,1)S(1)}, u32[]{:S(2)}, u32[]{:S(2)}) collective-permute-start(bf16[768,256]{1,0:T(8,128)(2,1)S(1)} %maximum_select_fusion.2), channel_id=1, source_target_pairs={{0,16},{16,0},{1,17},{17,1},{2,18},{18,2},{3,19},{19,3},{4,20},{20... | collective-permute-start | bytes 1179656 | tf_op jit(solution)/shard_map/ppermute | solution.py:371
  23.3 6.5 %collective-permute-start.4 = (bf16[4,128,128]{2,1,0:T(8,128)(2,1)S(1)}, bf16[4,128,128]{2,1,0:T(8,128)(2,1)S(1)}, u32[]{:S(2)}, u32[]{:S(2)}) collective-permute-start(bf16[4,128,128]{2,1,0:T(8,128)(2,1)S(1)} %fusion.5), channel_id=1, source_target_pairs={{0,4},{1,5},{2,6},{3,7},{4,0},{5,1},{6,2},{7,3},{8,12},{9,13},{10,... | collective-permute-start | bytes 393224 | tf_op jit(solution)/shard_map/ppermute | solution.py:248
  28.0 21.2 %collective-permute-start.12 = (bf16[768,256]{1,0:T(8,128)(2,1)S(1)}, bf16[768,256]{1,0:T(8,128)(2,1)S(1)}, u32[]{:S(2)}, u32[]{:S(2)}) collective-permute-start(bf16[768,256]{1,0:T(8,128)(2,1)S(1)} %maximum_select_fusion.3), channel_id=1, source_target_pairs={{0,16},{16,0},{1,17},{17,1},{2,18},{18,2},{3,19},{19,3},{4,20},{20... | collective-permute-start | bytes 1179656 | tf_op jit(solution)/shard_map/ppermute | solution.py:371
  29.9 10.0 %collective-permute-start.9 = (bf16[4,128,128]{2,1,0:T(8,128)(2,1)S(1)}, bf16[4,128,128]{2,1,0:T(8,128)(2,1)S(1)}, u32[]{:S(2)}, u32[]{:S(2)}) collective-permute-start(bf16[4,128,128]{2,1,0:T(8,128)(2,1)S(1)} %add_convert_fusion), channel_id=1, source_target_pairs={{0,8},{1,9},{2,10},{3,11},{4,12},{5,13},{6,14},{7,15},{8,0},{9,1},... | collective-permute-start | bytes 393224 | tf_op jit(solution)/shard_map/ppermute | solution.py:248
  32.1 12.2 %collective-permute-start.14 = (bf16[640,256]{1,0:T(8,128)(2,1)S(1)}, bf16[640,256]{1,0:T(8,128)(2,1)S(1)}, u32[]{:S(2)}, u32[]{:S(2)}) collective-permute-start(bf16[640,256]{1,0:T(8,128)(2,1)S(1)} %collective-permute-done.7.refs_4_), channel_id=1, source_target_pairs={{0,4},{1,5},{4,8},{5,9},{8,12},{9,13},{12,14},{13,15},{14,10},{15,... | collective-permute-start | bytes 983048 | tf_op jit(solution)/shard_map/ppermute | solution.py:352
  35.2 9.1 %collective-permute-start.15 = (bf16[640,256]{1,0:T(8,128)(2,1)S(1)}, bf16[640,256]{1,0:T(8,128)(2,1)S(1)}, u32[]{:S(2)}, u32[]{:S(2)}) collective-permute-start(bf16[640,256]{1,0:T(8,128)(2,1)S(1)} %collective-permute-done.8.refs_5_), channel_id=1, source_target_pairs={{4,0},{5,1},{8,4},{9,5},{12,8},{13,9},{14,12},{15,13},{10,14},{11,... | collective-permute-start | bytes 983048 | tf_op jit(solution)/shard_map/ppermute | solution.py:353
  39.9 7.4 %collective-permute-start.10 = (bf16[2,4,128,128]{3,2,1,0:T(8,128)(2,1)S(1)}, bf16[2,4,128,128]{3,2,1,0:T(8,128)(2,1)S(1)}, u32[]{:S(2)}, u32[]{:S(2)}) collective-permute-start(bf16[2,4,128,128]{3,2,1,0:T(8,128)(2,1)S(1)} %pad_maximum_fusion), channel_id=1, source_target_pairs={{0,2},{1,3},{2,0},{3,1},{4,6},{5,7},{6,4},{7,5},{8,10},{9,11},{10,... | collective-permute-start | bytes 786440 | tf_op jit(solution)/shard_map/ppermute | solution.py:248
  44.4 3.0 %copy-start.5 = (f32[2048]{0:T(1024)S(1)}, f32[2048]{0:T(1024)}, u32[]{:S(2)}) copy-start(f32[2048]{0:T(1024)} %param.13) | copy-start | bytes 24580
  44.5 9.9 %collective-permute-start.16 = (bf16[768,256]{1,0:T(8,128)(2,1)S(1)}, bf16[768,256]{1,0:T(8,128)(2,1)S(1)}, u32[]{:S(2)}, u32[]{:S(2)}) collective-permute-start(bf16[768,256]{1,0:T(8,128)(2,1)S(1)} %maximum_select_fusion.4), channel_id=1, source_target_pairs={{0,16},{16,0},{1,17},{17,1},{2,18},{18,2},{3,19},{19,3},{4,20},{20... | collective-permute-start | bytes 1179656 | tf_op jit(solution)/shard_map/ppermute | solution.py:371
  45.1 6.6 %collective-permute-start.18 = (bf16[256,256]{1,0:T(8,128)(2,1)S(1)}, bf16[256,256]{1,0:T(8,128)(2,1)S(1)}, u32[]{:S(2)}, u32[]{:S(2)}) collective-permute-start(bf16[256,256]{1,0:T(8,128)(2,1)S(1)} %slice.109), channel_id=1, source_target_pairs={{0,4},{1,5},{4,8},{5,9},{8,12},{9,13},{12,14},{13,15},{14,10},{15,... | collective-permute-start | bytes 393224 | tf_op jit(solution)/shard_map/ppermute | solution.py:352
  47.0 5.7 %collective-permute-start.19 = (bf16[384,256]{1,0:T(8,128)(2,1)S(1)}, bf16[384,256]{1,0:T(8,128)(2,1)S(1)}, u32[]{:S(2)}, u32[]{:S(2)}) collective-permute-start(bf16[384,256]{1,0:T(8,128)(2,1)S(1)} %slice.110), channel_id=1, source_target_pairs={{4,0},{5,1},{8,4},{9,5},{12,8},{13,9},{14,12},{15,13},{10,14},{11,... | collective-permute-start | bytes 589832 | tf_op jit(solution)/shard_map/ppermute | solution.py:353
  47.4 1.8 %copy-start.1 = (bf16[1024,256]{1,0:T(8,128)(2,1)S(1)}, bf16[1024,256]{1,0:T(8,128)(2,1)}, u32[]{:S(2)}) copy-start(bf16[1024,256]{1,0:T(8,128)(2,1)} %copy-done) | copy-start | bytes 1572868
  51.5 10.0 %collective-permute-start.13 = (bf16[256,1280]{1,0:T(8,128)(2,1)S(1)}, bf16[256,1280]{1,0:T(8,128)(2,1)S(1)}, u32[]{:S(2)}, u32[]{:S(2)}) collective-permute-start(bf16[256,1280]{1,0:T(8,128)(2,1)S(1)} %get-tuple-element.40), channel_id=1, source_target_pairs={{0,1},{1,0},{2,3},{3,2},{4,5},{5,4},{6,7},{7,6},{8,9},{9,8},{10,11... | collective-permute-start | bytes 1966088 | tf_op jit(solution)/shard_map/ppermute | solution.py:248
  52.8 6.3 %collective-permute-start.20 = (bf16[384,256]{1,0:T(8,128)(2,1)S(1)}, bf16[384,256]{1,0:T(8,128)(2,1)S(1)}, u32[]{:S(2)}, u32[]{:S(2)}) collective-permute-start(bf16[384,256]{1,0:T(8,128)(2,1)S(1)} %fusion), channel_id=1, source_target_pairs={{0,16},{16,0},{1,17},{17,1},{2,18},{18,2},{3,19},{19,3},{4,20},{20... | collective-permute-start | bytes 589832 | tf_op jit(solution)/shard_map/ppermute | solution.py:371
  55.7 5.8 %collective-permute-start.17 = (bf16[256,512]{1,0:T(8,128)(2,1)S(1)}, bf16[256,512]{1,0:T(8,128)(2,1)S(1)}, u32[]{:S(2)}, u32[]{:S(2)}) collective-permute-start(bf16[256,512]{1,0:T(8,128)(2,1)S(1)} %get-tuple-element.44), channel_id=1, source_target_pairs={{0,1},{1,0},{2,3},{3,2},{4,5},{5,4},{6,7},{7,6},{8,9},{9,8},{10,11... | collective-permute-start | bytes 786440 | tf_op jit(solution)/shard_map/ppermute | solution.py:248
  60.1 1.4 %collective-permute-start.21 = (bf16[256,256]{1,0:T(8,128)(2,1)S(1)}, bf16[256,256]{1,0:T(8,128)(2,1)S(1)}, u32[]{:S(2)}, u32[]{:S(2)}) collective-permute-start(bf16[256,256]{1,0:T(8,128)(2,1)S(1)} %get-tuple-element.48), channel_id=1, source_target_pairs={{0,1},{1,0},{2,3},{3,2},{4,5},{5,4},{6,7},{7,6},{8,9},{9,8},{10,11... | collective-permute-start | bytes 393224 | tf_op jit(solution)/shard_map/ppermute | solution.py:248

commit v5 on v4

--- a/solution.py
+++ b/solution.py
@@ -342,6 +342,8 @@
         def ring_after(r):
             if r == 3:
                 return reached[2:3] + crossed[:1]
+            if r == 4:
+                return crossed[1:2]
             return []
 
         for r in range(1, rounds + 1):
@@ -392,7 +394,7 @@
     side_shape = jax.ShapeDtypeStruct((half, stretch), jnp.float32)
     acc_own = call(
         functools.partial(local_kernel, True), side_shape, [SM] + [VM] * 4, us(2.1), 1 << 20,
-        info, tie(lam_own, reached[0]), keys, values, queries,
+        info, tie(lam_own, reached[1]), keys, values, queries,
     )
     acc_got = call(
         functools.partial(local_kernel, False), side_shape, [SM] + [VM] * 3, us(2.1), 1 << 20,

time: 63.3 us -> 63.3 us (level)
  transfers between devices with their start and end apart: 22 -> 22, of which waited for: 10 -> 10; matrix products, arithmetic and copies ran while one was open for 3% -> 4% of each run, Pallas kernels for 31% -> 31%
where the time goes in v5:
time: 63.3 us; the launch traced here: 63.1 us
  starting transfers between devices  23.9 us (38%)
  Pallas kernels  21.1 us (33%)
  waiting for transfers between devices  15.4 us (24%)
  local copies, waits for them, and re-layouts  1.04 us (2%)
  other arithmetic  0.75 us (1%)
    pallas_call x8, Pallas kernels, call(): pl.pallas_call(kernel, out_shape=out_shape, in_specs=in_specs, out_specs=...  14 us
    ppermute x4, starting transfers between devices, body(): right = lax.ppermute(right, 'seq', clockwise)  9.46 us
    ppermute x10, starting transfers between devices, swap(): return lax.ppermute(block, 'seq', route)  8.33 us
    ppermute x4, waiting for transfers between devices, body(): left = lax.ppermute(left, 'seq', counter)  8.02 us
    pallas_call x2, Pallas kernels, split(): pl.pallas_call(functools.partial(split_kernel, len(arrays)), out_shape=bf...  5.48 us
    ppermute x4, starting transfers between devices, body(): crossed.append(lax.ppermute(wanted, 'grp', [(0, 1), (1, 0)]))  5.44 us
    ppermute x4, waiting for transfers between devices, body(): crossed.append(lax.ppermute(wanted, 'grp', [(0, 1), (1, 0)]))  3.38 us
    ppermute x10, waiting for transfers between devices, swap(): return lax.ppermute(block, 'seq', route)  2.6 us
  transfers between devices with their start and end apart: 22, of which 10 were waited for; matrix products, arithmetic and copies ran while one was open for 4% of the time, Pallas kernels for 31%

profile of v5, /device:TPU:0, one launch (start us, length us, event | category | flops | bytes accessed | tf_op | source)
XLA Modules:
  0.0 63.1 jit_solution(1163888128089545481)
XLA Ops:
  0.0 0.5 collective-permute-start
  0.5 2.9 %shard_map.83 = bf16[512,1024]{1,0:T(8,128)(2,1)} custom-call(bf16[256,2048]{1,0:T(8,128)(2,1)} %refs_0_.5, bf16[256,2048]{1,0:T(8,128)(2,1)} %refs_1_.3, s32[1,256]{1,0:T(1,128)} %bitcast.25, s32[256]{0:T(256)} %refs_3_.1), custom_call_target="tpu_custom_call" | custom-call | flops 2300000000 | bytes 1048576 | tf_op jit(solution)/shard_map/pallas_call | solution.py:255
  3.4 0.1 collective-permute-start.2
  3.6 0.2 fusion.3.lam_ref.lam0_ref
  3.9 0.2 maximum_select_fusion.refs_2_.refs_0_
  4.1 0.0 copy-start.2
  4.1 0.0 copy-start.3
  4.2 3.1 %collective-permute-start.5 = (bf16[640,256]{1,0:T(8,128)(2,1)S(1)}, bf16[640,256]{1,0:T(8,128)(2,1)S(1)}, u32[]{:S(2)}, u32[]{:S(2)}) collective-permute-start(bf16[640,256]{1,0:T(8,128)(2,1)S(1)} %slice_select_fusion), channel_id=1, source_target_pairs={{0,4},{1,5},{4,8},{5,9},{8,12},{9,13},{12,14},{13,15},{14,10},{15,... | collective-permute-start | bytes 983048 | tf_op jit(solution)/shard_map/ppermute | solution.py:354
  7.2 0.0 collective-permute-start.6
  7.2 2.5 %shard_map.82 = bf16[272,1024]{1,0:T(8,128)(2,1)} custom-call(bf16[256,2048]{1,0:T(8,128)(2,1)} %q_ref.3, s32[1,256]{1,0:T(1,128)} %bitcast.26, bf16[1024,256]{1,0:T(8,128)(2,1)} %copy-done), custom_call_target="tpu_custom_call" | custom-call | flops 2300000000 | bytes 1048576 | tf_op jit(solution)/shard_map/pallas_call | solution.py:255
  9.8 0.1 collective-permute-start.1
  9.9 0.7 %dynamic-slice_bitcast_fusion.info = s32[15]{0:T(128)S(1)} fusion(s32[2,16,15]{2,1,0:T(8,128)} %constant.36.clone, s32[]{:T(128)S(6)} %select_n.85, s32[]{:T(128)S(6)} %select_n.86), kind=kLoop, calls=%fused_computation.27 | loop fusion | bytes 128 | tf_op jit(solution)/shard_map/reshape | solution.py:244
  10.6 0.0 collective-permute-done.2.got_ref.refs_0_
  10.6 1.0 %shard_map.84 = (f32[8,128,128]{2,1,0:T(8,128)S(1)}, bf16[8,128,128]{2,1,0:T(8,128)(2,1)S(1)}, bf16[8,128,128]{2,1,0:T(8,128)(2,1)S(1)}) custom-call(s32[15]{0:T(128)S(1)} %dynamic-slice_bitcast_fusion.info, bf16[256,2048]{1,0:T(8,128)(2,1)S(1)} %copy-done.2, bf16[256,2048]{1,0:T(8,128)(2,1)S(1)} %copy-done.3, ...), custom_call_target="tpu_custom_call" | custom-call | flops 1150000000 | bytes 1048576 | tf_op jit(solution)/shard_map/pallas_call | solution.py:21
  11.6 0.0 copy-start.4
  11.6 2.0 %collective-permute-start.3 = (bf16[8,128,128]{2,1,0:T(8,128)(2,1)S(1)}, bf16[8,128,128]{2,1,0:T(8,128)(2,1)S(1)}, u32[]{:S(2)}, u32[]{:S(2)}) collective-permute-start(bf16[8,128,128]{2,1,0:T(8,128)(2,1)S(1)} %get-tuple-element.28), channel_id=1, source_target_pairs={{0,2},{1,3},{2,0},{3,1},{4,6},{5,7},{6,4},{7,5},{8,10},{9,11},{10,... | collective-permute-start | bytes 786440 | tf_op jit(solution)/shard_map/ppermute | solution.py:248
  13.7 1.4 %collective-permute-done.5.refs_1_ = bf16[640,256]{1,0:T(8,128)(2,1)S(1)} collective-permute-done((bf16[640,256]{1,0:T(8,128)(2,1)S(1)}, bf16[640,256]{1,0:T(8,128)(2,1)S(1)}, u32[]{:S(2)}, u32[]{:S(2)}) %collective-permute-start.5) | collective-permute-done | bytes 327712 | tf_op jit(solution)/shard_map/ppermute | solution.py:354
  15.1 1.5 %collective-permute-done.6.refs_2_ = bf16[640,256]{1,0:T(8,128)(2,1)S(1)} collective-permute-done((bf16[640,256]{1,0:T(8,128)(2,1)S(1)}, bf16[640,256]{1,0:T(8,128)(2,1)S(1)}, u32[]{:S(2)}, u32[]{:S(2)}) %collective-permute-start.6) | collective-permute-done | bytes 327712 | tf_op jit(solution)/shard_map/ppermute | solution.py:355
  16.6 1.6 %collective-permute-start.7 = (bf16[640,256]{1,0:T(8,128)(2,1)S(1)}, bf16[640,256]{1,0:T(8,128)(2,1)S(1)}, u32[]{:S(2)}, u32[]{:S(2)}) collective-permute-start(bf16[640,256]{1,0:T(8,128)(2,1)S(1)} %collective-permute-done.5.refs_1_), channel_id=1, source_target_pairs={{0,4},{1,5},{4,8},{5,9},{8,12},{9,13},{12,14},{13,15},{14,10},{15,... | collective-permute-start | bytes 983048 | tf_op jit(solution)/shard_map/ppermute | solution.py:354
  18.2 0.5 collective-permute-start.8
  18.6 0.1 fusion.18
  18.7 0.1 maximum_select_fusion.2
  18.8 1.6 %collective-permute-start.11 = (bf16[768,256]{1,0:T(8,128)(2,1)S(1)}, bf16[768,256]{1,0:T(8,128)(2,1)S(1)}, u32[]{:S(2)}, u32[]{:S(2)}) collective-permute-start(bf16[768,256]{1,0:T(8,128)(2,1)S(1)} %maximum_select_fusion.2), channel_id=1, source_target_pairs={{0,16},{16,0},{1,17},{17,1},{2,18},{18,2},{3,19},{19,3},{4,20},{20... | collective-permute-start | bytes 1179656 | tf_op jit(solution)/shard_map/ppermute | solution.py:373
  20.4 0.2 fusion.1.lam_ref.lam1_ref
  20.6 0.3 collective-permute-done.3.refs_1_
  21.0 1.6 %collective-permute-start.4 = (bf16[4,128,128]{2,1,0:T(8,128)(2,1)S(1)}, bf16[4,128,128]{2,1,0:T(8,128)(2,1)S(1)}, u32[]{:S(2)}, u32[]{:S(2)}) collective-permute-start(bf16[4,128,128]{2,1,0:T(8,128)(2,1)S(1)} %fusion.5), channel_id=1, source_target_pairs={{0,4},{1,5},{2,6},{3,7},{4,0},{5,1},{6,2},{7,3},{8,12},{9,13},{10,... | collective-permute-start | bytes 393224 | tf_op jit(solution)/shard_map/ppermute | solution.py:248
  22.6 2.6 %shard_map.85.base0_ref = f32[1024,256]{1,0:T(8,128)S(1)} custom-call(s32[15]{0:T(128)S(1)} %dynamic-slice_bitcast_fusion.info, f32[8,18,256]{2,1,0:T(8,128)S(1)} %fusion.3.lam_ref.lam0_ref, bf16[256,2048]{1,0:T(8,128)(2,1)S(1)} %copy-done.2, bf16[256,2048]{1,0:T(8,128)(2,1)S(1)} %copy-done.3, bf16[256,2048]{1,0:T(8,128)(2,1)S(1)} %copy-done.4), custom_call_target="tpu_custom_call" | custom-call | flops 2415000064 | bytes 1048576 | tf_op jit(solution)/shard_map/pallas_call | solution.py:21
  25.2 2.6 %collective-permute-done.8.refs_5_ = bf16[640,256]{1,0:T(8,128)(2,1)S(1)} collective-permute-done((bf16[640,256]{1,0:T(8,128)(2,1)S(1)}, bf16[640,256]{1,0:T(8,128)(2,1)S(1)}, u32[]{:S(2)}, u32[]{:S(2)}) %collective-permute-start.8) | collective-permute-done | bytes 327712 | tf_op jit(solution)/shard_map/ppermute | solution.py:355
  27.8 0.0 collective-permute-done.7.refs_4_
  27.9 0.1 maximum_select_fusion.3
  28.0 1.7 %collective-permute-start.12 = (bf16[768,256]{1,0:T(8,128)(2,1)S(1)}, bf16[768,256]{1,0:T(8,128)(2,1)S(1)}, u32[]{:S(2)}, u32[]{:S(2)}) collective-permute-start(bf16[768,256]{1,0:T(8,128)(2,1)S(1)} %maximum_select_fusion.3), channel_id=1, source_target_pairs={{0,16},{16,0},{1,17},{17,1},{2,18},{18,2},{3,19},{19,3},{4,20},{20... | collective-permute-start | bytes 1179656 | tf_op jit(solution)/shard_map/ppermute | solution.py:373
  29.7 2.6 %collective-permute-start.9 = (bf16[4,128,128]{2,1,0:T(8,128)(2,1)S(1)}, bf16[4,128,128]{2,1,0:T(8,128)(2,1)S(1)}, u32[]{:S(2)}, u32[]{:S(2)}) collective-permute-start(bf16[4,128,128]{2,1,0:T(8,128)(2,1)S(1)} %add_convert_fusion), channel_id=1, source_target_pairs={{0,8},{1,9},{2,10},{3,11},{4,12},{5,13},{6,14},{7,15},{8,0},{9,1},... | collective-permute-start | bytes 393224 | tf_op jit(solution)/shard_map/ppermute | solution.py:248
  32.3 2.9 %collective-permute-start.14 = (bf16[640,256]{1,0:T(8,128)(2,1)S(1)}, bf16[640,256]{1,0:T(8,128)(2,1)S(1)}, u32[]{:S(2)}, u32[]{:S(2)}) collective-permute-start(bf16[640,256]{1,0:T(8,128)(2,1)S(1)} %collective-permute-done.7.refs_4_), channel_id=1, source_target_pairs={{0,4},{1,5},{4,8},{5,9},{8,12},{9,13},{12,14},{13,15},{14,10},{15,... | collective-permute-start | bytes 983048 | tf_op jit(solution)/shard_map/ppermute | solution.py:354
  35.2 0.0 collective-permute-start.15
  35.2 2.6 %shard_map.86.base1_ref = f32[1024,256]{1,0:T(8,128)S(1)} custom-call(s32[15]{0:T(128)S(1)} %dynamic-slice_bitcast_fusion.info, f32[8,18,256]{2,1,0:T(8,128)S(1)} %fusion.1.lam_ref.lam1_ref, bf16[512,1024]{1,0:T(8,128)(2,1)S(1)} %collective-permute-done.2.got_ref.refs_0_, bf16[272,1024]{1,0:T(8,128)(2,1)S(1)} %collective-permute-done.1.refs_1_.got_ref), custom_call_target="tpu_custom_call" | custom-call | flops 2415000064 | bytes 1048576 | tf_op jit(solution)/shard_map/pallas_call | solution.py:21
  37.8 1.3 %shard_map.87.base_ref = f32[1024,512]{1,0:T(8,128)S(1)} custom-call(s32[15]{0:T(128)S(1)} %dynamic-slice_bitcast_fusion.info, bf16[256,2048]{1,0:T(8,128)(2,1)S(1)} %copy-done.4, bf16[272,1024]{1,0:T(8,128)(2,1)S(1)} %collective-permute-done.1.refs_1_.got_ref, f32[8,18,256]{2,1,0:T(8,128)S(1)} %fusion.3.lam_ref.lam0_ref, ...), custom_call_target="tpu_custom_call" | custom-call | flops 1840000000 | bytes 1048576 | tf_op jit(solution)/shard_map/pallas_call | solution.py:21
  39.1 0.7 %collective-permute-done.9 = bf16[4,128,128]{2,1,0:T(8,128)(2,1)S(1)} collective-permute-done((bf16[4,128,128]{2,1,0:T(8,128)(2,1)S(1)}, bf16[4,128,128]{2,1,0:T(8,128)(2,1)S(1)}, u32[]{:S(2)}, u32[]{:S(2)}) %collective-permute-start.9) | collective-permute-done | bytes 131104 | tf_op jit(solution)/shard_map/ppermute | solution.py:248
  39.8 1.3 %collective-permute-start.10 = (bf16[2,4,128,128]{3,2,1,0:T(8,128)(2,1)S(1)}, bf16[2,4,128,128]{3,2,1,0:T(8,128)(2,1)S(1)}, u32[]{:S(2)}, u32[]{:S(2)}) collective-permute-start(bf16[2,4,128,128]{3,2,1,0:T(8,128)(2,1)S(1)} %pad_maximum_fusion), channel_id=1, source_target_pairs={{0,2},{1,3},{2,0},{3,1},{4,6},{5,7},{6,4},{7,5},{8,10},{9,11},{10,... | collective-permute-start | bytes 786440 | tf_op jit(solution)/shard_map/ppermute | solution.py:248
  41.1 3.0 %collective-permute-done.15.refs_1_ = bf16[640,256]{1,0:T(8,128)(2,1)S(1)} collective-permute-done((bf16[640,256]{1,0:T(8,128)(2,1)S(1)}, bf16[640,256]{1,0:T(8,128)(2,1)S(1)}, u32[]{:S(2)}, u32[]{:S(2)}) %collective-permute-start.15) | collective-permute-done | bytes 327712 | tf_op jit(solution)/shard_map/ppermute | solution.py:355
  44.2 0.0 collective-permute-done.14.refs_0_
  44.2 0.0 copy-start.5
  44.2 0.1 maximum_select_fusion.4
  44.3 0.5 collective-permute-start.16
  44.8 0.0 collective-permute-done.12.refs_6_
  44.8 1.9 %collective-permute-start.18 = (bf16[256,256]{1,0:T(8,128)(2,1)S(1)}, bf16[256,256]{1,0:T(8,128)(2,1)S(1)}, u32[]{:S(2)}, u32[]{:S(2)}) collective-permute-start(bf16[256,256]{1,0:T(8,128)(2,1)S(1)} %slice.109), channel_id=1, source_target_pairs={{0,4},{1,5},{4,8},{5,9},{8,12},{9,13},{12,14},{13,15},{14,10},{15,... | collective-permute-start | bytes 393224 | tf_op jit(solution)/shard_map/ppermute | solution.py:354
  46.7 0.2 collective-permute-start.19
  47.0 0.3 collective-permute-done.10
  47.3 0.1 maximum_select_fusion.1
  47.4 1.7 %shard_map.88.normed_ref = bf16[512,1024]{1,0:T(8,128)(2,1)S(1)} custom-call(s32[15]{0:T(128)S(1)} %dynamic-slice_bitcast_fusion.info, bf16[256,2048]{1,0:T(8,128)(2,1)S(1)} %copy-done.4, bf16[272,1024]{1,0:T(8,128)(2,1)S(1)} %collective-permute-done.1.refs_1_.got_ref, f32[8,18,256]{2,1,0:T(8,128)S(1)} %fusion.3.lam_ref.lam0_ref, ...), custom_call_target="tpu_custom_call" | custom-call | flops 2300000000 | bytes 1048576 | tf_op jit(solution)/shard_map/pallas_call | solution.py:21
  49.2 2.3 %shard_map.89 = (f32[256,1280]{1,0:T(8,128)S(1)}, bf16[256,1280]{1,0:T(8,128)(2,1)S(1)}) custom-call(s32[15]{0:T(128)S(1)} %dynamic-slice_bitcast_fusion.info, bf16[512,1024]{1,0:T(8,128)(2,1)S(1)} %shard_map.88.normed_ref, bf16[1024,256]{1,0:T(8,128)(2,1)S(1)} %copy-done.1, bf16[640,256]{1,0:T(8,128)(2,1)S(1)} %collective-permute-done.5.refs_1_, ...), custom_call_target="tpu_custom_call" | custom-call | flops 2875000064 | bytes 1048576 | tf_op jit(solution)/shard_map/pallas_call | solution.py:21
  51.5 0.1 collective-permute-start.13
  51.6 0.0 collective-permute-done.18.refs_0_
  51.6 0.9 %collective-permute-done.19.refs_1_ = bf16[384,256]{1,0:T(8,128)(2,1)S(1)} collective-permute-done((bf16[384,256]{1,0:T(8,128)(2,1)S(1)}, bf16[384,256]{1,0:T(8,128)(2,1)S(1)}, u32[]{:S(2)}, u32[]{:S(2)}) %collective-permute-start.19) | collective-permute-done | bytes 196640 | tf_op jit(solution)/shard_map/ppermute | solution.py:355
  52.5 0.1 fusion
  52.5 1.7 %collective-permute-start.20 = (bf16[384,256]{1,0:T(8,128)(2,1)S(1)}, bf16[384,256]{1,0:T(8,128)(2,1)S(1)}, u32[]{:S(2)}, u32[]{:S(2)}) collective-permute-start(bf16[384,256]{1,0:T(8,128)(2,1)S(1)} %fusion), channel_id=1, source_target_pairs={{0,16},{16,0},{1,17},{17,1},{2,18},{18,2},{3,19},{19,3},{4,20},{20... | collective-permute-start | bytes 589832 | tf_op jit(solution)/shard_map/ppermute | solution.py:373
  54.2 1.4 %shard_map.90 = (f32[256,512]{1,0:T(8,128)S(1)}, bf16[256,512]{1,0:T(8,128)(2,1)S(1)}) custom-call(s32[15]{0:T(128)S(1)} %dynamic-slice_bitcast_fusion.info, bf16[512,1024]{1,0:T(8,128)(2,1)S(1)} %shard_map.88.normed_ref, bf16[640,256]{1,0:T(8,128)(2,1)S(1)} %collective-permute-done.14.refs_0_, bf16[640,256]{1,0:T(8,128)(2,1)S(1)} %collective-permute-done.15.refs_1_, ...), custom_call_target="tpu_custom_call" | custom-call | flops 1150000000 | bytes 1048576 | tf_op jit(solution)/shard_map/pallas_call | solution.py:21
  55.6 0.1 collective-permute-start.17
  55.7 3.4 %collective-permute-done.20.refs_2_ = bf16[384,256]{1,0:T(8,128)(2,1)S(1)} collective-permute-done((bf16[384,256]{1,0:T(8,128)(2,1)S(1)}, bf16[384,256]{1,0:T(8,128)(2,1)S(1)}, u32[]{:S(2)}, u32[]{:S(2)}) %collective-permute-start.20) | collective-permute-done | bytes 196640 | tf_op jit(solution)/shard_map/ppermute | solution.py:373
  59.0 1.0 %shard_map.91 = (f32[256,256]{1,0:T(8,128)S(1)}, bf16[256,256]{1,0:T(8,128)(2,1)S(1)}) custom-call(s32[15]{0:T(128)S(1)} %dynamic-slice_bitcast_fusion.info, bf16[512,1024]{1,0:T(8,128)(2,1)S(1)} %shard_map.88.normed_ref, bf16[256,256]{1,0:T(8,128)(2,1)S(1)} %collective-permute-done.18.refs_0_, bf16[384,256]{1,0:T(8,128)(2,1)S(1)} %collective-permute-done.19.refs_1_, ...), custom_call_target="tpu_custom_call" | custom-call | flops 575000000 | bytes 1048576 | tf_op jit(solution)/shard_map/pallas_call | solution.py:21
  60.1 0.1 collective-permute-start.21
  60.2 1.3 %collective-permute-done.21.refs_5_ = bf16[256,256]{1,0:T(8,128)(2,1)S(1)} collective-permute-done((bf16[256,256]{1,0:T(8,128)(2,1)S(1)}, bf16[256,256]{1,0:T(8,128)(2,1)S(1)}, u32[]{:S(2)}, u32[]{:S(2)}) %collective-permute-start.21) | collective-permute-done | bytes 131104 | tf_op jit(solution)/shard_map/ppermute | solution.py:248
  61.5 0.0 collective-permute-done.17.refs_3_
  61.5 0.0 collective-permute-done.13.refs_1_
  61.5 1.6 %shard_map.92 = bf16[256,2048]{1,0:T(8,128)(2,1)} custom-call(s32[15]{0:T(128)S(1)} %dynamic-slice_bitcast_fusion.info, f32[256,1280]{1,0:T(8,128)S(1)} %get-tuple-element.39.refs_0_, bf16[256,1280]{1,0:T(8,128)(2,1)S(1)} %collective-permute-done.13.refs_1_, f32[256,512]{1,0:T(8,128)S(1)} %get-tuple-element.43.refs_2_, ...), custom_call_target="tpu_custom_call" | custom-call | flops 1150000000 | bytes 1048576 | tf_op jit(solution)/shard_map/pallas_call | solution.py:438
  (35 shorter events, 0.5 us)
Async XLA Ops:
  0.0 3.9 %collective-permute-start = (bf16[2048,128]{1,0:T(8,128)(2,1)}, bf16[2048,128]{1,0:T(8,128)(2,1)S(1)}, u32[]{:S(2)}, u32[]{:S(2)}) collective-permute-start(bf16[2048,128]{1,0:T(8,128)(2,1)} %param.14), channel_id=1, source_target_pairs={{0,1},{1,0},{2,3},{3,2},{4,5},{5,4},{6,7},{7,6},{8,9},{9,8},{10,11... | collective-permute-start | bytes 1572872 | tf_op jit(solution)/shard_map/ppermute | solution.py:248
  0.5 3.1 %copy-start.7 = (f32[64,18,16]{0,2,1:T(8,128)S(1)}, f32[64,18,16]{0,2,1:T(8,128)}, u32[]{:S(2)}) copy-start(f32[64,18,16]{0,2,1:T(8,128)} %param.12) | copy-start | bytes 221188
  0.5 3.1 %copy-start.6 = (bf16[2048,128]{1,0:T(8,128)(2,1)S(1)}, bf16[2048,128]{1,0:T(8,128)(2,1)}, u32[]{:S(2)}) copy-start(bf16[2048,128]{1,0:T(8,128)(2,1)} %param.14) | copy-start | bytes 1572868
  0.5 3.1 %copy-start.8 = (s32[256]{0:T(256)S(1)}, s32[256]{0:T(256)}, u32[]{:S(2)}) copy-start(s32[256]{0:T(256)} %refs_3_.1) | copy-start | bytes 3076
  3.4 7.2 %collective-permute-start.2 = (bf16[512,1024]{1,0:T(8,128)(2,1)}, bf16[512,1024]{1,0:T(8,128)(2,1)S(1)}, u32[]{:S(2)}, u32[]{:S(2)}) collective-permute-start(bf16[512,1024]{1,0:T(8,128)(2,1)} %shard_map.83), channel_id=1, source_target_pairs={{0,1},{1,0},{2,3},{3,2},{4,5},{5,4},{6,7},{7,6},{8,9},{9,8},{10,11... | collective-permute-start | bytes 3145736 | tf_op jit(solution)/shard_map/ppermute | solution.py:248
  4.1 3.2 %copy-start = (bf16[1024,256]{1,0:T(8,128)(2,1)}, bf16[1024,256]{1,0:T(8,128)(2,1)S(1)}, u32[]{:S(2)}) copy-start(bf16[1024,256]{1,0:T(8,128)(2,1)S(1)} %maximum_select_fusion.refs_2_.refs_0_) | copy-start | bytes 1572868
  4.1 6.4 %copy-start.2 = (bf16[256,2048]{1,0:T(8,128)(2,1)S(1)}, bf16[256,2048]{1,0:T(8,128)(2,1)}, u32[]{:S(2)}) copy-start(bf16[256,2048]{1,0:T(8,128)(2,1)} %refs_0_.5) | copy-start | bytes 3145732
  4.1 6.4 %copy-start.3 = (bf16[256,2048]{1,0:T(8,128)(2,1)S(1)}, bf16[256,2048]{1,0:T(8,128)(2,1)}, u32[]{:S(2)}) copy-start(bf16[256,2048]{1,0:T(8,128)(2,1)} %refs_1_.3) | copy-start | bytes 3145732
  4.2 10.9 %collective-permute-start.5 = (bf16[640,256]{1,0:T(8,128)(2,1)S(1)}, bf16[640,256]{1,0:T(8,128)(2,1)S(1)}, u32[]{:S(2)}, u32[]{:S(2)}) collective-permute-start(bf16[640,256]{1,0:T(8,128)(2,1)S(1)} %slice_select_fusion), channel_id=1, source_target_pairs={{0,4},{1,5},{4,8},{5,9},{8,12},{9,13},{12,14},{13,15},{14,10},{15,... | collective-permute-start | bytes 983048 | tf_op jit(solution)/shard_map/ppermute | solution.py:354
  7.2 9.4 %collective-permute-start.6 = (bf16[640,256]{1,0:T(8,128)(2,1)S(1)}, bf16[640,256]{1,0:T(8,128)(2,1)S(1)}, u32[]{:S(2)}, u32[]{:S(2)}) collective-permute-start(bf16[640,256]{1,0:T(8,128)(2,1)S(1)} %slice_select_fusion), channel_id=1, source_target_pairs={{4,0},{5,1},{8,4},{9,5},{12,8},{13,9},{14,12},{15,13},{10,14},{11,... | collective-permute-start | bytes 983048 | tf_op jit(solution)/shard_map/ppermute | solution.py:355
  9.8 10.6 %collective-permute-start.1 = (bf16[272,1024]{1,0:T(8,128)(2,1)}, bf16[272,1024]{1,0:T(8,128)(2,1)S(1)}, u32[]{:S(2)}, u32[]{:S(2)}) collective-permute-start(bf16[272,1024]{1,0:T(8,128)(2,1)} %shard_map.82), channel_id=1, source_target_pairs={{0,1},{1,0},{2,3},{3,2},{4,5},{5,4},{6,7},{7,6},{8,9},{9,8},{10,11... | collective-permute-start | bytes 1671176 | tf_op jit(solution)/shard_map/ppermute | solution.py:248
  11.6 11.0 %copy-start.4 = (bf16[256,2048]{1,0:T(8,128)(2,1)S(1)}, bf16[256,2048]{1,0:T(8,128)(2,1)}, u32[]{:S(2)}) copy-start(bf16[256,2048]{1,0:T(8,128)(2,1)} %q_ref.3) | copy-start | bytes 3145732
  11.6 9.2 %collective-permute-start.3 = (bf16[8,128,128]{2,1,0:T(8,128)(2,1)S(1)}, bf16[8,128,128]{2,1,0:T(8,128)(2,1)S(1)}, u32[]{:S(2)}, u32[]{:S(2)}) collective-permute-start(bf16[8,128,128]{2,1,0:T(8,128)(2,1)S(1)} %get-tuple-element.28), channel_id=1, source_target_pairs={{0,2},{1,3},{2,0},{3,1},{4,6},{5,7},{6,4},{7,5},{8,10},{9,11},{10,... | collective-permute-start | bytes 786440 | tf_op jit(solution)/shard_map/ppermute | solution.py:248
  16.6 11.2 %collective-permute-start.7 = (bf16[640,256]{1,0:T(8,128)(2,1)S(1)}, bf16[640,256]{1,0:T(8,128)(2,1)S(1)}, u32[]{:S(2)}, u32[]{:S(2)}) collective-permute-start(bf16[640,256]{1,0:T(8,128)(2,1)S(1)} %collective-permute-done.5.refs_1_), channel_id=1, source_target_pairs={{0,4},{1,5},{4,8},{5,9},{8,12},{9,13},{12,14},{13,15},{14,10},{15,... | collective-permute-start | bytes 983048 | tf_op jit(solution)/shard_map/ppermute | solution.py:354
  18.2 9.6 %collective-permute-start.8 = (bf16[640,256]{1,0:T(8,128)(2,1)S(1)}, bf16[640,256]{1,0:T(8,128)(2,1)S(1)}, u32[]{:S(2)}, u32[]{:S(2)}) collective-permute-start(bf16[640,256]{1,0:T(8,128)(2,1)S(1)} %collective-permute-done.6.refs_2_), channel_id=1, source_target_pairs={{4,0},{5,1},{8,4},{9,5},{12,8},{13,9},{14,12},{15,13},{10,14},{11,... | collective-permute-start | bytes 983048 | tf_op jit(solution)/shard_map/ppermute | solution.py:355
  18.8 13.5 %collective-permute-start.11 = (bf16[768,256]{1,0:T(8,128)(2,1)S(1)}, bf16[768,256]{1,0:T(8,128)(2,1)S(1)}, u32[]{:S(2)}, u32[]{:S(2)}) collective-permute-start(bf16[768,256]{1,0:T(8,128)(2,1)S(1)} %maximum_select_fusion.2), channel_id=1, source_target_pairs={{0,16},{16,0},{1,17},{17,1},{2,18},{18,2},{3,19},{19,3},{4,20},{20... | collective-permute-start | bytes 1179656 | tf_op jit(solution)/shard_map/ppermute | solution.py:373
  21.0 8.7 %collective-permute-start.4 = (bf16[4,128,128]{2,1,0:T(8,128)(2,1)S(1)}, bf16[4,128,128]{2,1,0:T(8,128)(2,1)S(1)}, u32[]{:S(2)}, u32[]{:S(2)}) collective-permute-start(bf16[4,128,128]{2,1,0:T(8,128)(2,1)S(1)} %fusion.5), channel_id=1, source_target_pairs={{0,4},{1,5},{2,6},{3,7},{4,0},{5,1},{6,2},{7,3},{8,12},{9,13},{10,... | collective-permute-start | bytes 393224 | tf_op jit(solution)/shard_map/ppermute | solution.py:248
  28.0 16.8 %collective-permute-start.12 = (bf16[768,256]{1,0:T(8,128)(2,1)S(1)}, bf16[768,256]{1,0:T(8,128)(2,1)S(1)}, u32[]{:S(2)}, u32[]{:S(2)}) collective-permute-start(bf16[768,256]{1,0:T(8,128)(2,1)S(1)} %maximum_select_fusion.3), channel_id=1, source_target_pairs={{0,16},{16,0},{1,17},{17,1},{2,18},{18,2},{3,19},{19,3},{4,20},{20... | collective-permute-start | bytes 1179656 | tf_op jit(solution)/shard_map/ppermute | solution.py:373
  29.7 10.1 %collective-permute-start.9 = (bf16[4,128,128]{2,1,0:T(8,128)(2,1)S(1)}, bf16[4,128,128]{2,1,0:T(8,128)(2,1)S(1)}, u32[]{:S(2)}, u32[]{:S(2)}) collective-permute-start(bf16[4,128,128]{2,1,0:T(8,128)(2,1)S(1)} %add_convert_fusion), channel_id=1, source_target_pairs={{0,8},{1,9},{2,10},{3,11},{4,12},{5,13},{6,14},{7,15},{8,0},{9,1},... | collective-permute-start | bytes 393224 | tf_op jit(solution)/shard_map/ppermute | solution.py:248
  32.3 11.9 %collective-permute-start.14 = (bf16[640,256]{1,0:T(8,128)(2,1)S(1)}, bf16[640,256]{1,0:T(8,128)(2,1)S(1)}, u32[]{:S(2)}, u32[]{:S(2)}) collective-permute-start(bf16[640,256]{1,0:T(8,128)(2,1)S(1)} %collective-permute-done.7.refs_4_), channel_id=1, source_target_pairs={{0,4},{1,5},{4,8},{5,9},{8,12},{9,13},{12,14},{13,15},{14,10},{15,... | collective-permute-start | bytes 983048 | tf_op jit(solution)/shard_map/ppermute | solution.py:354
  35.2 8.9 %collective-permute-start.15 = (bf16[640,256]{1,0:T(8,128)(2,1)S(1)}, bf16[640,256]{1,0:T(8,128)(2,1)S(1)}, u32[]{:S(2)}, u32[]{:S(2)}) collective-permute-start(bf16[640,256]{1,0:T(8,128)(2,1)S(1)} %collective-permute-done.8.refs_5_), channel_id=1, source_target_pairs={{4,0},{5,1},{8,4},{9,5},{12,8},{13,9},{14,12},{15,13},{10,14},{11,... | collective-permute-start | bytes 983048 | tf_op jit(solution)/shard_map/ppermute | solution.py:355
  39.8 7.5 %collective-permute-start.10 = (bf16[2,4,128,128]{3,2,1,0:T(8,128)(2,1)S(1)}, bf16[2,4,128,128]{3,2,1,0:T(8,128)(2,1)S(1)}, u32[]{:S(2)}, u32[]{:S(2)}) collective-permute-start(bf16[2,4,128,128]{3,2,1,0:T(8,128)(2,1)S(1)} %pad_maximum_fusion), channel_id=1, source_target_pairs={{0,2},{1,3},{2,0},{3,1},{4,6},{5,7},{6,4},{7,5},{8,10},{9,11},{10,... | collective-permute-start | bytes 786440 | tf_op jit(solution)/shard_map/ppermute | solution.py:248
  44.2 3.2 %copy-start.5 = (f32[2048]{0:T(1024)S(1)}, f32[2048]{0:T(1024)}, u32[]{:S(2)}) copy-start(f32[2048]{0:T(1024)} %param.13) | copy-start | bytes 24580
  44.3 9.9 %collective-permute-start.16 = (bf16[768,256]{1,0:T(8,128)(2,1)S(1)}, bf16[768,256]{1,0:T(8,128)(2,1)S(1)}, u32[]{:S(2)}, u32[]{:S(2)}) collective-permute-start(bf16[768,256]{1,0:T(8,128)(2,1)S(1)} %maximum_select_fusion.4), channel_id=1, source_target_pairs={{0,16},{16,0},{1,17},{17,1},{2,18},{18,2},{3,19},{19,3},{4,20},{20... | collective-permute-start | bytes 1179656 | tf_op jit(solution)/shard_map/ppermute | solution.py:373
  44.8 6.8 %collective-permute-start.18 = (bf16[256,256]{1,0:T(8,128)(2,1)S(1)}, bf16[256,256]{1,0:T(8,128)(2,1)S(1)}, u32[]{:S(2)}, u32[]{:S(2)}) collective-permute-start(bf16[256,256]{1,0:T(8,128)(2,1)S(1)} %slice.109), channel_id=1, source_target_pairs={{0,4},{1,5},{4,8},{5,9},{8,12},{9,13},{12,14},{13,15},{14,10},{15,... | collective-permute-start | bytes 393224 | tf_op jit(solution)/shard_map/ppermute | solution.py:354
  46.7 5.7 %collective-permute-start.19 = (bf16[384,256]{1,0:T(8,128)(2,1)S(1)}, bf16[384,256]{1,0:T(8,128)(2,1)S(1)}, u32[]{:S(2)}, u32[]{:S(2)}) collective-permute-start(bf16[384,256]{1,0:T(8,128)(2,1)S(1)} %slice.110), channel_id=1, source_target_pairs={{4,0},{5,1},{8,4},{9,5},{12,8},{13,9},{14,12},{15,13},{10,14},{11,... | collective-permute-start | bytes 589832 | tf_op jit(solution)/shard_map/ppermute | solution.py:355
  47.4 1.7 %copy-start.1 = (bf16[1024,256]{1,0:T(8,128)(2,1)S(1)}, bf16[1024,256]{1,0:T(8,128)(2,1)}, u32[]{:S(2)}) copy-start(bf16[1024,256]{1,0:T(8,128)(2,1)} %copy-done) | copy-start | bytes 1572868
  51.5 10.0 %collective-permute-start.13 = (bf16[256,1280]{1,0:T(8,128)(2,1)S(1)}, bf16[256,1280]{1,0:T(8,128)(2,1)S(1)}, u32[]{:S(2)}, u32[]{:S(2)}) collective-permute-start(bf16[256,1280]{1,0:T(8,128)(2,1)S(1)} %get-tuple-element.40), channel_id=1, source_target_pairs={{0,1},{1,0},{2,3},{3,2},{4,5},{5,4},{6,7},{7,6},{8,9},{9,8},{10,11... | collective-permute-start | bytes 1966088 | tf_op jit(solution)/shard_map/ppermute | solution.py:248
  52.5 6.5 %collective-permute-start.20 = (bf16[384,256]{1,0:T(8,128)(2,1)S(1)}, bf16[384,256]{1,0:T(8,128)(2,1)S(1)}, u32[]{:S(2)}, u32[]{:S(2)}) collective-permute-start(bf16[384,256]{1,0:T(8,128)(2,1)S(1)} %fusion), channel_id=1, source_target_pairs={{0,16},{16,0},{1,17},{17,1},{2,18},{18,2},{3,19},{19,3},{4,20},{20... | collective-permute-start | bytes 589832 | tf_op jit(solution)/shard_map/ppermute | solution.py:373
  55.6 5.9 %collective-permute-start.17 = (bf16[256,512]{1,0:T(8,128)(2,1)S(1)}, bf16[256,512]{1,0:T(8,128)(2,1)S(1)}, u32[]{:S(2)}, u32[]{:S(2)}) collective-permute-start(bf16[256,512]{1,0:T(8,128)(2,1)S(1)} %get-tuple-element.44), channel_id=1, source_target_pairs={{0,1},{1,0},{2,3},{3,2},{4,5},{5,4},{6,7},{7,6},{8,9},{9,8},{10,11... | collective-permute-start | bytes 786440 | tf_op jit(solution)/shard_map/ppermute | solution.py:248
  60.1 1.4 %collective-permute-start.21 = (bf16[256,256]{1,0:T(8,128)(2,1)S(1)}, bf16[256,256]{1,0:T(8,128)(2,1)S(1)}, u32[]{:S(2)}, u32[]{:S(2)}) collective-permute-start(bf16[256,256]{1,0:T(8,128)(2,1)S(1)} %get-tuple-element.48), channel_id=1, source_target_pairs={{0,1},{1,0},{2,3},{3,2},{4,5},{5,4},{6,7},{7,6},{8,9},{9,8},{10,11... | collective-permute-start | bytes 393224 | tf_op jit(solution)/shard_map/ppermute | solution.py:248

commit v6 on v5

--- a/solution.py
+++ b/solution.py
@@ -384,7 +384,7 @@
 
     while len(quarters) + 2 < log_blocks:
         level(len(quarters) + 2)
-    joined = jnp.stack(quarters)
+    joined = tie(jnp.stack(quarters), *crossed[1:2])
     rest = swap(joined, 1)
     both = jnp.where(
         upper == 0, jnp.concatenate([joined, rest], axis=1), jnp.concatenate([rest, joined], axis=1)

time: 63.3 us -> 63.4 us (level)
  no operation moved by 1% of the time
where the time goes in v6:
time: 63.4 us; the launch traced here: 63.1 us
  starting transfers between devices  23.9 us (38%)
  Pallas kernels  21.1 us (33%)
  waiting for transfers between devices  15.4 us (24%)
  local copies, waits for them, and re-layouts  1.04 us (2%)
  other arithmetic  0.76 us (1%)
    pallas_call x8, Pallas kernels, call(): pl.pallas_call(kernel, out_shape=out_shape, in_specs=in_specs, out_specs=...  14 us
    ppermute x4, starting transfers between devices, body(): right = lax.ppermute(right, 'seq', clockwise)  9.46 us
    ppermute x10, starting transfers between devices, swap(): return lax.ppermute(block, 'seq', route)  8.33 us
    ppermute x4, waiting for transfers between devices, body(): left = lax.ppermute(left, 'seq', counter)  7.99 us
    pallas_call x2, Pallas kernels, split(): pl.pallas_call(functools.partial(split_kernel, len(arrays)), out_shape=bf...  5.48 us
    ppermute x4, starting transfers between devices, body(): crossed.append(lax.ppermute(wanted, 'grp', [(0, 1), (1, 0)]))  5.44 us
    ppermute x4, waiting for transfers between devices, body(): crossed.append(lax.ppermute(wanted, 'grp', [(0, 1), (1, 0)]))  3.41 us
    ppermute x10, waiting for transfers between devices, swap(): return lax.ppermute(block, 'seq', route)  2.6 us
  transfers between devices with their start and end apart: 22, of which 10 were waited for; matrix products, arithmetic and copies ran while one was open for 4% of the time, Pallas kernels for 31%

profile of v6, /device:TPU:0, one launch (start us, length us, event | category | flops | bytes accessed | tf_op | source)
XLA Modules:
  0.0 63.1 jit_solution(5356804275657306549)
XLA Ops:
  0.0 0.5 collective-permute-start
  0.5 2.9 %shard_map.83 = bf16[512,1024]{1,0:T(8,128)(2,1)} custom-call(bf16[256,2048]{1,0:T(8,128)(2,1)} %refs_0_.5, bf16[256,2048]{1,0:T(8,128)(2,1)} %refs_1_.3, s32[1,256]{1,0:T(1,128)} %bitcast.23, s32[256]{0:T(256)} %refs_3_.1), custom_call_target="tpu_custom_call" | custom-call | flops 2300000000 | bytes 1048576 | tf_op jit(solution)/shard_map/pallas_call | solution.py:255
  3.4 0.1 collective-permute-start.2
  3.6 0.2 fusion.3.lam_ref.lam0_ref
  3.9 0.0 collective-permute-done
  3.9 0.2 maximum_select_fusion.refs_2_.refs_0_
  4.1 0.0 copy-start.2
  4.1 0.0 copy-start.3
  4.2 3.1 %collective-permute-start.5 = (bf16[640,256]{1,0:T(8,128)(2,1)S(1)}, bf16[640,256]{1,0:T(8,128)(2,1)S(1)}, u32[]{:S(2)}, u32[]{:S(2)}) collective-permute-start(bf16[640,256]{1,0:T(8,128)(2,1)S(1)} %slice_select_fusion), channel_id=1, source_target_pairs={{0,4},{1,5},{4,8},{5,9},{8,12},{9,13},{12,14},{13,15},{14,10},{15,... | collective-permute-start | bytes 983048 | tf_op jit(solution)/shard_map/ppermute | solution.py:354
  7.2 0.0 collective-permute-start.6
  7.2 2.5 %shard_map.82 = bf16[272,1024]{1,0:T(8,128)(2,1)} custom-call(bf16[256,2048]{1,0:T(8,128)(2,1)} %q_ref.3, s32[1,256]{1,0:T(1,128)} %bitcast.24, bf16[1024,256]{1,0:T(8,128)(2,1)} %copy-done), custom_call_target="tpu_custom_call" | custom-call | flops 2300000000 | bytes 1048576 | tf_op jit(solution)/shard_map/pallas_call | solution.py:255
  9.8 0.1 collective-permute-start.1
  9.9 0.7 %dynamic-slice_bitcast_fusion.info = s32[15]{0:T(128)S(1)} fusion(s32[2,16,15]{2,1,0:T(8,128)} %constant.36.clone, s32[]{:T(128)S(6)} %select_n.85, s32[]{:T(128)S(6)} %select_n.86), kind=kLoop, calls=%fused_computation.27 | loop fusion | bytes 128 | tf_op jit(solution)/shard_map/reshape | solution.py:244
  10.6 1.0 %shard_map.84 = (f32[8,128,128]{2,1,0:T(8,128)S(1)}, bf16[8,128,128]{2,1,0:T(8,128)(2,1)S(1)}, bf16[8,128,128]{2,1,0:T(8,128)(2,1)S(1)}) custom-call(s32[15]{0:T(128)S(1)} %dynamic-slice_bitcast_fusion.info, bf16[256,2048]{1,0:T(8,128)(2,1)S(1)} %copy-done.2, bf16[256,2048]{1,0:T(8,128)(2,1)S(1)} %copy-done.3, ...), custom_call_target="tpu_custom_call" | custom-call | flops 1150000000 | bytes 1048576 | tf_op jit(solution)/shard_map/pallas_call | solution.py:21
  11.6 0.0 copy-start.4
  11.6 2.0 %collective-permute-start.3 = (bf16[8,128,128]{2,1,0:T(8,128)(2,1)S(1)}, bf16[8,128,128]{2,1,0:T(8,128)(2,1)S(1)}, u32[]{:S(2)}, u32[]{:S(2)}) collective-permute-start(bf16[8,128,128]{2,1,0:T(8,128)(2,1)S(1)} %get-tuple-element.29), channel_id=1, source_target_pairs={{0,2},{1,3},{2,0},{3,1},{4,6},{5,7},{6,4},{7,5},{8,10},{9,11},{10,... | collective-permute-start | bytes 786440 | tf_op jit(solution)/shard_map/ppermute | solution.py:248
  13.7 1.4 %collective-permute-done.5.refs_1_ = bf16[640,256]{1,0:T(8,128)(2,1)S(1)} collective-permute-done((bf16[640,256]{1,0:T(8,128)(2,1)S(1)}, bf16[640,256]{1,0:T(8,128)(2,1)S(1)}, u32[]{:S(2)}, u32[]{:S(2)}) %collective-permute-start.5) | collective-permute-done | bytes 327712 | tf_op jit(solution)/shard_map/ppermute | solution.py:354
  15.1 1.5 %collective-permute-done.6.refs_2_ = bf16[640,256]{1,0:T(8,128)(2,1)S(1)} collective-permute-done((bf16[640,256]{1,0:T(8,128)(2,1)S(1)}, bf16[640,256]{1,0:T(8,128)(2,1)S(1)}, u32[]{:S(2)}, u32[]{:S(2)}) %collective-permute-start.6) | collective-permute-done | bytes 327712 | tf_op jit(solution)/shard_map/ppermute | solution.py:355
  16.6 1.6 %collective-permute-start.7 = (bf16[640,256]{1,0:T(8,128)(2,1)S(1)}, bf16[640,256]{1,0:T(8,128)(2,1)S(1)}, u32[]{:S(2)}, u32[]{:S(2)}) collective-permute-start(bf16[640,256]{1,0:T(8,128)(2,1)S(1)} %collective-permute-done.5.refs_1_), channel_id=1, source_target_pairs={{0,4},{1,5},{4,8},{5,9},{8,12},{9,13},{12,14},{13,15},{14,10},{15,... | collective-permute-start | bytes 983048 | tf_op jit(solution)/shard_map/ppermute | solution.py:354
  18.2 0.5 collective-permute-start.8
  18.6 0.1 fusion.16
  18.7 0.1 maximum_select_fusion.3
  18.8 1.6 %collective-permute-start.12 = (bf16[768,256]{1,0:T(8,128)(2,1)S(1)}, bf16[768,256]{1,0:T(8,128)(2,1)S(1)}, u32[]{:S(2)}, u32[]{:S(2)}) collective-permute-start(bf16[768,256]{1,0:T(8,128)(2,1)S(1)} %maximum_select_fusion.3), channel_id=1, source_target_pairs={{0,16},{16,0},{1,17},{17,1},{2,18},{18,2},{3,19},{19,3},{4,20},{20... | collective-permute-start | bytes 1179656 | tf_op jit(solution)/shard_map/ppermute | solution.py:373
  20.4 0.0 collective-permute-done.1.refs_1_.got_ref
  20.4 0.2 fusion.1.lam_ref.lam1_ref
  20.6 0.3 collective-permute-done.3.refs_1_
  21.0 1.6 %collective-permute-start.4 = (bf16[4,128,128]{2,1,0:T(8,128)(2,1)S(1)}, bf16[4,128,128]{2,1,0:T(8,128)(2,1)S(1)}, u32[]{:S(2)}, u32[]{:S(2)}) collective-permute-start(bf16[4,128,128]{2,1,0:T(8,128)(2,1)S(1)} %fusion.5), channel_id=1, source_target_pairs={{0,4},{1,5},{2,6},{3,7},{4,0},{5,1},{6,2},{7,3},{8,12},{9,13},{10,... | collective-permute-start | bytes 393224 | tf_op jit(solution)/shard_map/ppermute | solution.py:248
  22.6 2.6 %shard_map.85.base0_ref = f32[1024,256]{1,0:T(8,128)S(1)} custom-call(s32[15]{0:T(128)S(1)} %dynamic-slice_bitcast_fusion.info, f32[8,18,256]{2,1,0:T(8,128)S(1)} %fusion.3.lam_ref.lam0_ref, bf16[256,2048]{1,0:T(8,128)(2,1)S(1)} %copy-done.2, bf16[256,2048]{1,0:T(8,128)(2,1)S(1)} %copy-done.3, bf16[256,2048]{1,0:T(8,128)(2,1)S(1)} %copy-done.4), custom_call_target="tpu_custom_call" | custom-call | flops 2415000064 | bytes 1048576 | tf_op jit(solution)/shard_map/pallas_call | solution.py:21
  25.2 2.6 %collective-permute-done.8.refs_5_ = bf16[640,256]{1,0:T(8,128)(2,1)S(1)} collective-permute-done((bf16[640,256]{1,0:T(8,128)(2,1)S(1)}, bf16[640,256]{1,0:T(8,128)(2,1)S(1)}, u32[]{:S(2)}, u32[]{:S(2)}) %collective-permute-start.8) | collective-permute-done | bytes 327712 | tf_op jit(solution)/shard_map/ppermute | solution.py:355
  27.8 0.0 collective-permute-done.7.refs_4_
  27.9 0.1 maximum_select_fusion.2
  28.0 1.7 %collective-permute-start.10 = (bf16[768,256]{1,0:T(8,128)(2,1)S(1)}, bf16[768,256]{1,0:T(8,128)(2,1)S(1)}, u32[]{:S(2)}, u32[]{:S(2)}) collective-permute-start(bf16[768,256]{1,0:T(8,128)(2,1)S(1)} %maximum_select_fusion.2), channel_id=1, source_target_pairs={{0,16},{16,0},{1,17},{17,1},{2,18},{18,2},{3,19},{19,3},{4,20},{20... | collective-permute-start | bytes 1179656 | tf_op jit(solution)/shard_map/ppermute | solution.py:373
  29.7 0.0 collective-permute-done.4
  29.7 2.6 %collective-permute-start.9 = (bf16[4,128,128]{2,1,0:T(8,128)(2,1)S(1)}, bf16[4,128,128]{2,1,0:T(8,128)(2,1)S(1)}, u32[]{:S(2)}, u32[]{:S(2)}) collective-permute-start(bf16[4,128,128]{2,1,0:T(8,128)(2,1)S(1)} %add_convert_fusion), channel_id=1, source_target_pairs={{0,8},{1,9},{2,10},{3,11},{4,12},{5,13},{6,14},{7,15},{8,0},{9,1},... | collective-permute-start | bytes 393224 | tf_op jit(solution)/shard_map/ppermute | solution.py:248
  32.3 0.0 collective-permute-done.12.refs_3_
  32.3 2.9 %collective-permute-start.14 = (bf16[640,256]{1,0:T(8,128)(2,1)S(1)}, bf16[640,256]{1,0:T(8,128)(2,1)S(1)}, u32[]{:S(2)}, u32[]{:S(2)}) collective-permute-start(bf16[640,256]{1,0:T(8,128)(2,1)S(1)} %collective-permute-done.7.refs_4_), channel_id=1, source_target_pairs={{0,4},{1,5},{4,8},{5,9},{8,12},{9,13},{12,14},{13,15},{14,10},{15,... | collective-permute-start | bytes 983048 | tf_op jit(solution)/shard_map/ppermute | solution.py:354
  35.2 0.0 collective-permute-start.15
  35.2 2.6 %shard_map.86.base1_ref = f32[1024,256]{1,0:T(8,128)S(1)} custom-call(s32[15]{0:T(128)S(1)} %dynamic-slice_bitcast_fusion.info, f32[8,18,256]{2,1,0:T(8,128)S(1)} %fusion.1.lam_ref.lam1_ref, bf16[512,1024]{1,0:T(8,128)(2,1)S(1)} %collective-permute-done.2.got_ref.refs_0_, bf16[272,1024]{1,0:T(8,128)(2,1)S(1)} %collective-permute-done.1.refs_1_.got_ref), custom_call_target="tpu_custom_call" | custom-call | flops 2415000064 | bytes 1048576 | tf_op jit(solution)/shard_map/pallas_call | solution.py:21
  37.8 1.3 %shard_map.87.base_ref = f32[1024,512]{1,0:T(8,128)S(1)} custom-call(s32[15]{0:T(128)S(1)} %dynamic-slice_bitcast_fusion.info, bf16[256,2048]{1,0:T(8,128)(2,1)S(1)} %copy-done.4, bf16[272,1024]{1,0:T(8,128)(2,1)S(1)} %collective-permute-done.1.refs_1_.got_ref, f32[8,18,256]{2,1,0:T(8,128)S(1)} %fusion.3.lam_ref.lam0_ref, ...), custom_call_target="tpu_custom_call" | custom-call | flops 1840000000 | bytes 1048576 | tf_op jit(solution)/shard_map/pallas_call | solution.py:21
  39.1 0.7 %collective-permute-done.9 = bf16[4,128,128]{2,1,0:T(8,128)(2,1)S(1)} collective-permute-done((bf16[4,128,128]{2,1,0:T(8,128)(2,1)S(1)}, bf16[4,128,128]{2,1,0:T(8,128)(2,1)S(1)}, u32[]{:S(2)}, u32[]{:S(2)}) %collective-permute-start.9) | collective-permute-done | bytes 131104 | tf_op jit(solution)/shard_map/ppermute | solution.py:248
  39.8 1.3 %collective-permute-start.11 = (bf16[2,4,128,128]{3,2,1,0:T(8,128)(2,1)S(1)}, bf16[2,4,128,128]{3,2,1,0:T(8,128)(2,1)S(1)}, u32[]{:S(2)}, u32[]{:S(2)}) collective-permute-start(bf16[2,4,128,128]{3,2,1,0:T(8,128)(2,1)S(1)} %pad_maximum_fusion), channel_id=1, source_target_pairs={{0,2},{1,3},{2,0},{3,1},{4,6},{5,7},{6,4},{7,5},{8,10},{9,11},{10,... | collective-permute-start | bytes 786440 | tf_op jit(solution)/shard_map/ppermute | solution.py:248
  41.1 3.0 %collective-permute-done.15.refs_1_ = bf16[640,256]{1,0:T(8,128)(2,1)S(1)} collective-permute-done((bf16[640,256]{1,0:T(8,128)(2,1)S(1)}, bf16[640,256]{1,0:T(8,128)(2,1)S(1)}, u32[]{:S(2)}, u32[]{:S(2)}) %collective-permute-start.15) | collective-permute-done | bytes 327712 | tf_op jit(solution)/shard_map/ppermute | solution.py:355
  44.2 0.0 collective-permute-done.14.refs_0_
  44.2 0.0 copy-start.5
  44.2 0.1 maximum_select_fusion.4
  44.3 0.5 collective-permute-start.16
  44.8 1.9 %collective-permute-start.18 = (bf16[256,256]{1,0:T(8,128)(2,1)S(1)}, bf16[256,256]{1,0:T(8,128)(2,1)S(1)}, u32[]{:S(2)}, u32[]{:S(2)}) collective-permute-start(bf16[256,256]{1,0:T(8,128)(2,1)S(1)} %slice.109), channel_id=1, source_target_pairs={{0,4},{1,5},{4,8},{5,9},{8,12},{9,13},{12,14},{13,15},{14,10},{15,... | collective-permute-start | bytes 393224 | tf_op jit(solution)/shard_map/ppermute | solution.py:354
  46.7 0.2 collective-permute-start.19
  47.0 0.3 collective-permute-done.11
  47.4 1.7 %shard_map.88.normed_ref = bf16[512,1024]{1,0:T(8,128)(2,1)S(1)} custom-call(s32[15]{0:T(128)S(1)} %dynamic-slice_bitcast_fusion.info, bf16[256,2048]{1,0:T(8,128)(2,1)S(1)} %copy-done.4, bf16[272,1024]{1,0:T(8,128)(2,1)S(1)} %collective-permute-done.1.refs_1_.got_ref, f32[8,18,256]{2,1,0:T(8,128)S(1)} %fusion.3.lam_ref.lam0_ref, ...), custom_call_target="tpu_custom_call" | custom-call | flops 2300000000 | bytes 1048576 | tf_op jit(solution)/shard_map/pallas_call | solution.py:21
  49.2 2.3 %shard_map.89 = (f32[256,1280]{1,0:T(8,128)S(1)}, bf16[256,1280]{1,0:T(8,128)(2,1)S(1)}) custom-call(s32[15]{0:T(128)S(1)} %dynamic-slice_bitcast_fusion.info, bf16[512,1024]{1,0:T(8,128)(2,1)S(1)} %shard_map.88.normed_ref, bf16[1024,256]{1,0:T(8,128)(2,1)S(1)} %copy-done.1, bf16[640,256]{1,0:T(8,128)(2,1)S(1)} %collective-permute-done.5.refs_1_, ...), custom_call_target="tpu_custom_call" | custom-call | flops 2875000064 | bytes 1048576 | tf_op jit(solution)/shard_map/pallas_call | solution.py:21
  51.5 0.1 collective-permute-start.13
  51.6 0.8 %collective-permute-done.19.refs_1_ = bf16[384,256]{1,0:T(8,128)(2,1)S(1)} collective-permute-done((bf16[384,256]{1,0:T(8,128)(2,1)S(1)}, bf16[384,256]{1,0:T(8,128)(2,1)S(1)}, u32[]{:S(2)}, u32[]{:S(2)}) %collective-permute-start.19) | collective-permute-done | bytes 196640 | tf_op jit(solution)/shard_map/ppermute | solution.py:355
  52.5 0.1 fusion
  52.5 1.7 %collective-permute-start.20 = (bf16[384,256]{1,0:T(8,128)(2,1)S(1)}, bf16[384,256]{1,0:T(8,128)(2,1)S(1)}, u32[]{:S(2)}, u32[]{:S(2)}) collective-permute-start(bf16[384,256]{1,0:T(8,128)(2,1)S(1)} %fusion), channel_id=1, source_target_pairs={{0,16},{16,0},{1,17},{17,1},{2,18},{18,2},{3,19},{19,3},{4,20},{20... | collective-permute-start | bytes 589832 | tf_op jit(solution)/shard_map/ppermute | solution.py:373
  54.2 1.4 %shard_map.90 = (f32[256,512]{1,0:T(8,128)S(1)}, bf16[256,512]{1,0:T(8,128)(2,1)S(1)}) custom-call(s32[15]{0:T(128)S(1)} %dynamic-slice_bitcast_fusion.info, bf16[512,1024]{1,0:T(8,128)(2,1)S(1)} %shard_map.88.normed_ref, bf16[640,256]{1,0:T(8,128)(2,1)S(1)} %collective-permute-done.14.refs_0_, bf16[640,256]{1,0:T(8,128)(2,1)S(1)} %collective-permute-done.15.refs_1_, ...), custom_call_target="tpu_custom_call" | custom-call | flops 1150000000 | bytes 1048576 | tf_op jit(solution)/shard_map/pallas_call | solution.py:21
  55.6 0.1 collective-permute-start.17
  55.7 3.4 %collective-permute-done.20.refs_2_ = bf16[384,256]{1,0:T(8,128)(2,1)S(1)} collective-permute-done((bf16[384,256]{1,0:T(8,128)(2,1)S(1)}, bf16[384,256]{1,0:T(8,128)(2,1)S(1)}, u32[]{:S(2)}, u32[]{:S(2)}) %collective-permute-start.20) | collective-permute-done | bytes 196640 | tf_op jit(solution)/shard_map/ppermute | solution.py:373
  59.1 1.0 %shard_map.91 = (f32[256,256]{1,0:T(8,128)S(1)}, bf16[256,256]{1,0:T(8,128)(2,1)S(1)}) custom-call(s32[15]{0:T(128)S(1)} %dynamic-slice_bitcast_fusion.info, bf16[512,1024]{1,0:T(8,128)(2,1)S(1)} %shard_map.88.normed_ref, bf16[256,256]{1,0:T(8,128)(2,1)S(1)} %collective-permute-done.18.refs_0_, bf16[384,256]{1,0:T(8,128)(2,1)S(1)} %collective-permute-done.19.refs_1_, ...), custom_call_target="tpu_custom_call" | custom-call | flops 575000000 | bytes 1048576 | tf_op jit(solution)/shard_map/pallas_call | solution.py:21
  60.1 0.1 collective-permute-start.21
  60.2 1.3 %collective-permute-done.21.refs_5_ = bf16[256,256]{1,0:T(8,128)(2,1)S(1)} collective-permute-done((bf16[256,256]{1,0:T(8,128)(2,1)S(1)}, bf16[256,256]{1,0:T(8,128)(2,1)S(1)}, u32[]{:S(2)}, u32[]{:S(2)}) %collective-permute-start.21) | collective-permute-done | bytes 131104 | tf_op jit(solution)/shard_map/ppermute | solution.py:248
  61.5 0.0 collective-permute-done.17.refs_3_
  61.5 0.0 collective-permute-done.13.refs_1_
  61.5 1.6 %shard_map.92 = bf16[256,2048]{1,0:T(8,128)(2,1)} custom-call(s32[15]{0:T(128)S(1)} %dynamic-slice_bitcast_fusion.info, f32[256,1280]{1,0:T(8,128)S(1)} %get-tuple-element.41.refs_0_, bf16[256,1280]{1,0:T(8,128)(2,1)S(1)} %collective-permute-done.13.refs_1_, f32[256,512]{1,0:T(8,128)S(1)} %get-tuple-element.45.refs_2_, ...), custom_call_target="tpu_custom_call" | custom-call | flops 1150000000 | bytes 1048576 | tf_op jit(solution)/shard_map/pallas_call | solution.py:438
  (35 shorter events, 0.5 us)
Async XLA Ops:
  0.0 3.9 %collective-permute-start = (bf16[2048,128]{1,0:T(8,128)(2,1)}, bf16[2048,128]{1,0:T(8,128)(2,1)S(1)}, u32[]{:S(2)}, u32[]{:S(2)}) collective-permute-start(bf16[2048,128]{1,0:T(8,128)(2,1)} %param.14), channel_id=1, source_target_pairs={{0,1},{1,0},{2,3},{3,2},{4,5},{5,4},{6,7},{7,6},{8,9},{9,8},{10,11... | collective-permute-start | bytes 1572872 | tf_op jit(solution)/shard_map/ppermute | solution.py:248
  0.5 3.1 %copy-start.7 = (f32[64,18,16]{0,2,1:T(8,128)S(1)}, f32[64,18,16]{0,2,1:T(8,128)}, u32[]{:S(2)}) copy-start(f32[64,18,16]{0,2,1:T(8,128)} %param.12) | copy-start | bytes 221188
  0.5 3.1 %copy-start.6 = (bf16[2048,128]{1,0:T(8,128)(2,1)S(1)}, bf16[2048,128]{1,0:T(8,128)(2,1)}, u32[]{:S(2)}) copy-start(bf16[2048,128]{1,0:T(8,128)(2,1)} %param.14) | copy-start | bytes 1572868
  0.5 3.1 %copy-start.8 = (s32[256]{0:T(256)S(1)}, s32[256]{0:T(256)}, u32[]{:S(2)}) copy-start(s32[256]{0:T(256)} %refs_3_.1) | copy-start | bytes 3076
  3.4 7.2 %collective-permute-start.2 = (bf16[512,1024]{1,0:T(8,128)(2,1)}, bf16[512,1024]{1,0:T(8,128)(2,1)S(1)}, u32[]{:S(2)}, u32[]{:S(2)}) collective-permute-start(bf16[512,1024]{1,0:T(8,128)(2,1)} %shard_map.83), channel_id=1, source_target_pairs={{0,1},{1,0},{2,3},{3,2},{4,5},{5,4},{6,7},{7,6},{8,9},{9,8},{10,11... | collective-permute-start | bytes 3145736 | tf_op jit(solution)/shard_map/ppermute | solution.py:248
  4.1 3.2 %copy-start = (bf16[1024,256]{1,0:T(8,128)(2,1)}, bf16[1024,256]{1,0:T(8,128)(2,1)S(1)}, u32[]{:S(2)}) copy-start(bf16[1024,256]{1,0:T(8,128)(2,1)S(1)} %maximum_select_fusion.refs_2_.refs_0_) | copy-start | bytes 1572868
  4.1 6.4 %copy-start.2 = (bf16[256,2048]{1,0:T(8,128)(2,1)S(1)}, bf16[256,2048]{1,0:T(8,128)(2,1)}, u32[]{:S(2)}) copy-start(bf16[256,2048]{1,0:T(8,128)(2,1)} %refs_0_.5) | copy-start | bytes 3145732
  4.1 6.4 %copy-start.3 = (bf16[256,2048]{1,0:T(8,128)(2,1)S(1)}, bf16[256,2048]{1,0:T(8,128)(2,1)}, u32[]{:S(2)}) copy-start(bf16[256,2048]{1,0:T(8,128)(2,1)} %refs_1_.3) | copy-start | bytes 3145732
  4.2 10.9 %collective-permute-start.5 = (bf16[640,256]{1,0:T(8,128)(2,1)S(1)}, bf16[640,256]{1,0:T(8,128)(2,1)S(1)}, u32[]{:S(2)}, u32[]{:S(2)}) collective-permute-start(bf16[640,256]{1,0:T(8,128)(2,1)S(1)} %slice_select_fusion), channel_id=1, source_target_pairs={{0,4},{1,5},{4,8},{5,9},{8,12},{9,13},{12,14},{13,15},{14,10},{15,... | collective-permute-start | bytes 983048 | tf_op jit(solution)/shard_map/ppermute | solution.py:354
  7.2 9.4 %collective-permute-start.6 = (bf16[640,256]{1,0:T(8,128)(2,1)S(1)}, bf16[640,256]{1,0:T(8,128)(2,1)S(1)}, u32[]{:S(2)}, u32[]{:S(2)}) collective-permute-start(bf16[640,256]{1,0:T(8,128)(2,1)S(1)} %slice_select_fusion), channel_id=1, source_target_pairs={{4,0},{5,1},{8,4},{9,5},{12,8},{13,9},{14,12},{15,13},{10,14},{11,... | collective-permute-start | bytes 983048 | tf_op jit(solution)/shard_map/ppermute | solution.py:355
  9.8 10.6 %collective-permute-start.1 = (bf16[272,1024]{1,0:T(8,128)(2,1)}, bf16[272,1024]{1,0:T(8,128)(2,1)S(1)}, u32[]{:S(2)}, u32[]{:S(2)}) collective-permute-start(bf16[272,1024]{1,0:T(8,128)(2,1)} %shard_map.82), channel_id=1, source_target_pairs={{0,1},{1,0},{2,3},{3,2},{4,5},{5,4},{6,7},{7,6},{8,9},{9,8},{10,11... | collective-permute-start | bytes 1671176 | tf_op jit(solution)/shard_map/ppermute | solution.py:248
  11.6 11.0 %copy-start.4 = (bf16[256,2048]{1,0:T(8,128)(2,1)S(1)}, bf16[256,2048]{1,0:T(8,128)(2,1)}, u32[]{:S(2)}) copy-start(bf16[256,2048]{1,0:T(8,128)(2,1)} %q_ref.3) | copy-start | bytes 3145732
  11.6 9.2 %collective-permute-start.3 = (bf16[8,128,128]{2,1,0:T(8,128)(2,1)S(1)}, bf16[8,128,128]{2,1,0:T(8,128)(2,1)S(1)}, u32[]{:S(2)}, u32[]{:S(2)}) collective-permute-start(bf16[8,128,128]{2,1,0:T(8,128)(2,1)S(1)} %get-tuple-element.29), channel_id=1, source_target_pairs={{0,2},{1,3},{2,0},{3,1},{4,6},{5,7},{6,4},{7,5},{8,10},{9,11},{10,... | collective-permute-start | bytes 786440 | tf_op jit(solution)/shard_map/ppermute | solution.py:248
  16.6 11.2 %collective-permute-start.7 = (bf16[640,256]{1,0:T(8,128)(2,1)S(1)}, bf16[640,256]{1,0:T(8,128)(2,1)S(1)}, u32[]{:S(2)}, u32[]{:S(2)}) collective-permute-start(bf16[640,256]{1,0:T(8,128)(2,1)S(1)} %collective-permute-done.5.refs_1_), channel_id=1, source_target_pairs={{0,4},{1,5},{4,8},{5,9},{8,12},{9,13},{12,14},{13,15},{14,10},{15,... | collective-permute-start | bytes 983048 | tf_op jit(solution)/shard_map/ppermute | solution.py:354
  18.2 9.6 %collective-permute-start.8 = (bf16[640,256]{1,0:T(8,128)(2,1)S(1)}, bf16[640,256]{1,0:T(8,128)(2,1)S(1)}, u32[]{:S(2)}, u32[]{:S(2)}) collective-permute-start(bf16[640,256]{1,0:T(8,128)(2,1)S(1)} %collective-permute-done.6.refs_2_), channel_id=1, source_target_pairs={{4,0},{5,1},{8,4},{9,5},{12,8},{13,9},{14,12},{15,13},{10,14},{11,... | collective-permute-start | bytes 983048 | tf_op jit(solution)/shard_map/ppermute | solution.py:355
  18.8 13.5 %collective-permute-start.12 = (bf16[768,256]{1,0:T(8,128)(2,1)S(1)}, bf16[768,256]{1,0:T(8,128)(2,1)S(1)}, u32[]{:S(2)}, u32[]{:S(2)}) collective-permute-start(bf16[768,256]{1,0:T(8,128)(2,1)S(1)} %maximum_select_fusion.3), channel_id=1, source_target_pairs={{0,16},{16,0},{1,17},{17,1},{2,18},{18,2},{3,19},{19,3},{4,20},{20... | collective-permute-start | bytes 1179656 | tf_op jit(solution)/shard_map/ppermute | solution.py:373
  21.0 8.7 %collective-permute-start.4 = (bf16[4,128,128]{2,1,0:T(8,128)(2,1)S(1)}, bf16[4,128,128]{2,1,0:T(8,128)(2,1)S(1)}, u32[]{:S(2)}, u32[]{:S(2)}) collective-permute-start(bf16[4,128,128]{2,1,0:T(8,128)(2,1)S(1)} %fusion.5), channel_id=1, source_target_pairs={{0,4},{1,5},{2,6},{3,7},{4,0},{5,1},{6,2},{7,3},{8,12},{9,13},{10,... | collective-permute-start | bytes 393224 | tf_op jit(solution)/shard_map/ppermute | solution.py:248
  28.0 11.8 %collective-permute-start.10 = (bf16[768,256]{1,0:T(8,128)(2,1)S(1)}, bf16[768,256]{1,0:T(8,128)(2,1)S(1)}, u32[]{:S(2)}, u32[]{:S(2)}) collective-permute-start(bf16[768,256]{1,0:T(8,128)(2,1)S(1)} %maximum_select_fusion.2), channel_id=1, source_target_pairs={{0,16},{16,0},{1,17},{17,1},{2,18},{18,2},{3,19},{19,3},{4,20},{20... | collective-permute-start | bytes 1179656 | tf_op jit(solution)/shard_map/ppermute | solution.py:373
  29.7 10.1 %collective-permute-start.9 = (bf16[4,128,128]{2,1,0:T(8,128)(2,1)S(1)}, bf16[4,128,128]{2,1,0:T(8,128)(2,1)S(1)}, u32[]{:S(2)}, u32[]{:S(2)}) collective-permute-start(bf16[4,128,128]{2,1,0:T(8,128)(2,1)S(1)} %add_convert_fusion), channel_id=1, source_target_pairs={{0,8},{1,9},{2,10},{3,11},{4,12},{5,13},{6,14},{7,15},{8,0},{9,1},... | collective-permute-start | bytes 393224 | tf_op jit(solution)/shard_map/ppermute | solution.py:248
  32.3 11.9 %collective-permute-start.14 = (bf16[640,256]{1,0:T(8,128)(2,1)S(1)}, bf16[640,256]{1,0:T(8,128)(2,1)S(1)}, u32[]{:S(2)}, u32[]{:S(2)}) collective-permute-start(bf16[640,256]{1,0:T(8,128)(2,1)S(1)} %collective-permute-done.7.refs_4_), channel_id=1, source_target_pairs={{0,4},{1,5},{4,8},{5,9},{8,12},{9,13},{12,14},{13,15},{14,10},{15,... | collective-permute-start | bytes 983048 | tf_op jit(solution)/shard_map/ppermute | solution.py:354
  35.2 8.9 %collective-permute-start.15 = (bf16[640,256]{1,0:T(8,128)(2,1)S(1)}, bf16[640,256]{1,0:T(8,128)(2,1)S(1)}, u32[]{:S(2)}, u32[]{:S(2)}) collective-permute-start(bf16[640,256]{1,0:T(8,128)(2,1)S(1)} %collective-permute-done.8.refs_5_), channel_id=1, source_target_pairs={{4,0},{5,1},{8,4},{9,5},{12,8},{13,9},{14,12},{15,13},{10,14},{11,... | collective-permute-start | bytes 983048 | tf_op jit(solution)/shard_map/ppermute | solution.py:355
  39.8 7.5 %collective-permute-start.11 = (bf16[2,4,128,128]{3,2,1,0:T(8,128)(2,1)S(1)}, bf16[2,4,128,128]{3,2,1,0:T(8,128)(2,1)S(1)}, u32[]{:S(2)}, u32[]{:S(2)}) collective-permute-start(bf16[2,4,128,128]{3,2,1,0:T(8,128)(2,1)S(1)} %pad_maximum_fusion), channel_id=1, source_target_pairs={{0,2},{1,3},{2,0},{3,1},{4,6},{5,7},{6,4},{7,5},{8,10},{9,11},{10,... | collective-permute-start | bytes 786440 | tf_op jit(solution)/shard_map/ppermute | solution.py:248
  44.2 3.2 %copy-start.5 = (f32[2048]{0:T(1024)S(1)}, f32[2048]{0:T(1024)}, u32[]{:S(2)}) copy-start(f32[2048]{0:T(1024)} %param.13) | copy-start | bytes 24580
  44.3 9.9 %collective-permute-start.16 = (bf16[768,256]{1,0:T(8,128)(2,1)S(1)}, bf16[768,256]{1,0:T(8,128)(2,1)S(1)}, u32[]{:S(2)}, u32[]{:S(2)}) collective-permute-start(bf16[768,256]{1,0:T(8,128)(2,1)S(1)} %maximum_select_fusion.4), channel_id=1, source_target_pairs={{0,16},{16,0},{1,17},{17,1},{2,18},{18,2},{3,19},{19,3},{4,20},{20... | collective-permute-start | bytes 1179656 | tf_op jit(solution)/shard_map/ppermute | solution.py:373
  44.8 6.8 %collective-permute-start.18 = (bf16[256,256]{1,0:T(8,128)(2,1)S(1)}, bf16[256,256]{1,0:T(8,128)(2,1)S(1)}, u32[]{:S(2)}, u32[]{:S(2)}) collective-permute-start(bf16[256,256]{1,0:T(8,128)(2,1)S(1)} %slice.109), channel_id=1, source_target_pairs={{0,4},{1,5},{4,8},{5,9},{8,12},{9,13},{12,14},{13,15},{14,10},{15,... | collective-permute-start | bytes 393224 | tf_op jit(solution)/shard_map/ppermute | solution.py:354
  46.7 5.7 %collective-permute-start.19 = (bf16[384,256]{1,0:T(8,128)(2,1)S(1)}, bf16[384,256]{1,0:T(8,128)(2,1)S(1)}, u32[]{:S(2)}, u32[]{:S(2)}) collective-permute-start(bf16[384,256]{1,0:T(8,128)(2,1)S(1)} %slice.110), channel_id=1, source_target_pairs={{4,0},{5,1},{8,4},{9,5},{12,8},{13,9},{14,12},{15,13},{10,14},{11,... | collective-permute-start | bytes 589832 | tf_op jit(solution)/shard_map/ppermute | solution.py:355
  47.4 1.7 %copy-start.1 = (bf16[1024,256]{1,0:T(8,128)(2,1)S(1)}, bf16[1024,256]{1,0:T(8,128)(2,1)}, u32[]{:S(2)}) copy-start(bf16[1024,256]{1,0:T(8,128)(2,1)} %copy-done) | copy-start | bytes 1572868
  51.5 10.0 %collective-permute-start.13 = (bf16[256,1280]{1,0:T(8,128)(2,1)S(1)}, bf16[256,1280]{1,0:T(8,128)(2,1)S(1)}, u32[]{:S(2)}, u32[]{:S(2)}) collective-permute-start(bf16[256,1280]{1,0:T(8,128)(2,1)S(1)} %get-tuple-element.42), channel_id=1, source_target_pairs={{0,1},{1,0},{2,3},{3,2},{4,5},{5,4},{6,7},{7,6},{8,9},{9,8},{10,11... | collective-permute-start | bytes 1966088 | tf_op jit(solution)/shard_map/ppermute | solution.py:248
  52.5 6.5 %collective-permute-start.20 = (bf16[384,256]{1,0:T(8,128)(2,1)S(1)}, bf16[384,256]{1,0:T(8,128)(2,1)S(1)}, u32[]{:S(2)}, u32[]{:S(2)}) collective-permute-start(bf16[384,256]{1,0:T(8,128)(2,1)S(1)} %fusion), channel_id=1, source_target_pairs={{0,16},{16,0},{1,17},{17,1},{2,18},{18,2},{3,19},{19,3},{4,20},{20... | collective-permute-start | bytes 589832 | tf_op jit(solution)/shard_map/ppermute | solution.py:373
  55.6 5.9 %collective-permute-start.17 = (bf16[256,512]{1,0:T(8,128)(2,1)S(1)}, bf16[256,512]{1,0:T(8,128)(2,1)S(1)}, u32[]{:S(2)}, u32[]{:S(2)}) collective-permute-start(bf16[256,512]{1,0:T(8,128)(2,1)S(1)} %get-tuple-element.46), channel_id=1, source_target_pairs={{0,1},{1,0},{2,3},{3,2},{4,5},{5,4},{6,7},{7,6},{8,9},{9,8},{10,11... | collective-permute-start | bytes 786440 | tf_op jit(solution)/shard_map/ppermute | solution.py:248
  60.1 1.4 %collective-permute-start.21 = (bf16[256,256]{1,0:T(8,128)(2,1)S(1)}, bf16[256,256]{1,0:T(8,128)(2,1)S(1)}, u32[]{:S(2)}, u32[]{:S(2)}) collective-permute-start(bf16[256,256]{1,0:T(8,128)(2,1)S(1)} %get-tuple-element.50), channel_id=1, source_target_pairs={{0,1},{1,0},{2,3},{3,2},{4,5},{5,4},{6,7},{7,6},{8,9},{9,8},{10,11... | collective-permute-start | bytes 393224 | tf_op jit(solution)/shard_map/ppermute | solution.py:248
